TPU v7x, 512 devices: a whole 4x8x8 slice. The times are simulated.
512 devices in a mesh: band: 64 (over z_hi, y, core), dx: 4 (over x), dy: 2 (over z_lo).
Axes of the slice: x: 4, y: 8, z: 8 (z_hi: 4, z_lo: 2; z = z_hi * 2 + z_lo), core: 2. Of those that a mesh axis runs over, the one named last changes fastest.
Arguments:
- orbitals: bfloat16 [384, 64, 16, 128], P('band', 'dx', 'dy'), may hold values from -20 to 20
- potential: float32 [64, 16, 128], P('dx', 'dy'), may hold values from -6 to 6
Outputs:
- new_orbitals: bfloat16 [384, 64, 16, 128], P('band', 'dx', 'dy')
- subspace: float32 [384, 384], P(None, 'band')
All inputs are finite; a program needn't handle non-finite values.
Results may differ from a plain program's by a relative error of at most 0.0068.
Values may be sent and summed in bfloat16 or wider, within the bound.
No kernel may reach another device: no remote copies, remote signals or barrier semaphores. Data moves between devices by JAX's collectives and lax.ppermute only.
A program may use at most 64 MiB of HBM per device.

v0:
```python
import jax
import jax.numpy as jnp
from jax import lax
from jax.sharding import PartitionSpec as P

STEPS = 2


COEFFS = (
    -5369.0 / 1800.0,
    12.0 / 7.0,
    -15.0 / 56.0,
    10.0 / 189.0,
    -1.0 / 112.0,
    2.0 / 1925.0,
    -1.0 / 16632.0,
)
TAU_STEP = 0.1
HIGH = lax.Precision.HIGHEST


def extended(block, sides, width):
    for axis, dim in sides:
        count = lax.axis_size(axis)
        forward = [(i, i + 1) for i in range(count - 1)]
        forward.append((count - 1, 0))
        backward = [(target, source) for source, target in forward]
        low = lax.ppermute(
            lax.slice_in_dim(block, block.shape[dim] - width, None, axis=dim), axis, forward
        )
        high = lax.ppermute(lax.slice_in_dim(block, 0, width, axis=dim), axis, backward)
        block = jnp.concatenate([low, block, high], axis=dim)
    return block


def gram(left, right):
    return lax.dot_general(
        left, right, (((1,), (1,)), ((), ())), preferred_element_type=jnp.float32
    )


def combine(matrix, panel):
    return lax.dot_general(
        matrix, panel, (((0,), (0,)), ((), ())), precision=HIGH, preferred_element_type=jnp.float32
    )


def apply_hamiltonian(psi_band, potential):
    padded = extended(psi_band, (("dx", 1), ("dy", 2)), 6).astype(jnp.float32)
    width_x = psi_band.shape[1]
    width_y = psi_band.shape[2]
    centre = padded[:, 6 : 6 + width_x, 6 : 6 + width_y, :]
    total = 3.0 * COEFFS[0] * centre
    for offset in range(1, 7):
        along_x = (
            padded[:, 6 + offset : 6 + offset + width_x, 6 : 6 + width_y, :]
            + padded[:, 6 - offset : 6 - offset + width_x, 6 : 6 + width_y, :]
        )
        along_y = (
            padded[:, 6 : 6 + width_x, 6 + offset : 6 + offset + width_y, :]
            + padded[:, 6 : 6 + width_x, 6 - offset : 6 - offset + width_y, :]
        )
        along_z = jnp.roll(centre, offset, 3) + jnp.roll(centre, -offset, 3)
        total = total + COEFFS[offset] * (along_x + along_y + along_z)
    return (-0.5 * total + potential[None] * centre).astype(jnp.bfloat16)


def update_cells(cell_orbitals, cell_image, volume):
    nbands = cell_orbitals.shape[0]
    eye = jnp.eye(nbands, dtype=jnp.float32)
    hsub = lax.psum(gram(cell_orbitals, cell_image), ("band", "dx", "dy")) * volume
    h_rounded = hsub.astype(jnp.bfloat16)
    rotated = lax.dot_general(
        h_rounded, cell_orbitals, (((0,), (0,)), ((), ())), preferred_element_type=jnp.float32
    )
    updated = (
        cell_orbitals.astype(jnp.float32)
        - TAU_STEP * cell_image.astype(jnp.float32)
        + TAU_STEP * rotated
    )
    correlation = (
        lax.psum(
            lax.dot_general(
                updated,
                updated,
                (((1,), (1,)), ((), ())),
                precision=HIGH,
                preferred_element_type=jnp.float32,
            ),
            ("band", "dx", "dy"),
        )
        * volume
    )
    correction = 1.5 * eye - 0.5 * correlation
    fixed = combine(correction, updated).astype(jnp.bfloat16)
    return (fixed, hsub)


def to_band_layout(cell_panel, band_shape):
    back = lax.all_to_all(cell_panel, "band", split_axis=0, concat_axis=1, tiled=True)
    return back.reshape(band_shape)


def per_device(orbitals, potential):
    band_shape = orbitals.shape
    local_bands = band_shape[0]
    cells_dev = band_shape[1] * band_shape[2] * band_shape[3]
    volume = 1.0 / (cells_dev * lax.axis_size("dx") * lax.axis_size("dy"))
    psi_band = orbitals
    for sweep in range(STEPS):
        image = apply_hamiltonian(psi_band, potential)
        cell_orbitals, cell_image = (
            lax.all_to_all(
                psi_band.reshape(local_bands, cells_dev),
                "band",
                split_axis=1,
                concat_axis=0,
                tiled=True,
            ),
            lax.all_to_all(
                image.reshape(local_bands, cells_dev),
                "band",
                split_axis=1,
                concat_axis=0,
                tiled=True,
            ),
        )
        fixed, hsub = update_cells(cell_orbitals, cell_image, volume)
        psi_band = to_band_layout(fixed, band_shape)
    columns = lax.dynamic_slice_in_dim(hsub, lax.axis_index("band") * local_bands, local_bands, 1)
    return (psi_band, columns)


def solution(mesh):
    in_specs = (P("band", "dx", "dy", None), P("dx", "dy", None))
    out_specs = (P("band", "dx", "dy", None), P(None, "band"))
    return jax.shard_map(
        per_device, mesh=mesh, in_specs=in_specs, out_specs=out_specs, check_vma=False
    )
```

profile of v0, /device:TPU:1, one launch (start us, length us, event | category | flops | bytes accessed | tf_op | source)
XLA Modules:
  0.0 1271.8 jit_solution(9825839375846442902)
XLA Ops:
  7.2 1.0 fusion.100
  8.2 3.9 collective-permute-start
  12.1 3.2 collective-permute-start.1
  15.3 1.0 constant_dynamic-update-slice_fusion.1
  16.3 0.9 collective-permute-done.1
  17.4 4.0 collective-permute-start.3
  21.4 1.9 collective-permute-start.2
  23.4 0.8 copy.14
  24.2 18.1 %all-to-all-start = ((bf16[6,64,256]{2,0,1:T(8,128)(2,1)}), bf16[6,64,256]{2,0,1:T(8,128)(2,1)S(1)}, u32[]{:S(2)}, u32[]{:S(2)}) async-start(bf16[6,64,256]{2,0,1:T(8,128)(2,1)} %copy.14), calls=%async_computation | async-start | bytes 524288 | tf_op jit(solution)/shard_map/all_to_all | solution.py:113
  42.4 0.5 maximum_convert_fusion
  45.0 0.3 copy-done.2
  45.3 2.4 fusion.37
  47.8 0.8 copy.15
  48.7 7.6 all-to-all-done
  56.2 6.4 all-to-all-start.1
  62.7 13.7 %all-to-all-done.1 = bf16[6,64,256]{2,0,1:T(8,128)(2,1)S(1)} async-done(((bf16[6,64,256]{2,0,1:T(8,128)(2,1)}), bf16[6,64,256]{2,0,1:T(8,128)(2,1)S(1)}, u32[]{:S(2)}, u32[]{:S(2)}) %all-to-all-start.1) | async-done | bytes 196640 | tf_op jit(solution)/shard_map/all_to_all | solution.py:120
  76.5 1.1 convolution_bitcast_fusion
  77.7 264.8 %all-reduce.5.cloned.1.call-done = f32[384,384]{0,1:T(8,128)} async-done(((f32[384,384]{0,1:T(8,128)}), f32[384,384]{0,1:T(8,128)}) %all-reduce.5.cloned.1.call-update) | async-done | bytes 589840 | tf_op jit(solution)/shard_map/psum | solution.py:71
  342.5 1.3 fusion
  343.8 1.6 fusion.101
  345.5 269.6 %all-reduce.7.cloned.1.call-done = f32[384,384]{1,0:T(8,128)} async-done(((f32[384,384]{1,0:T(8,128)}), f32[384,384]{1,0:T(8,128)}) %all-reduce.7.cloned.1.call-update) | async-done | bytes 589840 | tf_op jit(solution)/shard_map/psum | solution.py:82
  615.0 2.2 convolution_convert_fusion.1
  617.3 23.2 %all_to_all.105 = bf16[64,6,256]{2,1,0:T(8,128)(2,1)} all-to-all(bf16[64,6,256]{2,1,0:T(8,128)(2,1)S(1)} %all_to_all.86), channel_id=1, replica_groups=mesh['band'=64,'dx'=4,'dy'=2] {'band'}, dimensions={0} | all-to-all | bytes 393216 | tf_op jit(solution)/shard_map/all_to_all | solution.py:100
  640.5 1.0 copy.16
  641.6 2.6 collective-permute-start.4
  644.2 3.9 collective-permute-start.5
  648.3 1.2 collective-permute-done.5
  649.6 2.4 collective-permute-start.7
  652.0 2.9 collective-permute-start.6
  654.9 7.9 all-to-all-start.3
  662.8 4.8 collective-permute-done.6
  667.6 0.5 maximum_convert_fusion.1
  670.2 2.5 fusion.10
  672.8 0.8 copy.17
  673.6 3.0 all-to-all-done.3
  676.7 9.4 all-to-all-start.4
  686.2 13.7 %all-to-all-done.4 = bf16[6,64,256]{2,0,1:T(8,128)(2,1)S(1)} async-done(((bf16[6,64,256]{2,0,1:T(8,128)(2,1)}), bf16[6,64,256]{2,0,1:T(8,128)(2,1)S(1)}, u32[]{:S(2)}, u32[]{:S(2)}) %all-to-all-start.4) | async-done | bytes 196640 | tf_op jit(solution)/shard_map/all_to_all | solution.py:120
  700.0 1.1 fusion.102
  701.2 264.7 %all-reduce.9.cloned.1.call-done = f32[384,384]{0,1:T(8,128)} async-done(((f32[384,384]{0,1:T(8,128)}), f32[384,384]{0,1:T(8,128)}) %all-reduce.9.cloned.1.call-update) | async-done | bytes 589840 | tf_op jit(solution)/shard_map/psum | solution.py:71
  965.9 1.3 fusion.1
  967.2 1.6 fusion.103
  968.8 269.4 %all-reduce.11.cloned.1.call-done = f32[384,384]{1,0:T(8,128)} async-done(((f32[384,384]{1,0:T(8,128)}), f32[384,384]{1,0:T(8,128)}) %all-reduce.11.cloned.1.call-update) | async-done | bytes 589840 | tf_op jit(solution)/shard_map/psum | solution.py:82
  1238.3 2.2 convolution_convert_fusion
  1240.4 0.8 all_to_all.96
  1241.2 9.4 all-to-all-start.5
  1250.7 0.6 constant_dynamic-slice_fusion
  1251.3 13.2 %all-to-all-done.5 = bf16[64,6,256]{2,1,0:T(8,128)(2,1)S(1)} async-done(((bf16[64,6,256]{2,1,0:T(8,128)(2,1)}), bf16[64,6,256]{2,1,0:T(8,128)(2,1)S(1)}, u32[]{:S(2)}, u32[]{:S(2)}) %all-to-all-start.5) | async-done | bytes 196640 | tf_op jit(solution)/shard_map/all_to_all | solution.py:100
  1264.5 0.7 reshape.39
  (61 shorter events, 5.5 us)
Async XLA Ops:
  7.2 16.1 %copy-start.1 = (bf16[6,16,8,128]{3,2,1,0:T(8,128)(2,1)S(1)}, bf16[6,16,8,128]{3,2,1,0:T(8,128)(2,1)}, u32[]{:S(2)}) copy-start(bf16[6,16,8,128]{3,2,1,0:T(8,128)(2,1)} %param.2) | copy-start | bytes 589828
  8.2 7.2 collective-permute-start
  12.1 5.1 collective-permute-start.1
  17.4 25.0 %collective-permute-start.3 = (bf16[6,28,6,128]{3,2,1,0:T(8,128)(2,1)S(1)}, bf16[6,28,6,128]{3,2,1,0:T(8,128)(2,1)S(1)}, u32[]{:S(2)}, u32[]{:S(2)}) collective-permute-start(bf16[6,28,6,128]{3,2,1,0:T(8,128)(2,1)S(1)} %get-tuple-element.57), channel_id=1, source_target_pairs={{1,0},{0,1},{3,2},{2,3},{5,4},{4,5},{7,6},{6,7},{9,8},{8,9},{11,10... | collective-permute-start | bytes 774152 | tf_op jit(solution)/shard_map/ppermute | solution.py:31
  21.4 21.0 %collective-permute-start.2 = (bf16[6,28,6,128]{3,2,1,0:T(8,128)(2,1)S(1)}, bf16[6,28,6,128]{3,2,1,0:T(8,128)(2,1)S(1)}, u32[]{:S(2)}, u32[]{:S(2)}) collective-permute-start(bf16[6,28,6,128]{3,2,1,0:T(8,128)(2,1)S(1)} %get-tuple-element.56), channel_id=1, source_target_pairs={{0,1},{1,0},{2,3},{3,2},{4,5},{5,4},{6,7},{7,6},{8,9},{9,8},{10,11... | collective-permute-start | bytes 774152 | tf_op jit(solution)/shard_map/ppermute | solution.py:28
  24.2 32.0 %all-to-all-start = ((bf16[6,64,256]{2,0,1:T(8,128)(2,1)}), bf16[6,64,256]{2,0,1:T(8,128)(2,1)S(1)}, u32[]{:S(2)}, u32[]{:S(2)}) async-start(bf16[6,64,256]{2,0,1:T(8,128)(2,1)} %copy.14), calls=%async_computation | async-start | bytes 524288 | tf_op jit(solution)/shard_map/all_to_all | solution.py:113
  44.5 0.8 copy-start.2
  56.2 20.2 %all-to-all-start.1 = ((bf16[6,64,256]{2,0,1:T(8,128)(2,1)}), bf16[6,64,256]{2,0,1:T(8,128)(2,1)S(1)}, u32[]{:S(2)}, u32[]{:S(2)}) async-start(bf16[6,64,256]{2,0,1:T(8,128)(2,1)} %copy.15), calls=%async_computation.1 | async-start | bytes 524288 | tf_op jit(solution)/shard_map/all_to_all | solution.py:120
  62.6 279.9 %all-reduce.5.cloned.1.call-start = ((), (), s32[]{:S(2)}) async-start(), calls=%async_computation.6 | async-start | bytes 1179648 | tf_op jit(solution)/shard_map/psum | solution.py:71
  77.7 537.3 %all-reduce.7.cloned.1.call-start = ((), (), s32[]{:S(2)}) async-start(), calls=%async_computation.7 | async-start | bytes 1179648 | tf_op jit(solution)/shard_map/psum | solution.py:82
  641.6 6.7 collective-permute-start.4
  644.2 5.3 collective-permute-start.5
  649.6 13.2 %collective-permute-start.7 = (bf16[6,28,6,128]{3,2,1,0:T(8,128)(2,1)S(1)}, bf16[6,28,6,128]{3,2,1,0:T(8,128)(2,1)S(1)}, u32[]{:S(2)}, u32[]{:S(2)}) collective-permute-start(bf16[6,28,6,128]{3,2,1,0:T(8,128)(2,1)S(1)} %get-tuple-element.55), channel_id=1, source_target_pairs={{1,0},{0,1},{3,2},{2,3},{5,4},{4,5},{7,6},{6,7},{9,8},{8,9},{11,10... | collective-permute-start | bytes 774152 | tf_op jit(solution)/shard_map/ppermute | solution.py:31
  652.0 15.6 %collective-permute-start.6 = (bf16[6,28,6,128]{3,2,1,0:T(8,128)(2,1)S(1)}, bf16[6,28,6,128]{3,2,1,0:T(8,128)(2,1)S(1)}, u32[]{:S(2)}, u32[]{:S(2)}) collective-permute-start(bf16[6,28,6,128]{3,2,1,0:T(8,128)(2,1)S(1)} %get-tuple-element.54), channel_id=1, source_target_pairs={{0,1},{1,0},{2,3},{3,2},{4,5},{5,4},{6,7},{7,6},{8,9},{9,8},{10,11... | collective-permute-start | bytes 774152 | tf_op jit(solution)/shard_map/ppermute | solution.py:28
  654.9 21.8 %all-to-all-start.3 = ((bf16[6,64,256]{2,0,1:T(8,128)(2,1)}), bf16[6,64,256]{2,0,1:T(8,128)(2,1)S(1)}, u32[]{:S(2)}, u32[]{:S(2)}) async-start(bf16[6,64,256]{2,0,1:T(8,128)(2,1)} %bitcast.3), calls=%async_computation.3 | async-start | bytes 524288 | tf_op jit(solution)/shard_map/all_to_all | solution.py:113
  676.7 23.2 %all-to-all-start.4 = ((bf16[6,64,256]{2,0,1:T(8,128)(2,1)}), bf16[6,64,256]{2,0,1:T(8,128)(2,1)S(1)}, u32[]{:S(2)}, u32[]{:S(2)}) async-start(bf16[6,64,256]{2,0,1:T(8,128)(2,1)} %copy.17), calls=%async_computation.4 | async-start | bytes 524288 | tf_op jit(solution)/shard_map/all_to_all | solution.py:120
  686.1 279.8 %all-reduce.9.cloned.1.call-start = ((), (), s32[]{:S(2)}) async-start(), calls=%async_computation.8 | async-start | bytes 1179648 | tf_op jit(solution)/shard_map/psum | solution.py:71
  701.1 537.1 %all-reduce.11.cloned.1.call-start = ((), (), s32[]{:S(2)}) async-start(), calls=%async_computation.9 | async-start | bytes 1179648 | tf_op jit(solution)/shard_map/psum | solution.py:82
  967.2 283.5 %copy-start = (f32[384,384]{0,1:T(8,128)S(1)}, f32[384,384]{0,1:T(8,128)}, u32[]{:S(2)}) copy-start(f32[384,384]{0,1:T(8,128)} %all-reduce.9.cloned.1.call-done) | copy-start | bytes 1769476
  1241.2 23.3 %all-to-all-start.5 = ((bf16[64,6,256]{2,1,0:T(8,128)(2,1)}), bf16[64,6,256]{2,1,0:T(8,128)(2,1)S(1)}, u32[]{:S(2)}, u32[]{:S(2)}) async-start(bf16[64,6,256]{2,1,0:T(8,128)(2,1)} %all_to_all.96), calls=%async_computation.5 | async-start | bytes 524288 | tf_op jit(solution)/shard_map/all_to_all | solution.py:100
Sparse Core Ops, SparseCore 0:
  77.8 264.6 all-reduce.4
  348.3 266.7 all-reduce.6
  701.2 264.5 all-reduce.8
  971.5 266.7 all-reduce.10
where the time goes:
time: 1270 us
  waiting for transfers between devices  1130 us (89%)
  starting transfers between devices  76.2 us (6%)
  blocking collectives  23.2 us (2%)
  between operations  14.3 us (1%)
  local copies, waits for them, and re-layouts  12.9 us (1%)
    psum x2, waiting for transfers between devices, update_cells(): lax.psum(lax.dot_general(updated, updated, (((1,), (1,)), ((), ())), prec...  539 us
    psum x2, waiting for transfers between devices, update_cells(): lax.psum(gram(cell_orbitals, cell_image), ('band', 'dx', 'dy')) * volume  529 us
    all_to_all x2, waiting for transfers between devices, per_device(): lax.all_to_all(image.reshape(local_bands, cells_dev), 'band', split_axis=...  27.5 us
    all_to_all x2, starting transfers between devices, per_device(): lax.all_to_all(psi_band.reshape(local_bands, cells_dev), 'band', split_ax...  26.1 us
  transfers between devices with their start and end apart: 17, of which 13 were waited for; matrix products, arithmetic and copies ran while one was open for 1% of the time, Pallas kernels for 0%

commit v1 on v0

v1 whole, which is shorter than its diff:
```python
import jax
import jax.numpy as jnp
from jax import lax
from jax.sharding import Mesh, PartitionSpec as P

COEFFS = (
    -5369.0 / 1800.0,
    12.0 / 7.0,
    -15.0 / 56.0,
    10.0 / 189.0,
    -1.0 / 112.0,
    2.0 / 1925.0,
    -1.0 / 16632.0,
)
TAU = 0.1
BF = jnp.bfloat16
F32 = jnp.float32
BAND = ("zhi", "y", "core")
CHIPS = ("zhi", "y")
DOMAINS = ("dx", "dy")
BLK = 128
NGRAM = 5


def halo(block):
    count = lax.axis_size("dx")
    up = [(i, (i + 1) % count) for i in range(count)]
    down = [(b, a) for a, b in up]
    other = lax.ppermute(block, "dy", [(0, 1), (1, 0)])
    low = lax.ppermute(block[:, block.shape[1] - 6 :], "dx", up)
    high = lax.ppermute(block[:, :6], "dx", down)
    return other, low, high


def hamiltonian(block, potential):
    other, low, high = halo(block)
    wx, wy = block.shape[1], block.shape[2]
    f = block.astype(F32)
    px = jnp.concatenate([low, block, high], axis=1).astype(F32)
    o = other.astype(F32)
    py = jnp.concatenate([o[:, :, wy - 6 :], f, o[:, :, :6]], axis=2)
    total = 3.0 * COEFFS[0] * f
    for k in range(1, 7):
        along_x = px[:, 6 + k : 6 + k + wx] + px[:, 6 - k : 6 - k + wx]
        along_y = py[:, :, 6 + k : 6 + k + wy] + py[:, :, 6 - k : 6 - k + wy]
        along_z = jnp.roll(f, k, 3) + jnp.roll(f, -k, 3)
        total = total + COEFFS[k] * (along_x + along_y + along_z)
    return (-0.5 * total + potential[None] * f).astype(BF)


def swap(x, axes):
    return lax.all_to_all(x, axes, split_axis=0, concat_axis=0, tiled=True)


def spread(x, axes, size):
    return swap(jnp.broadcast_to(x[None], (size,) + x.shape), axes)


def gram(a, b):
    return lax.dot_general(a, b, (((1,), (1,)), ((), ())), preferred_element_type=F32)


def pairs(nblk):
    return [(r, c) for r in range(nblk) for c in range(r, nblk)]


def pack(g):
    nblk = g.shape[0] // BLK
    return [g[r * BLK : (r + 1) * BLK, c * BLK : (c + 1) * BLK] for r, c in pairs(nblk)]


def unpack(blocks, nblk):
    at = dict(zip(pairs(nblk), blocks))
    rows = [
        jnp.concatenate([at[r, c] if r <= c else at[c, r].T for c in range(nblk)], axis=1)
        for r in range(nblk)
    ]
    return jnp.concatenate(rows, axis=0)


def mm(a, b):
    return lax.dot_general(
        a, b, (((1,), (0,)), ((), ())), precision=lax.Precision.HIGH, preferred_element_type=F32
    )


def reduced(rows):
    n_core, n_dom, n_chip = (
        lax.axis_size("core"),
        lax.axis_size("dx") * lax.axis_size("dy"),
        lax.axis_size("zhi") * lax.axis_size("y"),
    )
    half = swap(rows.reshape(n_core, -1, BLK), "core").sum(0)
    part = swap(half.astype(BF).reshape(n_dom, -1, BLK), DOMAINS).astype(F32).sum(0)
    mine = swap(part.reshape(n_chip, -1, BLK), CHIPS).sum(0)
    part = spread(mine, CHIPS, n_chip).reshape(-1, BLK)
    half = spread(part, DOMAINS, n_dom).reshape(-1, BLK)
    return spread(half, "core", n_core).reshape(-1, BLK)


def algebra(s, g1, hw, hw2, w4, p, i, r):
    eye = jnp.eye(s.shape[0], dtype=F32)
    w1 = s - TAU * g1
    w2 = w1 - TAU * hw
    w3 = w2 - TAU * hw2
    e = TAU * g1.astype(BF).astype(F32)

    def outer(high, middle, low, step):
        b = mm(middle + 0.5 * mm(step, low), step)
        return high + b + b.T

    c1 = outer(w2, w1, s, e)
    m1 = 1.5 * eye - 0.5 * c1
    h2 = mm(mm(m1, outer(hw2, hw, g1, e)), m1)
    s1 = mm(mm(m1, c1), m1)
    w2b = mm(mm(m1, outer(w4, w3, w2, e)), m1)
    e2 = TAU * h2.astype(BF).astype(F32)
    c2 = outer(w2b, s1 - TAU * h2, s1, e2)
    m2 = 1.5 * eye - 0.5 * c2

    q = p.astype(F32) - TAU * i.astype(F32)
    t = q - TAU * r.astype(F32)
    psi1 = mm(m1, q + mm(e, p.astype(F32)))
    wpsi1 = mm(m1, t + mm(e, q))
    psi2 = mm(m2, wpsi1 + mm(e2, psi1))
    return psi2.astype(BF), h2


def per_device(orbitals, potential):
    shape = orbitals.shape
    nb = shape[0]
    n_band = lax.axis_size("zhi") * lax.axis_size("y") * lax.axis_size("core")
    cells = shape[1] * shape[2] * shape[3]
    bands = nb * n_band
    chunk = cells // n_band
    volume = 1.0 / (cells * lax.axis_size("dx") * lax.axis_size("dy"))

    image = hamiltonian(orbitals, potential)
    q = (orbitals.astype(F32) - TAU * image.astype(F32)).astype(BF)
    image_q = hamiltonian(q, potential)

    send = jnp.stack([orbitals, image, image_q]).reshape(3, nb, n_band, chunk // BLK, BLK)
    send = send.transpose(2, 0, 1, 3, 4).reshape(n_band, -1, BLK)
    got = swap(send, BAND).reshape(n_band, 3, nb, chunk // BLK, BLK)
    p, i, r = got.transpose(1, 0, 2, 3, 4).reshape(3, bands, chunk)

    qf = p.astype(F32) - TAU * i.astype(F32)
    qb = qf.astype(BF)
    tb = (qf - TAU * r.astype(F32)).astype(BF)
    grams = [gram(p, p), gram(p, i), gram(qb, i), gram(qb, r), gram(tb, tb)]
    nblk = bands // BLK
    rows = jnp.concatenate([b for g in grams for b in pack(g)], axis=0)
    count = rows.shape[0]
    unit = 8 * n_band * lax.axis_size("dx") * lax.axis_size("dy")
    rows = jnp.pad(rows, ((0, -count % unit), (0, 0)))
    total = reduced(rows)[:count] * volume
    per = nblk * (nblk + 1) // 2
    blocks = total.reshape(NGRAM, per, BLK, BLK)
    mats = [unpack([blocks[g, b] for b in range(per)], nblk) for g in range(NGRAM)]
    psi2, h2 = algebra(*mats, p, i, r)

    back = swap(psi2.reshape(n_band, nb, chunk), BAND)
    new = back.transpose(1, 0, 2).reshape(shape)
    columns = lax.dynamic_slice_in_dim(h2, lax.axis_index(BAND) * nb, nb, 1)
    return new, columns


def solution(mesh):
    n_band, n_dx, n_dy = mesh.devices.shape
    fine = Mesh(
        mesh.devices.reshape(-1, min(8, n_band // 2), 2, n_dx, n_dy), BAND + DOMAINS
    )
    in_specs = (P(BAND, "dx", "dy", None), P("dx", "dy", None))
    out_specs = (P(BAND, "dx", "dy", None), P(None, BAND))
    return jax.shard_map(
        per_device, mesh=fine, in_specs=in_specs, out_specs=out_specs, check_vma=False
    )
```

time: 1270 us -> 214 us (0.17)
  waiting for transfers between devices: 1130 us -> 14.6 us
  blocking collectives: 23.2 us -> 117 us
  starting transfers between devices: 76.2 us -> 24.3 us
    psum x4 -> x0, waiting for transfers between devices: 1070 us -> none  [the longest x2 539 us: update_cells(): lax.psum(lax.dot_general(updated, updated, (((1,), (1,)), ((), ())), prec...]
    all_to_all x1 -> x7, blocking collectives: 23.2 us -> 117 us  [swap(): return lax.all_to_all(x, axes, split_axis=0, concat_axis=0, tiled=True)]
    all_to_all x5 -> x1, starting transfers between devices: 51.2 us -> 4.41 us  [swap(): return lax.all_to_all(x, axes, split_axis=0, concat_axis=0, tiled=True)]
    all_to_all x5 -> x1, waiting for transfers between devices: 51.3 us -> 13.3 us  [swap(): return lax.all_to_all(x, axes, split_axis=0, concat_axis=0, tiled=True)]
  transfers between devices with their start and end apart: 17 -> 7, of which waited for: 13 -> 2; matrix products, arithmetic and copies ran while one was open for 1% -> 3% of each run, Pallas kernels for 0% -> 0%
where the time goes in v1:
time: 214 us; the launch traced here: 213 us
  blocking collectives  117 us (55%)
  starting transfers between devices  24.3 us (11%)
  matrix products  24 us (11%)
  local copies, waits for them, and re-layouts  21.8 us (10%)
  waiting for transfers between devices  14.6 us (7%)
  other arithmetic  9.89 us (5%)
    all_to_all x7, blocking collectives, swap(): return lax.all_to_all(x, axes, split_axis=0, concat_axis=0, tiled=True)  117 us
    dot_general x20, matrix products, mm(): lax.dot_general(a, b, (((1,), (0,)), ((), ())), precision=lax.Precision.H...  22.6 us
    all_to_all x1, waiting for transfers between devices, swap(): return lax.all_to_all(x, axes, split_axis=0, concat_axis=0, tiled=True)  13.3 us
    ppermute x2, starting transfers between devices, halo(): high = lax.ppermute(block[:, :6], 'dx', down)  7.95 us
    ppermute x2, starting transfers between devices, halo(): other = lax.ppermute(block, 'dy', [(0, 1), (1, 0)])  6.88 us
    unnamed x104, local copies, waits for them, and re-layouts  5.39 us
    ppermute x2, starting transfers between devices, halo(): low = lax.ppermute(block[:, block.shape[1] - 6:], 'dx', up)  5.04 us
    all_to_all x1, starting transfers between devices, swap(): return lax.all_to_all(x, axes, split_axis=0, concat_axis=0, tiled=True)  4.41 us
  transfers between devices with their start and end apart: 7, of which 2 were waited for; matrix products, arithmetic and copies ran while one was open for 3% of the time, Pallas kernels for 0%

profile of v1, /device:TPU:1, one launch (start us, length us, event | category | flops | bytes accessed | tf_op | source)
XLA Modules:
  0.0 213.0 jit_solution(5322549200233815080)
XLA Ops:
  0.6 5.0 %collective-permute-start.2 = (bf16[6,16,8,128]{3,2,1,0:T(8,128)(2,1)}, bf16[6,16,8,128]{3,2,1,0:T(8,128)(2,1)S(1)}, u32[]{:S(2)}, u32[]{:S(2)}) collective-permute-start(bf16[6,16,8,128]{3,2,1,0:T(8,128)(2,1)} %param.2), channel_id=1, source_target_pairs={{0,1},{1,0},{2,3},{3,2},{4,5},{5,4},{6,7},{7,6},{8,9},{9,8},{10,11... | collective-permute-start | bytes 589832 | tf_op jit(solution)/shard_map/ppermute | solution.py:29
  5.6 0.9 fusion.202
  6.6 3.1 %collective-permute-start = (bf16[6,6,8,128]{3,2,1,0:T(8,128)(2,1)S(1)}, bf16[6,6,8,128]{3,2,1,0:T(8,128)(2,1)S(1)}, u32[]{:S(2)}, u32[]{:S(2)}) collective-permute-start(bf16[6,6,8,128]{3,2,1,0:T(8,128)(2,1)S(1)} %get-tuple-element.100), channel_id=1, source_target_pairs={{0,2},{2,4},{4,6},{6,0},{1,3},{3,5},{5,7},{7,1},{8,10},{10,12},{12... | collective-permute-start | bytes 221192 | tf_op jit(solution)/shard_map/ppermute | solution.py:30
  9.7 3.4 %collective-permute-start.1 = (bf16[6,6,8,128]{3,2,1,0:T(8,128)(2,1)S(1)}, bf16[6,6,8,128]{3,2,1,0:T(8,128)(2,1)S(1)}, u32[]{:S(2)}, u32[]{:S(2)}) collective-permute-start(bf16[6,6,8,128]{3,2,1,0:T(8,128)(2,1)S(1)} %get-tuple-element.101), channel_id=1, source_target_pairs={{2,0},{4,2},{6,4},{0,6},{3,1},{5,3},{7,5},{1,7},{10,8},{12,10},{14... | collective-permute-start | bytes 221192 | tf_op jit(solution)/shard_map/ppermute | solution.py:31
  13.1 1.1 fusion.204
  16.5 2.7 %fusion.174 = (f32[6,16,8,128]{3,2,1,0:T(8,128)S(1)}, bf16[6,16,8,128]{3,2,1,0:T(8,128)(2,1)S(1)}, bf16[6,16,8,128]{3,2,1,0:T(8,128)(2,1)S(1)}) fusion(bf16[6,16,8,128]{3,2,1,0:T(8,128)(2,1)S(1)} %copy-done, f32[6,16,8,128]{3,2,1,0:T(8,128)S(1)} %convert_element_type.102, f32[16,8,128]{2,1,0:T(8,128)S(1)} %copy-done.9, ...), kind=kLoop, calls=%fused_computation.331 | loop fusion | flops 7569408 | bytes 11468800 | tf_op jit(solution)/shard_map/convert_element_type | solution.py:38
  19.2 1.9 collective-permute-start.5
  22.5 1.9 collective-permute-start.3
  24.5 4.6 %collective-permute-start.4 = (bf16[6,6,8,128]{3,2,1,0:T(8,128)(2,1)S(1)}, bf16[6,6,8,128]{3,2,1,0:T(8,128)(2,1)S(1)}, u32[]{:S(2)}, u32[]{:S(2)}) collective-permute-start(bf16[6,6,8,128]{3,2,1,0:T(8,128)(2,1)S(1)} %get-tuple-element.77), channel_id=1, source_target_pairs={{2,0},{4,2},{6,4},{0,6},{3,1},{5,3},{7,5},{1,7},{10,8},{12,10},{14... | collective-permute-start | bytes 221192 | tf_op jit(solution)/shard_map/ppermute | solution.py:31
  29.2 1.2 collective-permute-done.4
  30.6 2.7 %fusion.38 = bf16[6,16,8,128]{3,2,1,0:T(8,128)(2,1)S(1)} fusion(f32[6,16,6,128]{3,2,1,0:T(8,128)S(1)} %get-tuple-element.79, f32[6,16,8,128]{3,2,1,0:T(8,128)S(1)} %get-tuple-element.4, f32[6,16,6,128]{3,2,1,0:T(8,128)S(1)} %get-tuple-element.78, f32[6,28,8,128]{3,2,1,0:T(8,128)S(1)} %maximum_convert_fusion.1, f32[6,16,8,127]{3,2,1,0:T(8,128)S(1)} %get-tuple-element.73, ...), kind=kLoop, calls=%fused_computation.102 | loop fusion | flops 6979584 | bytes 10682368 | tf_op jit(solution)/shard_map/convert_element_type | solution.py:48
  33.3 1.0 maximum_bitcast_fusion
  34.8 39.7 %all_to_all.40 = bf16[64,36,128]{2,1,0:T(8,128)(2,1)S(1)} all-to-all(bf16[64,36,128]{2,1,0:T(8,128)(2,1)S(1)} %copy.142), channel_id=1, replica_groups=mesh['zhi'=4,'y'=8,'core'=2,'dx'=4,'dy'=2] {'zhi','y','core'}, dimensions={0} | all-to-all | bytes 1179648 | tf_op jit(solution)/shard_map/all_to_all | solution.py:52
  77.9 6.1 %all_to_all.41 = f32[2,2048,128]{2,1,0:T(8,128)S(1)} all-to-all(f32[2,2048,128]{2,1,0:T(8,128)S(1)} %bitcast.190), channel_id=1, replica_groups=mesh['zhi'=4,'y'=8,'core'=2,'dx'=4,'dy'=2] {'core'}, dimensions={0} | all-to-all | bytes 4194304 | tf_op jit(solution)/shard_map/all_to_all | solution.py:52
  84.1 14.5 %all_to_all.42 = bf16[8,256,128]{2,1,0:T(8,128)(2,1)S(1)} all-to-all(bf16[8,256,128]{2,1,0:T(8,128)(2,1)S(1)} %bitcast.196), channel_id=1, replica_groups=mesh['zhi'=4,'y'=8,'core'=2,'dx'=4,'dy'=2] {'dx','dy'}, dimensions={0} | all-to-all | bytes 1048576 | tf_op jit(solution)/shard_map/all_to_all | solution.py:52
  98.7 17.0 %all_to_all.43 = f32[32,8,128]{2,1,0:T(8,128)S(1)} all-to-all(f32[32,8,128]{2,1,0:T(8,128)S(1)} %bitcast.229), channel_id=1, replica_groups=mesh['zhi'=4,'y'=8,'core'=2,'dx'=4,'dy'=2] {'zhi','y'}, dimensions={0} | all-to-all | bytes 262144 | tf_op jit(solution)/shard_map/all_to_all | solution.py:52
  115.8 14.6 %all_to_all.44 = f32[32,8,128]{2,1,0:T(8,128)S(1)} all-to-all(f32[32,8,128]{2,1,0:T(8,128)S(1)} %broadcast_in_dim.10), channel_id=1, replica_groups=mesh['zhi'=4,'y'=8,'core'=2,'dx'=4,'dy'=2] {'zhi','y'}, dimensions={0} | all-to-all | bytes 262144 | tf_op jit(solution)/shard_map/all_to_all | solution.py:52
  130.4 14.5 %all_to_all.45 = f32[8,256,128]{2,1,0:T(8,128)S(1)} all-to-all(f32[8,256,128]{2,1,0:T(8,128)S(1)} %broadcast_in_dim.24), channel_id=1, replica_groups=mesh['zhi'=4,'y'=8,'core'=2,'dx'=4,'dy'=2] {'dx','dy'}, dimensions={0} | all-to-all | bytes 2097152 | tf_op jit(solution)/shard_map/all_to_all | solution.py:52
  145.1 10.1 %all_to_all.46 = f32[2,2048,128]{2,1,0:T(8,128)S(1)} all-to-all(f32[2,2048,128]{2,1,0:T(8,128)S(1)} %broadcast_in_dim.26), channel_id=1, replica_groups=mesh['zhi'=4,'y'=8,'core'=2,'dx'=4,'dy'=2] {'core'}, dimensions={0} | all-to-all | bytes 4194304 | tf_op jit(solution)/shard_map/all_to_all | solution.py:52
  155.3 0.8 slice_bitcast_fusion.2
  156.2 0.9 fusion.176
  157.9 1.1 convolution_add_fusion.2
  159.0 1.3 convolution_add_fusion.3
  162.5 0.7 fusion.28
  164.5 2.1 select_subtract_fusion
  166.6 1.2 fusion.209
  167.8 1.2 fusion.208
  169.1 0.7 fusion.26
  169.8 1.1 copy.173
  171.0 0.7 copy.170
  171.7 1.8 fusion.172
  173.6 2.8 %fusion.1 = f32[384,384]{1,0:T(8,128)} fusion(f32[384,384]{1,0:T(8,128)} %get-tuple-element.3, bf16[384,384]{1,0:T(8,128)(2,1)S(1)} %fusion.173, f32[128,128]{1,0:T(8,128)} %get-tuple-element.42, f32[128,128]{1,0:T(8,128)S(1)} %bitcast.225, f32[128,128]{1,0:T(8,128)S(1)} %copy-done.31, f32[128,384]{1,0:T(8,128)S(1)} %copy.171, ...), kind=kOutput, calls=%fused_computation.47 | convolution fusion | flops 341508096 | bytes 2064384 | tf_op jit(solution)/shard_map/dot_general | solution.py:82
  176.5 0.7 fusion.22
  177.3 0.8 fusion.207
  178.6 1.8 fusion.27
  180.4 1.1 copy.172
  181.5 0.9 copy.184
  182.4 0.9 copy.186
  183.4 1.6 copy.187
  185.7 0.9 fusion.6
  187.3 1.1 copy.176
  188.4 1.6 convolution_add_fusion.1
  190.0 1.8 fusion.8
  191.8 0.7 fusion.4
  193.0 0.8 reshape.59
  193.8 4.4 %all-to-all-start.7 = ((bf16[64,6,256]{2,1,0:T(8,128)(2,1)}), bf16[64,6,256]{2,1,0:T(8,128)(2,1)S(1)}, u32[]{:S(2)}, u32[]{:S(2)}) async-start(bf16[64,6,256]{2,1,0:T(8,128)(2,1)} %reshape.59), calls=%async_computation.7 | async-start | bytes 524288 | tf_op jit(solution)/shard_map/all_to_all | solution.py:52
  198.8 13.3 %all-to-all-done.7 = bf16[64,6,256]{2,1,0:T(8,128)(2,1)S(1)} async-done(((bf16[64,6,256]{2,1,0:T(8,128)(2,1)}), bf16[64,6,256]{2,1,0:T(8,128)(2,1)S(1)}, u32[]{:S(2)}, u32[]{:S(2)}) %all-to-all-start.7) | async-done | bytes 196640 | tf_op jit(solution)/shard_map/all_to_all | solution.py:52
  212.2 0.7 reshape.60
  (181 shorter events, 15.2 us)
Async XLA Ops:
  0.6 13.6 %copy-start = (bf16[6,16,8,128]{3,2,1,0:T(8,128)(2,1)S(1)}, bf16[6,16,8,128]{3,2,1,0:T(8,128)(2,1)}, u32[]{:S(2)}) copy-start(bf16[6,16,8,128]{3,2,1,0:T(8,128)(2,1)} %param.2) | copy-start | bytes 589828
  0.6 15.1 %collective-permute-start.2 = (bf16[6,16,8,128]{3,2,1,0:T(8,128)(2,1)}, bf16[6,16,8,128]{3,2,1,0:T(8,128)(2,1)S(1)}, u32[]{:S(2)}, u32[]{:S(2)}) collective-permute-start(bf16[6,16,8,128]{3,2,1,0:T(8,128)(2,1)} %param.2), channel_id=1, source_target_pairs={{0,1},{1,0},{2,3},{3,2},{4,5},{5,4},{6,7},{7,6},{8,9},{9,8},{10,11... | collective-permute-start | bytes 589832 | tf_op jit(solution)/shard_map/ppermute | solution.py:29
  6.6 9.1 %collective-permute-start = (bf16[6,6,8,128]{3,2,1,0:T(8,128)(2,1)S(1)}, bf16[6,6,8,128]{3,2,1,0:T(8,128)(2,1)S(1)}, u32[]{:S(2)}, u32[]{:S(2)}) collective-permute-start(bf16[6,6,8,128]{3,2,1,0:T(8,128)(2,1)S(1)} %get-tuple-element.100), channel_id=1, source_target_pairs={{0,2},{2,4},{4,6},{6,0},{1,3},{3,5},{5,7},{7,1},{8,10},{10,12},{12... | collective-permute-start | bytes 221192 | tf_op jit(solution)/shard_map/ppermute | solution.py:30
  9.7 6.0 %collective-permute-start.1 = (bf16[6,6,8,128]{3,2,1,0:T(8,128)(2,1)S(1)}, bf16[6,6,8,128]{3,2,1,0:T(8,128)(2,1)S(1)}, u32[]{:S(2)}, u32[]{:S(2)}) collective-permute-start(bf16[6,6,8,128]{3,2,1,0:T(8,128)(2,1)S(1)} %get-tuple-element.101), channel_id=1, source_target_pairs={{2,0},{4,2},{6,4},{0,6},{3,1},{5,3},{7,5},{1,7},{10,8},{12,10},{14... | collective-permute-start | bytes 221192 | tf_op jit(solution)/shard_map/ppermute | solution.py:31
  15.6 0.8 copy-start.9
  19.2 11.3 %collective-permute-start.5 = (bf16[6,16,8,128]{3,2,1,0:T(8,128)(2,1)S(1)}, bf16[6,16,8,128]{3,2,1,0:T(8,128)(2,1)S(1)}, u32[]{:S(2)}, u32[]{:S(2)}) collective-permute-start(bf16[6,16,8,128]{3,2,1,0:T(8,128)(2,1)S(1)} %get-tuple-element.5), channel_id=1, source_target_pairs={{0,1},{1,0},{2,3},{3,2},{4,5},{5,4},{6,7},{7,6},{8,9},{9,8},{10,11... | collective-permute-start | bytes 589832 | tf_op jit(solution)/shard_map/ppermute | solution.py:29
  22.5 6.6 %collective-permute-start.3 = (bf16[6,6,8,128]{3,2,1,0:T(8,128)(2,1)S(1)}, bf16[6,6,8,128]{3,2,1,0:T(8,128)(2,1)S(1)}, u32[]{:S(2)}, u32[]{:S(2)}) collective-permute-start(bf16[6,6,8,128]{3,2,1,0:T(8,128)(2,1)S(1)} %get-tuple-element.76), channel_id=1, source_target_pairs={{0,2},{2,4},{4,6},{6,0},{1,3},{3,5},{5,7},{7,1},{8,10},{10,12},{12... | collective-permute-start | bytes 221192 | tf_op jit(solution)/shard_map/ppermute | solution.py:30
  24.5 6.0 %collective-permute-start.4 = (bf16[6,6,8,128]{3,2,1,0:T(8,128)(2,1)S(1)}, bf16[6,6,8,128]{3,2,1,0:T(8,128)(2,1)S(1)}, u32[]{:S(2)}, u32[]{:S(2)}) collective-permute-start(bf16[6,6,8,128]{3,2,1,0:T(8,128)(2,1)S(1)} %get-tuple-element.77), channel_id=1, source_target_pairs={{2,0},{4,2},{6,4},{0,6},{3,1},{5,3},{7,5},{1,7},{10,8},{12,10},{14... | collective-permute-start | bytes 221192 | tf_op jit(solution)/shard_map/ppermute | solution.py:31
  156.2 5.6 %copy-start.14 = (f32[128,128]{1,0:T(8,128)}, f32[128,128]{1,0:T(8,128)S(1)}, u32[]{:S(2)}) copy-start(f32[128,128]{1,0:T(8,128)S(1)} %get-tuple-element.41) | copy-start | bytes 196612
  156.2 5.6 %copy-start.16 = (f32[128,128]{1,0:T(8,128)}, f32[128,128]{1,0:T(8,128)S(1)}, u32[]{:S(2)}) copy-start(f32[128,128]{1,0:T(8,128)S(1)} %get-tuple-element.44) | copy-start | bytes 196612
  156.2 7.4 %copy-start.10 = (f32[128,128]{1,0:T(8,128)}, f32[128,128]{1,0:T(8,128)S(1)}, u32[]{:S(2)}) copy-start(f32[128,128]{1,0:T(8,128)S(1)} %get-tuple-element.30) | copy-start | bytes 196612
  156.2 7.4 %copy-start.11 = (f32[128,128]{1,0:T(8,128)}, f32[128,128]{1,0:T(8,128)S(1)}, u32[]{:S(2)}) copy-start(f32[128,128]{1,0:T(8,128)S(1)} %get-tuple-element.33) | copy-start | bytes 196612
  156.2 7.4 %copy-start.12 = (f32[128,128]{1,0:T(8,128)}, f32[128,128]{1,0:T(8,128)S(1)}, u32[]{:S(2)}) copy-start(f32[128,128]{1,0:T(8,128)S(1)} %get-tuple-element.34) | copy-start | bytes 196612
  156.2 7.4 %copy-start.13 = (f32[128,128]{1,0:T(8,128)}, f32[128,128]{1,0:T(8,128)S(1)}, u32[]{:S(2)}) copy-start(f32[128,128]{1,0:T(8,128)S(1)} %get-tuple-element.35) | copy-start | bytes 196612
  157.1 4.6 %copy-start.18 = (f32[128,128]{1,0:T(8,128)}, f32[128,128]{1,0:T(8,128)S(1)}, u32[]{:S(2)}) copy-start(f32[128,128]{1,0:T(8,128)S(1)} %get-tuple-element.45) | copy-start | bytes 196612
  157.1 4.6 %copy-start.20 = (f32[128,128]{1,0:T(8,128)}, f32[128,128]{1,0:T(8,128)S(1)}, u32[]{:S(2)}) copy-start(f32[128,128]{1,0:T(8,128)S(1)} %get-tuple-element.46) | copy-start | bytes 196612
  157.8 5.8 %copy-start.4 = (f32[128,128]{1,0:T(8,128)}, f32[128,128]{1,0:T(8,128)S(1)}, u32[]{:S(2)}) copy-start(f32[128,128]{1,0:T(8,128)S(1)} %copy.155) | copy-start | bytes 196612
  160.6 0.7 copy-start.5
  162.5 1.0 copy-start.30
  163.6 0.8 copy-start.15
  163.6 0.9 copy-start.17
  163.6 0.9 copy-start.19
  163.6 0.9 copy-start.21
  164.5 2.1 copy-start.8
  164.5 3.3 %copy-start.7 = (f32[384,256]{1,0:T(8,128)S(1)}, f32[384,256]{1,0:T(8,128)}, u32[]{:S(2)}) copy-start(f32[384,256]{1,0:T(8,128)} %convolution_add_fusion.3) | copy-start | bytes 1179652
  167.8 3.0 %copy-start.3 = (f32[128,384]{0,1:T(8,128)S(1)}, f32[128,384]{0,1:T(8,128)}, u32[]{:S(2)}) copy-start(f32[128,384]{0,1:T(8,128)} %get-tuple-element.111) | copy-start | bytes 589828
  167.8 3.1 %copy-start.29 = (f32[128,128]{0,1:T(8,128)S(1)}, f32[128,128]{0,1:T(8,128)}, u32[]{:S(2)}) copy-start(f32[128,128]{0,1:T(8,128)} %get-tuple-element.17) | copy-start | bytes 196612
  170.9 2.8 %copy-start.6 = (f32[1,1,128,128]{2,3,1,0:T(8,128)S(1)}, f32[1,1,128,128]{2,3,1,0:T(8,128)}, u32[]{:S(2)}) copy-start(f32[1,1,128,128]{2,3,1,0:T(8,128)} %copy-done.5) | copy-start | bytes 196612
  171.7 1.9 copy-start.31
  173.6 2.9 %copy-start.1 = (f32[384,384]{0,1:T(8,128)S(1)}, f32[384,384]{0,1:T(8,128)}, u32[]{:S(2)}) copy-start(f32[384,384]{0,1:T(8,128)} %copy.173) | copy-start | bytes 1769476
  173.6 2.9 %copy-start.24 = (f32[128,128]{1,0:T(8,128)S(1)}, f32[128,128]{1,0:T(8,128)}, u32[]{:S(2)}) copy-start(f32[128,128]{1,0:T(8,128)} %get-tuple-element.29) | copy-start | bytes 196612
  173.6 2.9 %copy-start.25 = (f32[128,128]{1,0:T(8,128)S(1)}, f32[128,128]{1,0:T(8,128)}, u32[]{:S(2)}) copy-start(f32[128,128]{1,0:T(8,128)} %get-tuple-element.31) | copy-start | bytes 196612
  173.6 2.9 %copy-start.26 = (f32[128,128]{1,0:T(8,128)S(1)}, f32[128,128]{1,0:T(8,128)}, u32[]{:S(2)}) copy-start(f32[128,128]{1,0:T(8,128)} %get-tuple-element.32) | copy-start | bytes 196612
  173.6 2.9 %copy-start.27 = (f32[128,128]{1,0:T(8,128)S(1)}, f32[128,128]{1,0:T(8,128)}, u32[]{:S(2)}) copy-start(f32[128,128]{1,0:T(8,128)} %get-tuple-element.42) | copy-start | bytes 196612
  177.2 1.1 copy-start.28
  177.3 1.2 copy-start.32
  177.3 1.2 copy-start.33
  186.6 3.4 %copy-start.22 = (f32[128,128]{0,1:T(8,128)S(1)}, f32[128,128]{0,1:T(8,128)}, u32[]{:S(2)}) copy-start(f32[128,128]{0,1:T(8,128)} %get-tuple-element.8) | copy-start | bytes 196612
  186.6 3.4 %copy-start.23 = (f32[128,128]{0,1:T(8,128)S(1)}, f32[128,128]{0,1:T(8,128)}, u32[]{:S(2)}) copy-start(f32[128,128]{0,1:T(8,128)} %get-tuple-element.15) | copy-start | bytes 196612
  188.4 3.5 %copy-start.2 = (f32[384,384]{0,1:T(8,128)S(1)}, f32[384,384]{0,1:T(8,128)}, u32[]{:S(2)}) copy-start(f32[384,384]{0,1:T(8,128)} %copy.176) | copy-start | bytes 1769476
  193.8 18.4 %all-to-all-start.7 = ((bf16[64,6,256]{2,1,0:T(8,128)(2,1)}), bf16[64,6,256]{2,1,0:T(8,128)(2,1)S(1)}, u32[]{:S(2)}, u32[]{:S(2)}) async-start(bf16[64,6,256]{2,1,0:T(8,128)(2,1)} %reshape.59), calls=%async_computation.7 | async-start | bytes 524288 | tf_op jit(solution)/shard_map/all_to_all | solution.py:52

commit v2 on v1

v2 whole, which is shorter than its diff:
```python
import functools

import jax
import jax.numpy as jnp
from jax import lax
from jax.experimental import pallas as pl
from jax.experimental.pallas import tpu as pltpu
from jax.sharding import Mesh, PartitionSpec as P

COEFFS = (
    -5369.0 / 1800.0,
    12.0 / 7.0,
    -15.0 / 56.0,
    10.0 / 189.0,
    -1.0 / 112.0,
    2.0 / 1925.0,
    -1.0 / 16632.0,
)
TAU = 0.1
BF = jnp.bfloat16
F32 = jnp.float32
BAND = ("zhi", "yh", "yl", "core")
FAR = ("zhi", "yh")
NEAR = ("dx", "dy", "yl")
BLK = 128
NGRAM = 5


def halo(block):
    count = lax.axis_size("dx")
    up = [(i, (i + 1) % count) for i in range(count)]
    down = [(b, a) for a, b in up]
    other = lax.ppermute(block, "dy", [(0, 1), (1, 0)])
    low = lax.ppermute(block[:, block.shape[1] - 6 :], "dx", up)
    high = lax.ppermute(block[:, :6], "dx", down)
    return other, low, high


def hamiltonian(block, potential):
    other, low, high = halo(block)
    wx, wy = block.shape[1], block.shape[2]
    f = block.astype(F32)
    px = jnp.concatenate([low, block, high], axis=1).astype(F32)
    o = other.astype(F32)
    py = jnp.concatenate([o[:, :, wy - 6 :], f, o[:, :, :6]], axis=2)
    total = 3.0 * COEFFS[0] * f
    for k in range(1, 7):
        along_x = px[:, 6 + k : 6 + k + wx] + px[:, 6 - k : 6 - k + wx]
        along_y = py[:, :, 6 + k : 6 + k + wy] + py[:, :, 6 - k : 6 - k + wy]
        along_z = jnp.roll(f, k, 3) + jnp.roll(f, -k, 3)
        total = total + COEFFS[k] * (along_x + along_y + along_z)
    return (-0.5 * total + potential[None] * f).astype(BF)


def swap(x, axes):
    return lax.all_to_all(x, axes, split_axis=0, concat_axis=0, tiled=True)


def spread(x, axes, size):
    return swap(jnp.broadcast_to(x[None], (size,) + x.shape), axes)


def gram(a, b):
    return lax.dot_general(a, b, (((1,), (1,)), ((), ())), preferred_element_type=F32)


def pairs(nblk):
    return [(r, c) for r in range(nblk) for c in range(r, nblk)]


def pack(g):
    nblk = g.shape[0] // BLK
    return [g[r * BLK : (r + 1) * BLK, c * BLK : (c + 1) * BLK] for r, c in pairs(nblk)]


def reduced(rows):
    n_near, n_far = axes_size(NEAR), axes_size(FAR)
    half = swap(rows.reshape(2, -1, BLK), "core").sum(0)
    part = swap(half.astype(BF).reshape(n_near, -1, BLK), NEAR).astype(F32).sum(0)
    mine = spread(part, FAR, n_far).sum(0)
    half = spread(mine, NEAR, n_near).reshape(-1, BLK)
    return spread(half, "core", 2).reshape(-1, BLK)


def axes_size(axes):
    size = 1
    for axis in axes:
        size *= lax.axis_size(axis)
    return size


def dot(a, b):
    return jnp.dot(a, b, preferred_element_type=F32)


def split(x):
    high = x.astype(BF)
    return high, (x - high.astype(F32)).astype(BF)


def algebra_kernel(volume, rows_ref, p_ref, i_ref, r_ref, psi_ref, h_ref, mats):
    n = p_ref.shape[0]
    nblk = n // BLK
    spots = pairs(nblk)
    for g in range(NGRAM):
        for b, (r, c) in enumerate(spots):
            at = (g * len(spots) + b) * BLK
            tile = rows_ref[at : at + BLK] * volume
            mats[g, r * BLK : (r + 1) * BLK, c * BLK : (c + 1) * BLK] = tile
            if r != c:
                mats[g, c * BLK : (c + 1) * BLK, r * BLK : (r + 1) * BLK] = tile.T
    s, g1, hw, hw2, w4 = (mats[g] for g in range(NGRAM))
    w1 = s - TAU * g1
    w2 = w1 - TAU * hw
    w3 = w2 - TAU * hw2
    row = lax.broadcasted_iota(jnp.int32, (n, n), 0)
    col = lax.broadcasted_iota(jnp.int32, (n, n), 1)
    diag = jnp.where(row == col, 1.5, 0.0).astype(F32)

    def left(h, x):
        high, low = split(x)
        return dot(h, high) + dot(h, low)

    def right(x, h):
        high, low = split(x)
        return dot(high, h) + dot(low, h)

    def full(a, x):
        high, low = split(x)
        return dot(a[0], high) + dot(a[0], low) + dot(a[1], high)

    def outer(high, middle, low, h):
        b = TAU * right(middle + (0.5 * TAU) * left(h, low), h)
        return high + b + b.T

    h = g1.astype(BF)
    c1 = outer(w2, w1, s, h)
    m1 = split(diag - 0.5 * c1)

    def both(x):
        return full(m1, full(m1, x).T)

    h2 = both(outer(hw2, hw, g1, h))
    h_ref[...] = h2
    s1 = both(c1)
    w2b = both(outer(w4, w3, w2, h))
    hh = h2.astype(BF)
    m2 = split(diag - 0.5 * outer(w2b, s1 - TAU * h2, s1, hh))

    p, i = p_ref[...], i_ref[...]
    hp = TAU * dot(h, p)
    hq = hp - (TAU * TAU) * dot(h, i)
    q = p.astype(F32) - TAU * i.astype(F32)
    t = q - TAU * r_ref[...].astype(F32)
    psi1 = full(m1, q + hp)
    wpsi1 = full(m1, t + hq)
    psi_ref[...] = full(m2, wpsi1 + TAU * left(hh, psi1)).astype(BF)


def algebra(rows, p, i, r, volume):
    n, chunk = p.shape
    return pl.pallas_call(
        functools.partial(algebra_kernel, volume),
        out_shape=(
            jax.ShapeDtypeStruct((n, chunk), BF),
            jax.ShapeDtypeStruct((n, n), F32),
        ),
        in_specs=[pl.BlockSpec(memory_space=pltpu.VMEM)] * 4,
        out_specs=(pl.BlockSpec(memory_space=pltpu.VMEM),) * 2,
        scratch_shapes=[pltpu.VMEM((NGRAM, n, n), F32)],
        compiler_params=pltpu.CompilerParams(vmem_limit_bytes=48 * 1024 * 1024),
    )(rows, p, i, r)


def per_device(orbitals, potential):
    shape = orbitals.shape
    nb = shape[0]
    n_band = axes_size(BAND)
    cells = shape[1] * shape[2] * shape[3]
    bands = nb * n_band
    chunk = cells // n_band
    volume = 1.0 / (cells * lax.axis_size("dx") * lax.axis_size("dy"))

    image = hamiltonian(orbitals, potential)
    q = (orbitals.astype(F32) - TAU * image.astype(F32)).astype(BF)
    image_q = hamiltonian(q, potential)

    send = jnp.stack([orbitals, image, image_q]).reshape(3, nb, n_band, chunk // BLK, BLK)
    send = send.transpose(2, 0, 1, 3, 4).reshape(n_band, -1, BLK)
    got = swap(send, BAND).reshape(n_band, 3, nb, chunk // BLK, BLK)
    p, i, r = got.transpose(1, 0, 2, 3, 4).reshape(3, bands, chunk)

    qf = p.astype(F32) - TAU * i.astype(F32)
    qb = qf.astype(BF)
    tb = (qf - TAU * r.astype(F32)).astype(BF)
    grams = [gram(p, p), gram(p, i), gram(qb, i), gram(qb, r), gram(tb, tb)]
    rows = jnp.concatenate([b for g in grams for b in pack(g)], axis=0)
    unit = 8 * n_band * lax.axis_size("dx") * lax.axis_size("dy")
    rows = jnp.pad(rows, ((0, -rows.shape[0] % unit), (0, 0)))
    psi2, h2 = algebra(reduced(rows), p, i, r, volume)

    back = swap(psi2.reshape(n_band, nb, chunk), BAND)
    new = back.transpose(1, 0, 2).reshape(shape)
    columns = lax.dynamic_slice_in_dim(h2, lax.axis_index(BAND) * nb, nb, 1)
    return new, columns


def solution(mesh):
    n_band, n_dx, n_dy = mesh.devices.shape
    near = min(4, n_band // 2)
    far = min(2, n_band // 2 // near)
    fine = Mesh(mesh.devices.reshape(-1, far, near, 2, n_dx, n_dy), BAND + ("dx", "dy"))
    in_specs = (P(BAND, "dx", "dy", None), P("dx", "dy", None))
    out_specs = (P(BAND, "dx", "dy", None), P(None, BAND))
    return jax.shard_map(
        per_device, mesh=fine, in_specs=in_specs, out_specs=out_specs, check_vma=False
    )
```

time: 214 us -> 198 us (0.925)
  waiting for transfers between devices: 14.6 us -> 38.4 us
  blocking collectives: 117 us -> 93.9 us
  matrix products: 24 us -> 1.43 us
  local copies, waits for them, and re-layouts: 21.8 us -> 11.5 us
  Pallas kernels: 0 us -> 10.2 us
  starting transfers between devices: 24.3 us -> 33.9 us
  other arithmetic: 9.89 us -> 6.9 us
    all_to_all x1 -> x2, waiting for transfers between devices: 13.3 us -> 37.1 us  [swap(): return lax.all_to_all(x, axes, split_axis=0, concat_axis=0, tiled=True)]
    all_to_all x7 -> x5, blocking collectives: 117 us -> 93.9 us  [swap(): return lax.all_to_all(x, axes, split_axis=0, concat_axis=0, tiled=True)]
    dot_general x20 -> x0, matrix products: 22.6 us -> none  [mm(): lax.dot_general(a, b, (((1,), (0,)), ((), ())), precision=lax.Precision.H...]
    pallas_call x0 -> x1, Pallas kernels: none -> 10.2 us  [algebra(): pl.pallas_call(functools.partial(algebra_kernel, volume), out_shape=(jax....]
    all_to_all x1 -> x2, starting transfers between devices: 4.41 us -> 14 us  [swap(): return lax.all_to_all(x, axes, split_axis=0, concat_axis=0, tiled=True)]
    unnamed x104 -> x30, local copies, waits for them, and re-layouts: 5.39 us -> 1.57 us
    dot_general x5 -> x0, local copies, waits for them, and re-layouts: 3.67 us -> none  [mm(): lax.dot_general(a, b, (((1,), (0,)), ((), ())), precision=lax.Precision.H...]
  transfers between devices with their start and end apart: 7 -> 8, of which waited for: 2 -> 3; matrix products, arithmetic and copies ran while one was open for 3% -> 3% of each run, Pallas kernels for 0% -> 0%
where the time goes in v2:
time: 198 us; the launch traced here: 197 us
  blocking collectives  93.9 us (47%)
  waiting for transfers between devices  38.4 us (19%)
  starting transfers between devices  33.9 us (17%)
  local copies, waits for them, and re-layouts  11.5 us (6%)
  Pallas kernels  10.2 us (5%)
  other arithmetic  6.9 us (3%)
    all_to_all x5, blocking collectives, swap(): return lax.all_to_all(x, axes, split_axis=0, concat_axis=0, tiled=True)  93.9 us
    all_to_all x2, waiting for transfers between devices, swap(): return lax.all_to_all(x, axes, split_axis=0, concat_axis=0, tiled=True)  37.1 us
    all_to_all x2, starting transfers between devices, swap(): return lax.all_to_all(x, axes, split_axis=0, concat_axis=0, tiled=True)  14 us
    pallas_call x1, Pallas kernels, algebra(): pl.pallas_call(functools.partial(algebra_kernel, volume), out_shape=(jax....  10.2 us
    ppermute x2, starting transfers between devices, halo(): high = lax.ppermute(block[:, :6], 'dx', down)  7.95 us
    ppermute x2, starting transfers between devices, halo(): other = lax.ppermute(block, 'dy', [(0, 1), (1, 0)])  6.88 us
    ppermute x2, starting transfers between devices, halo(): low = lax.ppermute(block[:, block.shape[1] - 6:], 'dx', up)  5.04 us
    slice x24, local copies, waits for them, and re-layouts, hamiltonian(): along_z = jnp.roll(f, k, 3) + jnp.roll(f, -k, 3)  4 us
  transfers between devices with their start and end apart: 8, of which 3 were waited for; matrix products, arithmetic and copies ran while one was open for 3% of the time, Pallas kernels for 0%

profile of v2, /device:TPU:1, one launch (start us, length us, event | category | flops | bytes accessed | tf_op | source)
XLA Modules:
  0.0 197.4 jit_solution(14155080961918389571)
XLA Ops:
  0.6 5.0 %collective-permute-start.2 = (bf16[6,16,8,128]{3,2,1,0:T(8,128)(2,1)}, bf16[6,16,8,128]{3,2,1,0:T(8,128)(2,1)S(1)}, u32[]{:S(2)}, u32[]{:S(2)}) collective-permute-start(bf16[6,16,8,128]{3,2,1,0:T(8,128)(2,1)} %param.2), channel_id=1, source_target_pairs={{0,1},{1,0},{2,3},{3,2},{4,5},{5,4},{6,7},{7,6},{8,9},{9,8},{10,11... | collective-permute-start | bytes 589832 | tf_op jit(solution)/shard_map/ppermute | solution.py:33
  5.6 0.9 fusion.125
  6.6 3.1 %collective-permute-start = (bf16[6,6,8,128]{3,2,1,0:T(8,128)(2,1)S(1)}, bf16[6,6,8,128]{3,2,1,0:T(8,128)(2,1)S(1)}, u32[]{:S(2)}, u32[]{:S(2)}) collective-permute-start(bf16[6,6,8,128]{3,2,1,0:T(8,128)(2,1)S(1)} %get-tuple-element.72), channel_id=1, source_target_pairs={{0,2},{2,4},{4,6},{6,0},{1,3},{3,5},{5,7},{7,1},{8,10},{10,12},{12... | collective-permute-start | bytes 221192 | tf_op jit(solution)/shard_map/ppermute | solution.py:34
  9.7 3.4 %collective-permute-start.1 = (bf16[6,6,8,128]{3,2,1,0:T(8,128)(2,1)S(1)}, bf16[6,6,8,128]{3,2,1,0:T(8,128)(2,1)S(1)}, u32[]{:S(2)}, u32[]{:S(2)}) collective-permute-start(bf16[6,6,8,128]{3,2,1,0:T(8,128)(2,1)S(1)} %get-tuple-element.73), channel_id=1, source_target_pairs={{2,0},{4,2},{6,4},{0,6},{3,1},{5,3},{7,5},{1,7},{10,8},{12,10},{14... | collective-permute-start | bytes 221192 | tf_op jit(solution)/shard_map/ppermute | solution.py:35
  13.1 1.1 fusion.115
  14.2 0.1 fusion.116
  14.5 0.1 fusion.118
  14.7 0.1 fusion.120
  15.1 0.1 fusion.123
  15.4 0.1 fusion.127
  15.8 0.6 copy-done.1
  16.5 2.7 %fusion.98 = (f32[6,16,8,128]{3,2,1,0:T(8,128)S(1)}, bf16[6,16,8,128]{3,2,1,0:T(8,128)(2,1)S(1)}, bf16[6,16,8,128]{3,2,1,0:T(8,128)(2,1)S(1)}) fusion(bf16[6,16,8,128]{3,2,1,0:T(8,128)(2,1)S(1)} %copy-done, f32[6,16,8,128]{3,2,1,0:T(8,128)S(1)} %convert_element_type.76, f32[16,8,128]{2,1,0:T(8,128)S(1)} %copy-done.1, ...), kind=kLoop, calls=%fused_computation.202 | loop fusion | flops 7569408 | bytes 11468800 | tf_op jit(solution)/shard_map/convert_element_type | solution.py:42
  19.2 1.9 collective-permute-start.5
  22.5 1.9 collective-permute-start.3
  24.5 4.6 %collective-permute-start.4 = (bf16[6,6,8,128]{3,2,1,0:T(8,128)(2,1)S(1)}, bf16[6,6,8,128]{3,2,1,0:T(8,128)(2,1)S(1)}, u32[]{:S(2)}, u32[]{:S(2)}) collective-permute-start(bf16[6,6,8,128]{3,2,1,0:T(8,128)(2,1)S(1)} %get-tuple-element.49), channel_id=1, source_target_pairs={{2,0},{4,2},{6,4},{0,6},{3,1},{5,3},{7,5},{1,7},{10,8},{12,10},{14... | collective-permute-start | bytes 221192 | tf_op jit(solution)/shard_map/ppermute | solution.py:35
  29.2 1.2 collective-permute-done.4
  30.6 2.7 %fusion.9 = bf16[6,16,8,128]{3,2,1,0:T(8,128)(2,1)S(1)} fusion(f32[6,16,6,128]{3,2,1,0:T(8,128)S(1)} %get-tuple-element.51, f32[6,16,8,128]{3,2,1,0:T(8,128)S(1)} %get-tuple-element.16, f32[6,16,6,128]{3,2,1,0:T(8,128)S(1)} %get-tuple-element.50, f32[6,28,8,128]{3,2,1,0:T(8,128)S(1)} %maximum_convert_fusion.1, f32[6,16,8,127]{3,2,1,0:T(8,128)S(1)} %get-tuple-element.45, ...), kind=kLoop, calls=%fused_computation.51 | loop fusion | flops 6979584 | bytes 10682368 | tf_op jit(solution)/shard_map/convert_element_type | solution.py:52
  33.3 1.0 maximum_bitcast_fusion
  34.3 0.1 copy.28
  34.4 0.4 copy.29
  34.8 39.7 %all_to_all.35 = bf16[64,36,128]{2,1,0:T(8,128)(2,1)S(1)} all-to-all(bf16[64,36,128]{2,1,0:T(8,128)(2,1)S(1)} %copy.29), channel_id=1, replica_groups=mesh['zhi'=4,'yh'=2,'yl'=4,'core'=2,'dx'=4,'dy'=2] {'zhi','yh','yl','core'}, dimensions={0} | all-to-all | bytes 1179648 | tf_op jit(solution)/shard_map/all_to_all | solution.py:56
  74.5 0.1 copy.30
  74.8 0.2 copy.32
  75.1 0.2 copy.33
  75.3 0.2 copy.31
  75.5 0.3 fusion.97
  75.8 0.3 fusion.96
  76.1 0.3 fusion.92
  76.6 0.2 copy.34
  76.8 0.3 fusion.90
  77.2 0.2 copy.35
  77.4 0.3 fusion.87
  77.8 0.1 pad.4
  77.9 6.1 %all_to_all.36 = f32[2,2048,128]{2,1,0:T(8,128)S(1)} all-to-all(f32[2,2048,128]{2,1,0:T(8,128)S(1)} %bitcast.47), channel_id=1, replica_groups=mesh['zhi'=4,'yh'=2,'yl'=4,'core'=2,'dx'=4,'dy'=2] {'core'}, dimensions={0} | all-to-all | bytes 4194304 | tf_op jit(solution)/shard_map/all_to_all | solution.py:56
  84.0 0.1 reduce_sum.27
  84.1 22.3 %all_to_all.37 = bf16[32,64,128]{2,1,0:T(8,128)(2,1)S(1)} all-to-all(bf16[32,64,128]{2,1,0:T(8,128)(2,1)S(1)} %bitcast.58), channel_id=1, replica_groups=mesh['zhi'=4,'yh'=2,'yl'=4,'core'=2,'dx'=4,'dy'=2] {'dx','dy','yl'}, dimensions={0} | all-to-all | bytes 1048576 | tf_op jit(solution)/shard_map/all_to_all | solution.py:56
  106.6 17.0 %all_to_all.38 = f32[8,64,128]{2,1,0:T(8,128)S(1)} all-to-all(f32[8,64,128]{2,1,0:T(8,128)S(1)} %broadcast_in_dim.8), channel_id=1, replica_groups=mesh['zhi'=4,'yh'=2,'yl'=4,'core'=2,'dx'=4,'dy'=2] {'zhi','yh'}, dimensions={0} | all-to-all | bytes 524288 | tf_op jit(solution)/shard_map/all_to_all | solution.py:56
  123.6 1.1 broadcast_in_dim.9
  124.7 8.1 %all-to-all-start.4 = ((f32[32,64,128]{2,1,0:T(8,128)}), f32[32,64,128]{2,1,0:T(8,128)S(1)}, u32[]{:S(2)}, u32[]{:S(2)}) async-start(f32[32,64,128]{2,1,0:T(8,128)} %broadcast_in_dim.9), calls=%async_computation.4 | async-start | bytes 2097152 | tf_op jit(solution)/shard_map/all_to_all | solution.py:56
  133.0 24.1 %all-to-all-done.4 = f32[32,64,128]{2,1,0:T(8,128)S(1)} async-done(((f32[32,64,128]{2,1,0:T(8,128)}), f32[32,64,128]{2,1,0:T(8,128)S(1)}, u32[]{:S(2)}, u32[]{:S(2)}) %all-to-all-start.4) | async-done | bytes 1048608 | tf_op jit(solution)/shard_map/all_to_all | solution.py:56
  157.1 0.1 broadcast_in_dim.11
  157.2 8.7 %all_to_all.39 = f32[2,2048,128]{2,1,0:T(8,128)S(1)} all-to-all(f32[2,2048,128]{2,1,0:T(8,128)S(1)} %broadcast_in_dim.11), channel_id=1, replica_groups=mesh['zhi'=4,'yh'=2,'yl'=4,'core'=2,'dx'=4,'dy'=2] {'core'}, dimensions={0} | all-to-all | bytes 4194304 | tf_op jit(solution)/shard_map/all_to_all | solution.py:56
  165.9 10.2 %shard_map.41 = (bf16[384,256]{1,0:T(8,128)(2,1)S(1)}, f32[384,384]{1,0:T(8,128)S(1)}) custom-call(f32[4096,128]{1,0:T(8,128)S(1)} %bitcast.44, bf16[384,256]{1,0:T(8,128)(2,1)S(1)} %bitcast.45, bf16[384,256]{1,0:T(8,128)(2,1)S(1)} %get-tuple-element.81.i_ref, bf16[384,256]{1,0:T(8,128)(2,1)S(1)} %get-tuple-element.80.r_ref), custom_call_target="tpu_custom_call" | custom-call | tf_op jit(solution)/shard_map/pallas_call | solution.py:162
  176.1 0.8 reshape.51
  176.8 5.9 %all-to-all-start.6 = ((bf16[64,6,256]{2,1,0:T(8,128)(2,1)}), bf16[64,6,256]{2,1,0:T(8,128)(2,1)S(1)}, u32[]{:S(2)}, u32[]{:S(2)}) async-start(bf16[64,6,256]{2,1,0:T(8,128)(2,1)} %reshape.51), calls=%async_computation.6 | async-start | bytes 524288 | tf_op jit(solution)/shard_map/all_to_all | solution.py:56
  182.9 0.7 copy.37
  183.6 13.0 %all-to-all-done.6 = bf16[64,6,256]{2,1,0:T(8,128)(2,1)S(1)} async-done(((bf16[64,6,256]{2,1,0:T(8,128)(2,1)}), bf16[64,6,256]{2,1,0:T(8,128)(2,1)S(1)}, u32[]{:S(2)}, u32[]{:S(2)}) %all-to-all-start.6) | async-done | bytes 196640 | tf_op jit(solution)/shard_map/all_to_all | solution.py:56
  196.6 0.7 reshape.52
  (66 shorter events, 3.3 us)
Async XLA Ops:
  0.6 13.6 %copy-start = (bf16[6,16,8,128]{3,2,1,0:T(8,128)(2,1)S(1)}, bf16[6,16,8,128]{3,2,1,0:T(8,128)(2,1)}, u32[]{:S(2)}) copy-start(bf16[6,16,8,128]{3,2,1,0:T(8,128)(2,1)} %param.2) | copy-start | bytes 589828
  0.6 15.1 %collective-permute-start.2 = (bf16[6,16,8,128]{3,2,1,0:T(8,128)(2,1)}, bf16[6,16,8,128]{3,2,1,0:T(8,128)(2,1)S(1)}, u32[]{:S(2)}, u32[]{:S(2)}) collective-permute-start(bf16[6,16,8,128]{3,2,1,0:T(8,128)(2,1)} %param.2), channel_id=1, source_target_pairs={{0,1},{1,0},{2,3},{3,2},{4,5},{5,4},{6,7},{7,6},{8,9},{9,8},{10,11... | collective-permute-start | bytes 589832 | tf_op jit(solution)/shard_map/ppermute | solution.py:33
  6.6 9.1 %collective-permute-start = (bf16[6,6,8,128]{3,2,1,0:T(8,128)(2,1)S(1)}, bf16[6,6,8,128]{3,2,1,0:T(8,128)(2,1)S(1)}, u32[]{:S(2)}, u32[]{:S(2)}) collective-permute-start(bf16[6,6,8,128]{3,2,1,0:T(8,128)(2,1)S(1)} %get-tuple-element.72), channel_id=1, source_target_pairs={{0,2},{2,4},{4,6},{6,0},{1,3},{3,5},{5,7},{7,1},{8,10},{10,12},{12... | collective-permute-start | bytes 221192 | tf_op jit(solution)/shard_map/ppermute | solution.py:34
  9.7 6.0 %collective-permute-start.1 = (bf16[6,6,8,128]{3,2,1,0:T(8,128)(2,1)S(1)}, bf16[6,6,8,128]{3,2,1,0:T(8,128)(2,1)S(1)}, u32[]{:S(2)}, u32[]{:S(2)}) collective-permute-start(bf16[6,6,8,128]{3,2,1,0:T(8,128)(2,1)S(1)} %get-tuple-element.73), channel_id=1, source_target_pairs={{2,0},{4,2},{6,4},{0,6},{3,1},{5,3},{7,5},{1,7},{10,8},{12,10},{14... | collective-permute-start | bytes 221192 | tf_op jit(solution)/shard_map/ppermute | solution.py:35
  15.6 0.8 copy-start.1
  19.2 11.3 %collective-permute-start.5 = (bf16[6,16,8,128]{3,2,1,0:T(8,128)(2,1)S(1)}, bf16[6,16,8,128]{3,2,1,0:T(8,128)(2,1)S(1)}, u32[]{:S(2)}, u32[]{:S(2)}) collective-permute-start(bf16[6,16,8,128]{3,2,1,0:T(8,128)(2,1)S(1)} %get-tuple-element.17), channel_id=1, source_target_pairs={{0,1},{1,0},{2,3},{3,2},{4,5},{5,4},{6,7},{7,6},{8,9},{9,8},{10,11... | collective-permute-start | bytes 589832 | tf_op jit(solution)/shard_map/ppermute | solution.py:33
  22.5 6.6 %collective-permute-start.3 = (bf16[6,6,8,128]{3,2,1,0:T(8,128)(2,1)S(1)}, bf16[6,6,8,128]{3,2,1,0:T(8,128)(2,1)S(1)}, u32[]{:S(2)}, u32[]{:S(2)}) collective-permute-start(bf16[6,6,8,128]{3,2,1,0:T(8,128)(2,1)S(1)} %get-tuple-element.48), channel_id=1, source_target_pairs={{0,2},{2,4},{4,6},{6,0},{1,3},{3,5},{5,7},{7,1},{8,10},{10,12},{12... | collective-permute-start | bytes 221192 | tf_op jit(solution)/shard_map/ppermute | solution.py:34
  24.5 6.0 %collective-permute-start.4 = (bf16[6,6,8,128]{3,2,1,0:T(8,128)(2,1)S(1)}, bf16[6,6,8,128]{3,2,1,0:T(8,128)(2,1)S(1)}, u32[]{:S(2)}, u32[]{:S(2)}) collective-permute-start(bf16[6,6,8,128]{3,2,1,0:T(8,128)(2,1)S(1)} %get-tuple-element.49), channel_id=1, source_target_pairs={{2,0},{4,2},{6,4},{0,6},{3,1},{5,3},{7,5},{1,7},{10,8},{12,10},{14... | collective-permute-start | bytes 221192 | tf_op jit(solution)/shard_map/ppermute | solution.py:35
  124.7 32.3 %all-to-all-start.4 = ((f32[32,64,128]{2,1,0:T(8,128)}), f32[32,64,128]{2,1,0:T(8,128)S(1)}, u32[]{:S(2)}, u32[]{:S(2)}) async-start(f32[32,64,128]{2,1,0:T(8,128)} %broadcast_in_dim.9), calls=%async_computation.4 | async-start | bytes 2097152 | tf_op jit(solution)/shard_map/all_to_all | solution.py:56
  176.8 19.8 %all-to-all-start.6 = ((bf16[64,6,256]{2,1,0:T(8,128)(2,1)}), bf16[64,6,256]{2,1,0:T(8,128)(2,1)S(1)}, u32[]{:S(2)}, u32[]{:S(2)}) async-start(bf16[64,6,256]{2,1,0:T(8,128)(2,1)} %reshape.51), calls=%async_computation.6 | async-start | bytes 524288 | tf_op jit(solution)/shard_map/all_to_all | solution.py:56

commit v3 on v2

--- a/solution.py
+++ b/solution.py
@@ -2,6 +2,8 @@
 
 import jax
 import jax.numpy as jnp
+import ml_dtypes
+import numpy as np
 from jax import lax
 from jax.experimental import pallas as pl
 from jax.experimental.pallas import tpu as pltpu
@@ -26,30 +28,156 @@
 NGRAM = 5
 
 
-def halo(block):
+def parts(matrix):
+    high = matrix.astype(np.float32).astype(ml_dtypes.bfloat16)
+    return high, (matrix - high.astype(np.float64)).astype(np.float32).astype(ml_dtypes.bfloat16)
+
+
+def plane_matrix(out_rows, in_rows, wy):
+    where = {row: k for k, row in enumerate(in_rows)}
+    matrix = np.zeros((len(out_rows), len(in_rows)))
+    for k, (side, x, y) in enumerate(out_rows):
+        matrix[k, where[side, x, y]] += -1.5 * COEFFS[0]
+        for offset in range(1, 7):
+            for shift in (offset, -offset):
+                matrix[k, where[side, x + shift, y]] += -0.5 * COEFFS[offset]
+                at = (side * wy + y + shift) % (2 * wy)
+                matrix[k, where[at // wy, x, at % wy]] += -0.5 * COEFFS[offset]
+    return matrix
+
+
+def line_matrix(length):
+    matrix = np.zeros((length, length))
+    at = np.arange(length)
+    for offset in range(1, 7):
+        for shift in (offset, -offset):
+            matrix[at, (at + shift) % length] += -0.5 * COEFFS[offset]
+    return np.kron(np.eye(2), matrix)
+
+
+def slab(side, first, last, wy):
+    return [(side, x, y) for x in range(first, last) for y in range(wy)]
+
+
+def pack_kernel(p_ref, v_ref, own_ref, last_ref, first_ref, clast_ref, cfirst_ref):
+    nb, rows, _ = p_ref.shape
+    wide, narrow = last_ref.shape[1], clast_ref.shape[1]
+    v = v_ref[...]
+    high = v.astype(BF)
+    low = (v - high.astype(F32)).astype(BF)
+    own_ref[:nb] = p_ref[...]
+    own_ref[nb] = high
+    own_ref[nb + 1] = low
+    last_ref[:nb] = p_ref[:, rows - wide :]
+    last_ref[nb] = high[rows - wide :]
+    last_ref[nb + 1] = low[rows - wide :]
+    first_ref[:nb] = p_ref[:, :wide]
+    first_ref[nb] = high[:wide]
+    first_ref[nb + 1] = low[:wide]
+    clast_ref[...] = p_ref[:, rows - narrow :]
+    cfirst_ref[...] = p_ref[:, :narrow]
+
+
+def stencil_kernel(
+    p_ref, v_ref, other_ref, lo_ref, hi_ref, clo_ref, chi_ref,
+    a1h_ref, a1l_ref, a2h_ref, a2l_ref, zh_ref, zl_ref, i_ref, r_ref, field,
+):
+    nb, rows, _ = p_ref.shape
+    wide, narrow = lo_ref.shape[1], clo_ref.shape[1]
+
+    def around(low, high, other):
+        return jnp.concatenate([low[wide - narrow :], high[:narrow], other], axis=0).astype(F32)
+
+    v = around(lo_ref[nb], hi_ref[nb], other_ref[nb])
+    v = v + around(lo_ref[nb + 1], hi_ref[nb + 1], other_ref[nb + 1])
+    v = jnp.concatenate([v_ref[...], v], axis=0)
+    v = jnp.concatenate([v, v], axis=1)
+    for b in range(0, nb, 2):
+        at = 0
+        for ref in (p_ref, lo_ref, hi_ref, other_ref, clo_ref, chi_ref):
+            size = ref.shape[1]
+            field[at : at + size, :BLK] = ref[b]
+            field[at : at + size, BLK:] = ref[b + 1]
+            at += size
+        f = field[...]
+        centre = jnp.concatenate(
+            [
+                f[:rows],
+                f[rows + wide - narrow : rows + wide],
+                f[rows + wide : rows + wide + narrow],
+                f[rows + 2 * wide : 2 * rows + 2 * wide],
+            ],
+            axis=0,
+        )
+        image = dot(a1h_ref[...], f) + dot(a1l_ref[...], f)
+        image = image + dot(centre, zh_ref[...]) + dot(centre, zl_ref[...])
+        centre = centre.astype(F32)
+        image = (image + v * centre).astype(BF)
+        q = (centre - TAU * image.astype(F32)).astype(BF)
+        own = q[:rows]
+        second = dot(a2h_ref[...], q) + dot(a2l_ref[...], q)
+        second = second + dot(own, zh_ref[...]) + dot(own, zl_ref[...])
+        second = (second + v[:rows] * own.astype(F32)).astype(BF)
+        i_ref[b] = image[:rows, :BLK]
+        i_ref[b + 1] = image[:rows, BLK:]
+        r_ref[b] = second[:, :BLK]
+        r_ref[b + 1] = second[:, BLK:]
+
+
+def call(kernel, outs, args, scratch=(), limit=32):
+    return pl.pallas_call(
+        kernel,
+        out_shape=tuple(outs),
+        in_specs=[pl.BlockSpec(memory_space=pltpu.VMEM)] * len(args),
+        out_specs=(pl.BlockSpec(memory_space=pltpu.VMEM),) * len(outs),
+        scratch_shapes=list(scratch),
+        compiler_params=pltpu.CompilerParams(vmem_limit_bytes=limit * 1024 * 1024),
+    )(*args)
+
+
+def images(orbitals, potential):
+    nb, wx, wy, _ = orbitals.shape
+    rows, wide, narrow = wx * wy, 12 * wy, 6 * wy
+    p = orbitals.reshape(nb, rows, BLK)
+    v = potential.reshape(rows, BLK)
+
+    def shape(count, size):
+        return jax.ShapeDtypeStruct((count, size, BLK), BF)
+
+    own, last, first, clast, cfirst = call(
+        pack_kernel,
+        [shape(nb + 2, rows)] + [shape(nb + 2, wide)] * 2 + [shape(nb, narrow)] * 2,
+        (p, v),
+    )
     count = lax.axis_size("dx")
-    up = [(i, (i + 1) % count) for i in range(count)]
+    up = [(k, (k + 1) % count) for k in range(count)]
     down = [(b, a) for a, b in up]
-    other = lax.ppermute(block, "dy", [(0, 1), (1, 0)])
-    low = lax.ppermute(block[:, block.shape[1] - 6 :], "dx", up)
-    high = lax.ppermute(block[:, :6], "dx", down)
-    return other, low, high
-
-
-def hamiltonian(block, potential):
-    other, low, high = halo(block)
-    wx, wy = block.shape[1], block.shape[2]
-    f = block.astype(F32)
-    px = jnp.concatenate([low, block, high], axis=1).astype(F32)
-    o = other.astype(F32)
-    py = jnp.concatenate([o[:, :, wy - 6 :], f, o[:, :, :6]], axis=2)
-    total = 3.0 * COEFFS[0] * f
-    for k in range(1, 7):
-        along_x = px[:, 6 + k : 6 + k + wx] + px[:, 6 - k : 6 - k + wx]
-        along_y = py[:, :, 6 + k : 6 + k + wy] + py[:, :, 6 - k : 6 - k + wy]
-        along_z = jnp.roll(f, k, 3) + jnp.roll(f, -k, 3)
-        total = total + COEFFS[k] * (along_x + along_y + along_z)
-    return (-0.5 * total + potential[None] * f).astype(BF)
+    low = lax.ppermute(last, "dx", up)
+    high = lax.ppermute(first, "dx", down)
+    other = lax.ppermute(own, "dy", [(0, 1), (1, 0)])
+    cup = [(2 * a + k, 2 * b + 1 - k) for a, b in up for k in range(2)]
+    cdown = [(2 * a + k, 2 * b + 1 - k) for a, b in down for k in range(2)]
+    clow = lax.ppermute(clast, ("dx", "dy"), cup)
+    chigh = lax.ppermute(cfirst, ("dx", "dy"), cdown)
+
+    whole = (
+        slab(0, 0, wx, wy) + slab(0, -12, 0, wy) + slab(0, wx, wx + 12, wy)
+        + slab(1, 0, wx, wy) + slab(1, -6, 0, wy) + slab(1, wx, wx + 6, wy)
+    )
+    middle = (
+        slab(0, 0, wx, wy) + slab(0, -6, 0, wy) + slab(0, wx, wx + 6, wy) + slab(1, 0, wx, wy)
+    )
+    tables = (
+        *parts(plane_matrix(middle, whole, wy)),
+        *parts(plane_matrix(slab(0, 0, wx, wy), middle, wy)),
+        *parts(line_matrix(BLK)),
+    )
+    return call(
+        stencil_kernel,
+        [shape(nb, rows)] * 2,
+        (p, v, other, low, high, clow, chigh) + tuple(jnp.asarray(t) for t in tables),
+        [pltpu.VMEM((len(whole), 2 * BLK), BF)],
+    )
 
 
 def swap(x, axes):
@@ -75,10 +203,11 @@
 
 def reduced(rows):
     n_near, n_far = axes_size(NEAR), axes_size(FAR)
-    half = swap(rows.reshape(2, -1, BLK), "core").sum(0)
+    half = swap(rows.astype(BF).reshape(2, -1, BLK), "core").astype(F32).sum(0)
     part = swap(half.astype(BF).reshape(n_near, -1, BLK), NEAR).astype(F32).sum(0)
-    mine = spread(part, FAR, n_far).sum(0)
-    half = spread(mine, NEAR, n_near).reshape(-1, BLK)
+    mine = swap(part.reshape(n_far, -1, BLK), FAR).sum(0)
+    part = spread(mine, FAR, n_far).reshape(-1, BLK)
+    half = spread(part, NEAR, n_near).reshape(-1, BLK)
     return spread(half, "core", 2).reshape(-1, BLK)
 
 
@@ -159,17 +288,13 @@
 
 def algebra(rows, p, i, r, volume):
     n, chunk = p.shape
-    return pl.pallas_call(
+    return call(
         functools.partial(algebra_kernel, volume),
-        out_shape=(
-            jax.ShapeDtypeStruct((n, chunk), BF),
-            jax.ShapeDtypeStruct((n, n), F32),
-        ),
-        in_specs=[pl.BlockSpec(memory_space=pltpu.VMEM)] * 4,
-        out_specs=(pl.BlockSpec(memory_space=pltpu.VMEM),) * 2,
-        scratch_shapes=[pltpu.VMEM((NGRAM, n, n), F32)],
-        compiler_params=pltpu.CompilerParams(vmem_limit_bytes=48 * 1024 * 1024),
-    )(rows, p, i, r)
+        [jax.ShapeDtypeStruct((n, chunk), BF), jax.ShapeDtypeStruct((n, n), F32)],
+        (rows, p, i, r),
+        [pltpu.VMEM((NGRAM, n, n), F32)],
+        48,
+    )
 
 
 def per_device(orbitals, potential):
@@ -181,11 +306,9 @@
     chunk = cells // n_band
     volume = 1.0 / (cells * lax.axis_size("dx") * lax.axis_size("dy"))
 
-    image = hamiltonian(orbitals, potential)
-    q = (orbitals.astype(F32) - TAU * image.astype(F32)).astype(BF)
-    image_q = hamiltonian(q, potential)
-
-    send = jnp.stack([orbitals, image, image_q]).reshape(3, nb, n_band, chunk // BLK, BLK)
+    image, image_q = images(orbitals, potential)
+
+    send = jnp.stack([orbitals.reshape(image.shape), image, image_q]).reshape(3, nb, n_band, chunk // BLK, BLK)
     send = send.transpose(2, 0, 1, 3, 4).reshape(n_band, -1, BLK)
     got = swap(send, BAND).reshape(n_band, 3, nb, chunk // BLK, BLK)
     p, i, r = got.transpose(1, 0, 2, 3, 4).reshape(3, bands, chunk)
@@ -207,8 +330,8 @@
 
 def solution(mesh):
     n_band, n_dx, n_dy = mesh.devices.shape
-    near = min(4, n_band // 2)
-    far = min(2, n_band // 2 // near)
+    near = min(2, n_band // 2)
+    far = min(4, n_band // 2 // near)
     fine = Mesh(mesh.devices.reshape(-1, far, near, 2, n_dx, n_dy), BAND + ("dx", "dy"))
     in_specs = (P(BAND, "dx", "dy", None), P("dx", "dy", None))
     out_specs = (P(BAND, "dx", "dy", None), P(None, BAND))

time: 198 us -> 184 us (0.929)
  waiting for transfers between devices: 38.4 us -> 24.3 us
  starting transfers between devices: 33.9 us -> 28 us
  blocking collectives: 93.9 us -> 99.8 us
  other arithmetic: 6.9 us -> 1.71 us
  Pallas kernels: 10.2 us -> 13.3 us
    all_to_all x2, waiting for transfers between devices: 37.1 us -> 22.8 us  [swap(): return lax.all_to_all(x, axes, split_axis=0, concat_axis=0, tiled=True)]
    unnamed x30 -> x42, local copies, waits for them, and re-layouts: 1.57 us -> 8.38 us
    all_to_all x5 -> x6, blocking collectives: 93.9 us -> 99.8 us  [swap(): return lax.all_to_all(x, axes, split_axis=0, concat_axis=0, tiled=True)]
    convert_element_type x5 -> x0, other arithmetic: 5.57 us -> none  [the longest x2 2.75 us: hamiltonian(): f = block.astype(F32)]
    slice x28 -> x0, local copies, waits for them, and re-layouts: 5.08 us -> none  [the longest x24 4 us: hamiltonian(): along_z = jnp.roll(f, k, 3) + jnp.roll(f, -k, 3)]
    all_to_all x2, starting transfers between devices: 14 us -> 9.29 us  [swap(): return lax.all_to_all(x, axes, split_axis=0, concat_axis=0, tiled=True)]
    pallas_call x1 -> x3, Pallas kernels: 10.2 us -> 13.3 us  [call(): pl.pallas_call(kernel, out_shape=tuple(outs), in_specs=[pl.BlockSpec(memo...]
    ppermute x6 -> x5, starting transfers between devices: 19.9 us -> 18.7 us  [the longest x1 5.47 us: images(): chigh = lax.ppermute(cfirst, ('dx', 'dy'), cdown)]
  transfers between devices with their start and end apart: 8 -> 7, of which waited for: 3 -> 3; matrix products, arithmetic and copies ran while one was open for 3% -> 0% of each run, Pallas kernels for 0% -> 0%
where the time goes in v3:
time: 184 us; the launch traced here: 183 us
  blocking collectives  99.8 us (54%)
  starting transfers between devices  28 us (15%)
  waiting for transfers between devices  24.3 us (13%)
  Pallas kernels  13.3 us (7%)
  local copies, waits for them, and re-layouts  13.1 us (7%)
    all_to_all x6, blocking collectives, swap(): return lax.all_to_all(x, axes, split_axis=0, concat_axis=0, tiled=True)  99.8 us
    all_to_all x2, waiting for transfers between devices, swap(): return lax.all_to_all(x, axes, split_axis=0, concat_axis=0, tiled=True)  22.8 us
    pallas_call x3, Pallas kernels, call(): pl.pallas_call(kernel, out_shape=tuple(outs), in_specs=[pl.BlockSpec(memo...  13.3 us
    all_to_all x2, starting transfers between devices, swap(): return lax.all_to_all(x, axes, split_axis=0, concat_axis=0, tiled=True)  9.29 us
    unnamed x42, local copies, waits for them, and re-layouts  8.38 us
    ppermute x1, starting transfers between devices, images(): chigh = lax.ppermute(cfirst, ('dx', 'dy'), cdown)  5.47 us
    ppermute x1, starting transfers between devices, images(): other = lax.ppermute(own, 'dy', [(0, 1), (1, 0)])  4.83 us
  transfers between devices with their start and end apart: 7, of which 3 were waited for; matrix products, arithmetic and copies ran while one was open for 0% of the time, Pallas kernels for 0%

profile of v3, /device:TPU:1, one launch (start us, length us, event | category | flops | bytes accessed | tf_op | source)
XLA Modules:
  0.0 182.7 jit_solution(3721903439840975266)
XLA Ops:
  0.6 0.9 copy-done
  1.6 0.8 copy-done.3
  2.5 4.8 %collective-permute-start = (bf16[8,128,128]{2,1,0:T(8,128)(2,1)S(1)}, bf16[8,128,128]{2,1,0:T(8,128)(2,1)S(1)}, u32[]{:S(2)}, u32[]{:S(2)}) collective-permute-start(bf16[8,128,128]{2,1,0:T(8,128)(2,1)S(1)} %get-tuple-element.11), channel_id=1, source_target_pairs={{0,1},{1,0},{2,3},{3,2},{4,5},{5,4},{6,7},{7,6},{8,9},{9,8},{10,11... | collective-permute-start | bytes 786440 | tf_op jit(solution)/shard_map/ppermute | solution.py:157
  7.3 3.1 %collective-permute-start.1 = (bf16[8,96,128]{2,1,0:T(8,128)(2,1)S(1)}, bf16[8,96,128]{2,1,0:T(8,128)(2,1)S(1)}, u32[]{:S(2)}, u32[]{:S(2)}) collective-permute-start(bf16[8,96,128]{2,1,0:T(8,128)(2,1)S(1)} %get-tuple-element.12), channel_id=1, source_target_pairs={{0,2},{2,4},{4,6},{6,0},{1,3},{3,5},{5,7},{7,1},{8,10},{10,12},{12... | collective-permute-start | bytes 589832 | tf_op jit(solution)/shard_map/ppermute | solution.py:155
  10.5 3.4 %collective-permute-start.2 = (bf16[8,96,128]{2,1,0:T(8,128)(2,1)S(1)}, bf16[8,96,128]{2,1,0:T(8,128)(2,1)S(1)}, u32[]{:S(2)}, u32[]{:S(2)}) collective-permute-start(bf16[8,96,128]{2,1,0:T(8,128)(2,1)S(1)} %get-tuple-element.13), channel_id=1, source_target_pairs={{2,0},{4,2},{6,4},{0,6},{3,1},{5,3},{7,5},{1,7},{10,8},{12,10},{14... | collective-permute-start | bytes 589832 | tf_op jit(solution)/shard_map/ppermute | solution.py:156
  13.8 1.9 %collective-permute-start.3 = (bf16[6,48,128]{2,1,0:T(8,128)(2,1)S(1)}, bf16[6,48,128]{2,1,0:T(8,128)(2,1)S(1)}, u32[]{:S(2)}, u32[]{:S(2)}) collective-permute-start(bf16[6,48,128]{2,1,0:T(8,128)(2,1)S(1)} %get-tuple-element.14), channel_id=1, source_target_pairs={{0,3},{1,2},{2,5},{3,4},{4,7},{5,6},{6,1},{7,0},{8,11},{9,10},{10,... | collective-permute-start | bytes 221192 | tf_op jit(solution)/shard_map/ppermute | solution.py:160
  15.8 5.5 %collective-permute-start.4 = (bf16[6,48,128]{2,1,0:T(8,128)(2,1)S(1)}, bf16[6,48,128]{2,1,0:T(8,128)(2,1)S(1)}, u32[]{:S(2)}, u32[]{:S(2)}) collective-permute-start(bf16[6,48,128]{2,1,0:T(8,128)(2,1)S(1)} %get-tuple-element.15), channel_id=1, source_target_pairs={{2,1},{3,0},{4,3},{5,2},{6,5},{7,4},{0,7},{1,6},{10,9},{11,8},{12,... | collective-permute-start | bytes 221192 | tf_op jit(solution)/shard_map/ppermute | solution.py:161
  21.3 1.5 collective-permute-done.4.chi_ref
  22.8 1.0 copy-done.1
  23.8 1.0 copy-done.2
  24.8 0.9 copy-done.4
  25.7 0.9 copy-done.5
  26.6 0.9 copy-done.6
  27.5 0.9 copy-done.7
  28.4 3.1 %shard_map.96 = (bf16[6,128,128]{2,1,0:T(8,128)(2,1)S(1)}, bf16[6,128,128]{2,1,0:T(8,128)(2,1)S(1)}) custom-call(bf16[6,128,128]{2,1,0:T(8,128)(2,1)S(1)} %bitcast.50, f32[128,128]{1,0:T(8,128)S(1)} %bitcast.54, bf16[8,128,128]{2,1,0:T(8,128)(2,1)S(1)} %collective-permute-done.other_ref, bf16[8,96,128]{2,1,0:T(8,128)(2,1)S(1)} %collective-permute-done.1.lo_ref, ...), custom_call_target="tpu_custom_call" | custom-call | tf_op jit(solution)/shard_map/pallas_call | solution.py:128
  31.5 1.0 maximum_bitcast_fusion
  32.5 0.1 copy.36
  32.6 0.4 copy.37
  33.0 38.9 %all_to_all.40 = bf16[64,36,128]{2,1,0:T(8,128)(2,1)S(1)} all-to-all(bf16[64,36,128]{2,1,0:T(8,128)(2,1)S(1)} %copy.37), channel_id=1, replica_groups=mesh['zhi'=4,'yh'=4,'yl'=2,'core'=2,'dx'=4,'dy'=2] {'zhi','yh','yl','core'}, dimensions={0} | all-to-all | bytes 1179648 | tf_op jit(solution)/shard_map/all_to_all | solution.py:184
  71.9 0.1 copy.38
  72.1 0.1 subtract_convert_fusion
  72.3 0.2 copy.39
  72.5 0.3 convolution_convert_fusion.4
  72.8 0.2 copy.40
  73.1 0.3 convolution_convert_fusion.3
  73.4 0.2 copy.41
  73.6 0.3 convolution_convert_fusion.2
  74.0 0.2 copy.42
  74.2 0.3 convolution_convert_fusion.1
  74.6 0.2 copy.43
  74.8 0.3 convolution_convert_fusion
  75.3 5.3 %all_to_all.41 = bf16[2,2048,128]{2,1,0:T(8,128)(2,1)S(1)} all-to-all(bf16[2,2048,128]{2,1,0:T(8,128)(2,1)S(1)} %bitcast.60), channel_id=1, replica_groups=mesh['zhi'=4,'yh'=4,'yl'=2,'core'=2,'dx'=4,'dy'=2] {'core'}, dimensions={0} | all-to-all | bytes 2097152 | tf_op jit(solution)/shard_map/all_to_all | solution.py:184
  80.6 0.5 reduce_sum.30
  81.1 13.6 %all_to_all.42 = bf16[16,128,128]{2,1,0:T(8,128)(2,1)S(1)} all-to-all(bf16[16,128,128]{2,1,0:T(8,128)(2,1)S(1)} %bitcast.68), channel_id=1, replica_groups=mesh['zhi'=4,'yh'=4,'yl'=2,'core'=2,'dx'=4,'dy'=2] {'dx','dy','yl'}, dimensions={0} | all-to-all | bytes 1048576 | tf_op jit(solution)/shard_map/all_to_all | solution.py:184
  94.8 16.7 %all_to_all.43 = f32[16,8,128]{2,1,0:T(8,128)S(1)} all-to-all(f32[16,8,128]{2,1,0:T(8,128)S(1)} %bitcast.75), channel_id=1, replica_groups=mesh['zhi'=4,'yh'=4,'yl'=2,'core'=2,'dx'=4,'dy'=2] {'zhi','yh'}, dimensions={0} | all-to-all | bytes 131072 | tf_op jit(solution)/shard_map/all_to_all | solution.py:184
  111.6 13.9 %all_to_all.44 = f32[16,8,128]{2,1,0:T(8,128)S(1)} all-to-all(f32[16,8,128]{2,1,0:T(8,128)S(1)} %broadcast_in_dim.20), channel_id=1, replica_groups=mesh['zhi'=4,'yh'=4,'yl'=2,'core'=2,'dx'=4,'dy'=2] {'zhi','yh'}, dimensions={0} | all-to-all | bytes 131072 | tf_op jit(solution)/shard_map/all_to_all | solution.py:184
  125.4 1.1 broadcast_in_dim.22
  126.5 4.9 %all-to-all-start.5 = ((f32[16,128,128]{2,1,0:T(8,128)}), f32[16,128,128]{2,1,0:T(8,128)S(1)}, u32[]{:S(2)}, u32[]{:S(2)}) async-start(f32[16,128,128]{2,1,0:T(8,128)} %broadcast_in_dim.22), calls=%async_computation.5 | async-start | bytes 2097152 | tf_op jit(solution)/shard_map/all_to_all | solution.py:184
  131.6 9.6 %all-to-all-done.5 = f32[16,128,128]{2,1,0:T(8,128)S(1)} async-done(((f32[16,128,128]{2,1,0:T(8,128)}), f32[16,128,128]{2,1,0:T(8,128)S(1)}, u32[]{:S(2)}, u32[]{:S(2)}) %all-to-all-start.5) | async-done | bytes 1048608 | tf_op jit(solution)/shard_map/all_to_all | solution.py:184
  141.2 0.1 broadcast_in_dim.24
  141.4 11.3 %all_to_all.45 = f32[2,2048,128]{2,1,0:T(8,128)S(1)} all-to-all(f32[2,2048,128]{2,1,0:T(8,128)S(1)} %broadcast_in_dim.24), channel_id=1, replica_groups=mesh['zhi'=4,'yh'=4,'yl'=2,'core'=2,'dx'=4,'dy'=2] {'core'}, dimensions={0} | all-to-all | bytes 4194304 | tf_op jit(solution)/shard_map/all_to_all | solution.py:184
  152.7 10.2 %shard_map.97 = (bf16[384,256]{1,0:T(8,128)(2,1)S(1)}, f32[384,384]{1,0:T(8,128)S(1)}) custom-call(f32[4096,128]{1,0:T(8,128)S(1)} %bitcast.48, bf16[384,256]{1,0:T(8,128)(2,1)S(1)} %bitcast.52, bf16[384,256]{1,0:T(8,128)(2,1)S(1)} %get-tuple-element.36.i_ref, bf16[384,256]{1,0:T(8,128)(2,1)S(1)} %get-tuple-element.35.r_ref), custom_call_target="tpu_custom_call" | custom-call | tf_op jit(solution)/shard_map/pallas_call | solution.py:128
  162.8 0.8 reshape.63
  163.6 4.4 %all-to-all-start.7 = ((bf16[64,6,256]{2,1,0:T(8,128)(2,1)}), bf16[64,6,256]{2,1,0:T(8,128)(2,1)S(1)}, u32[]{:S(2)}, u32[]{:S(2)}) async-start(bf16[64,6,256]{2,1,0:T(8,128)(2,1)} %reshape.63), calls=%async_computation.7 | async-start | bytes 524288 | tf_op jit(solution)/shard_map/all_to_all | solution.py:184
  168.0 0.1 constant_dynamic-slice_fusion
  168.1 0.7 copy.45
  168.8 13.1 %all-to-all-done.7 = bf16[64,6,256]{2,1,0:T(8,128)(2,1)S(1)} async-done(((bf16[64,6,256]{2,1,0:T(8,128)(2,1)}), bf16[64,6,256]{2,1,0:T(8,128)(2,1)S(1)}, u32[]{:S(2)}, u32[]{:S(2)}) %all-to-all-start.7) | async-done | bytes 196640 | tf_op jit(solution)/shard_map/all_to_all | solution.py:184
  182.0 0.7 reshape.64
  (46 shorter events, 0.7 us)
Async XLA Ops:
  0.6 0.9 copy-start
  1.6 0.8 copy-start.3
  2.5 20.3 %collective-permute-start = (bf16[8,128,128]{2,1,0:T(8,128)(2,1)S(1)}, bf16[8,128,128]{2,1,0:T(8,128)(2,1)S(1)}, u32[]{:S(2)}, u32[]{:S(2)}) collective-permute-start(bf16[8,128,128]{2,1,0:T(8,128)(2,1)S(1)} %get-tuple-element.11), channel_id=1, source_target_pairs={{0,1},{1,0},{2,3},{3,2},{4,5},{5,4},{6,7},{7,6},{8,9},{9,8},{10,11... | collective-permute-start | bytes 786440 | tf_op jit(solution)/shard_map/ppermute | solution.py:157
  7.3 15.5 %collective-permute-start.1 = (bf16[8,96,128]{2,1,0:T(8,128)(2,1)S(1)}, bf16[8,96,128]{2,1,0:T(8,128)(2,1)S(1)}, u32[]{:S(2)}, u32[]{:S(2)}) collective-permute-start(bf16[8,96,128]{2,1,0:T(8,128)(2,1)S(1)} %get-tuple-element.12), channel_id=1, source_target_pairs={{0,2},{2,4},{4,6},{6,0},{1,3},{3,5},{5,7},{7,1},{8,10},{10,12},{12... | collective-permute-start | bytes 589832 | tf_op jit(solution)/shard_map/ppermute | solution.py:155
  10.5 12.3 %collective-permute-start.2 = (bf16[8,96,128]{2,1,0:T(8,128)(2,1)S(1)}, bf16[8,96,128]{2,1,0:T(8,128)(2,1)S(1)}, u32[]{:S(2)}, u32[]{:S(2)}) collective-permute-start(bf16[8,96,128]{2,1,0:T(8,128)(2,1)S(1)} %get-tuple-element.13), channel_id=1, source_target_pairs={{2,0},{4,2},{6,4},{0,6},{3,1},{5,3},{7,5},{1,7},{10,8},{12,10},{14... | collective-permute-start | bytes 589832 | tf_op jit(solution)/shard_map/ppermute | solution.py:156
  13.8 7.4 %collective-permute-start.3 = (bf16[6,48,128]{2,1,0:T(8,128)(2,1)S(1)}, bf16[6,48,128]{2,1,0:T(8,128)(2,1)S(1)}, u32[]{:S(2)}, u32[]{:S(2)}) collective-permute-start(bf16[6,48,128]{2,1,0:T(8,128)(2,1)S(1)} %get-tuple-element.14), channel_id=1, source_target_pairs={{0,3},{1,2},{2,5},{3,4},{4,7},{5,6},{6,1},{7,0},{8,11},{9,10},{10,... | collective-permute-start | bytes 221192 | tf_op jit(solution)/shard_map/ppermute | solution.py:160
  15.8 7.0 %collective-permute-start.4 = (bf16[6,48,128]{2,1,0:T(8,128)(2,1)S(1)}, bf16[6,48,128]{2,1,0:T(8,128)(2,1)S(1)}, u32[]{:S(2)}, u32[]{:S(2)}) collective-permute-start(bf16[6,48,128]{2,1,0:T(8,128)(2,1)S(1)} %get-tuple-element.15), channel_id=1, source_target_pairs={{2,1},{3,0},{4,3},{5,2},{6,5},{7,4},{0,7},{1,6},{10,9},{11,8},{12,... | collective-permute-start | bytes 221192 | tf_op jit(solution)/shard_map/ppermute | solution.py:161
  22.8 1.0 copy-start.1
  23.8 1.0 copy-start.2
  24.8 0.9 copy-start.4
  25.7 0.9 copy-start.5
  26.6 0.9 copy-start.6
  27.5 0.9 copy-start.7
  126.5 14.7 %all-to-all-start.5 = ((f32[16,128,128]{2,1,0:T(8,128)}), f32[16,128,128]{2,1,0:T(8,128)S(1)}, u32[]{:S(2)}, u32[]{:S(2)}) async-start(f32[16,128,128]{2,1,0:T(8,128)} %broadcast_in_dim.22), calls=%async_computation.5 | async-start | bytes 2097152 | tf_op jit(solution)/shard_map/all_to_all | solution.py:184
  163.6 18.3 %all-to-all-start.7 = ((bf16[64,6,256]{2,1,0:T(8,128)(2,1)}), bf16[64,6,256]{2,1,0:T(8,128)(2,1)S(1)}, u32[]{:S(2)}, u32[]{:S(2)}) async-start(bf16[64,6,256]{2,1,0:T(8,128)(2,1)} %reshape.63), calls=%async_computation.7 | async-start | bytes 524288 | tf_op jit(solution)/shard_map/all_to_all | solution.py:184

commit v4 on v3

--- a/solution.py
+++ b/solution.py
@@ -22,7 +22,6 @@
 BF = jnp.bfloat16
 F32 = jnp.float32
 BAND = ("zhi", "yh", "yl", "core")
-FAR = ("zhi", "yh")
 NEAR = ("dx", "dy", "yl")
 BLK = 128
 NGRAM = 5
@@ -59,39 +58,49 @@
     return [(side, x, y) for x in range(first, last) for y in range(wy)]
 
 
-def pack_kernel(p_ref, v_ref, own_ref, last_ref, first_ref, clast_ref, cfirst_ref):
+def pack_kernel(
+    p_hbm, v_hbm, own_ref, last_ref, first_ref, clast_ref, cfirst_ref, v_ref, p_ref, sems
+):
+    copies = [
+        pltpu.make_async_copy(p_hbm, p_ref, sems.at[0]),
+        pltpu.make_async_copy(v_hbm, v_ref, sems.at[1]),
+    ]
+    for copy in copies:
+        copy.start()
+    for copy in copies:
+        copy.wait()
     nb, rows, _ = p_ref.shape
     wide, narrow = last_ref.shape[1], clast_ref.shape[1]
-    v = v_ref[...]
-    high = v.astype(BF)
-    low = (v - high.astype(F32)).astype(BF)
+    v = v_ref[...].astype(BF)
     own_ref[:nb] = p_ref[...]
-    own_ref[nb] = high
-    own_ref[nb + 1] = low
+    own_ref[nb] = v
     last_ref[:nb] = p_ref[:, rows - wide :]
-    last_ref[nb] = high[rows - wide :]
-    last_ref[nb + 1] = low[rows - wide :]
+    last_ref[nb] = v[rows - wide :]
     first_ref[:nb] = p_ref[:, :wide]
-    first_ref[nb] = high[:wide]
-    first_ref[nb + 1] = low[:wide]
+    first_ref[nb] = v[:wide]
     clast_ref[...] = p_ref[:, rows - narrow :]
     cfirst_ref[...] = p_ref[:, :narrow]
 
 
 def stencil_kernel(
     p_ref, v_ref, other_ref, lo_ref, hi_ref, clo_ref, chi_ref,
-    a1h_ref, a1l_ref, a2h_ref, a2l_ref, zh_ref, zl_ref, i_ref, r_ref, field,
+    a1h, a1l, a2h, a2l, zh, zl, i_ref, r_ref, field,
+    a1h_ref, a1l_ref, a2h_ref, a2l_ref, zh_ref, zl_ref, sems,
 ):
-    nb, rows, _ = p_ref.shape
+    tables = ((a1h, a1h_ref), (a1l, a1l_ref), (zh, zh_ref), (zl, zl_ref), (a2h, a2h_ref), (a2l, a2l_ref))
+    copies = [pltpu.make_async_copy(a, b, sems.at[k]) for k, (a, b) in enumerate(tables)]
+    for copy in copies:
+        copy.start()
+    nb, rows, _ = i_ref.shape
     wide, narrow = lo_ref.shape[1], clo_ref.shape[1]
 
     def around(low, high, other):
         return jnp.concatenate([low[wide - narrow :], high[:narrow], other], axis=0).astype(F32)
 
-    v = around(lo_ref[nb], hi_ref[nb], other_ref[nb])
-    v = v + around(lo_ref[nb + 1], hi_ref[nb + 1], other_ref[nb + 1])
-    v = jnp.concatenate([v_ref[...], v], axis=0)
+    v = jnp.concatenate([v_ref[...], around(lo_ref[nb], hi_ref[nb], other_ref[nb])], axis=0)
     v = jnp.concatenate([v, v], axis=1)
+    for copy in copies:
+        copy.wait()
     for b in range(0, nb, 2):
         at = 0
         for ref in (p_ref, lo_ref, hi_ref, other_ref, clo_ref, chi_ref):
@@ -124,11 +133,12 @@
         r_ref[b + 1] = second[:, BLK:]
 
 
-def call(kernel, outs, args, scratch=(), limit=32):
+def call(kernel, outs, args, scratch=(), limit=32, hbm=0):
+    specs = [pl.BlockSpec(memory_space=pltpu.VMEM)] * (len(args) - hbm)
     return pl.pallas_call(
         kernel,
         out_shape=tuple(outs),
-        in_specs=[pl.BlockSpec(memory_space=pltpu.VMEM)] * len(args),
+        in_specs=specs + [pl.BlockSpec(memory_space=pl.ANY)] * hbm,
         out_specs=(pl.BlockSpec(memory_space=pltpu.VMEM),) * len(outs),
         scratch_shapes=list(scratch),
         compiler_params=pltpu.CompilerParams(vmem_limit_bytes=limit * 1024 * 1024),
@@ -144,10 +154,13 @@
     def shape(count, size):
         return jax.ShapeDtypeStruct((count, size, BLK), BF)
 
-    own, last, first, clast, cfirst = call(
+    own, last, first, clast, cfirst, v = call(
         pack_kernel,
-        [shape(nb + 2, rows)] + [shape(nb + 2, wide)] * 2 + [shape(nb, narrow)] * 2,
+        [shape(nb + 1, rows)] + [shape(nb + 1, wide)] * 2 + [shape(nb, narrow)] * 2
+        + [jax.ShapeDtypeStruct((rows, BLK), F32)],
         (p, v),
+        [pltpu.VMEM(p.shape, BF), pltpu.SemaphoreType.DMA((2,))],
+        hbm=2,
     )
     count = lax.axis_size("dx")
     up = [(k, (k + 1) % count) for k in range(count)]
@@ -172,12 +185,16 @@
         *parts(plane_matrix(slab(0, 0, wx, wy), middle, wy)),
         *parts(line_matrix(BLK)),
     )
-    return call(
+    image, image_q = call(
         stencil_kernel,
         [shape(nb, rows)] * 2,
-        (p, v, other, low, high, clow, chigh) + tuple(jnp.asarray(t) for t in tables),
-        [pltpu.VMEM((len(whole), 2 * BLK), BF)],
-    )
+        (own, v, other, low, high, clow, chigh) + tuple(jnp.asarray(t) for t in tables),
+        [pltpu.VMEM((len(whole), 2 * BLK), BF)]
+        + [pltpu.VMEM(t.shape, BF) for t in tables]
+        + [pltpu.SemaphoreType.DMA((len(tables),))],
+        hbm=len(tables),
+    )
+    return own[:nb], image, image_q
 
 
 def swap(x, axes):
@@ -188,25 +205,58 @@
     return swap(jnp.broadcast_to(x[None], (size,) + x.shape), axes)
 
 
-def gram(a, b):
-    return lax.dot_general(a, b, (((1,), (1,)), ((), ())), preferred_element_type=F32)
-
-
 def pairs(nblk):
     return [(r, c) for r in range(nblk) for c in range(r, nblk)]
 
 
-def pack(g):
-    nblk = g.shape[0] // BLK
-    return [g[r * BLK : (r + 1) * BLK, c * BLK : (c + 1) * BLK] for r, c in pairs(nblk)]
+def tri(n):
+    return lax.broadcasted_iota(jnp.int32, (n, n), 0), lax.broadcasted_iota(jnp.int32, (n, n), 1)
+
+
+def gram_kernel(p_ref, i_ref, r_ref, rows_ref):
+    p, i, r = p_ref[...], i_ref[...], r_ref[...]
+    n = p.shape[0]
+    nblk = n // BLK
+    qf = p.astype(F32) - TAU * i.astype(F32)
+    q = qf.astype(BF)
+    t = (qf - TAU * r.astype(F32)).astype(BF)
+
+    def gram(a, b):
+        return lax.dot_general(a, b, (((1,), (1,)), ((), ())), preferred_element_type=F32)
+
+    s, g1, hw, hw2, w4 = gram(p, p), gram(i, p), gram(q, i), gram(r, q), gram(t, t)
+    row, col = tri(n)
+    at = 0
+    for a, b in ((s, g1), (hw, hw2)):
+        square = jnp.where(row > col, b, a).astype(BF)
+        for c in range(nblk):
+            rows_ref[at : at + n] = square[:, c * BLK : (c + 1) * BLK]
+            at += n
+    row, col = tri(BLK)
+
+    def diagonal(g, k):
+        block = g[k * BLK : (k + 1) * BLK, k * BLK : (k + 1) * BLK]
+        return jnp.sum(jnp.where(row == col, block, 0.0), axis=0, keepdims=True)
+
+    for k, c in pairs(nblk):
+        block = w4[k * BLK : (k + 1) * BLK, c * BLK : (c + 1) * BLK]
+        if k == c:
+            first, second = diagonal(g1, k), diagonal(hw2, k)
+            for at_row, line in (
+                (BLK - 4, first), (BLK - 3, pltpu.roll(first, 64, 1)),
+                (BLK - 2, second), (BLK - 1, pltpu.roll(second, 64, 1)),
+            ):
+                block = jnp.where((row == at_row) & (col < 64), line, block)
+        rows_ref[at : at + BLK] = block.astype(BF)
+        at += BLK
 
 
 def reduced(rows):
-    n_near, n_far = axes_size(NEAR), axes_size(FAR)
-    half = swap(rows.astype(BF).reshape(2, -1, BLK), "core").astype(F32).sum(0)
+    n_near = axes_size(NEAR)
+    half = swap(rows.reshape(2, -1, BLK), "core").astype(F32).sum(0)
     part = swap(half.astype(BF).reshape(n_near, -1, BLK), NEAR).astype(F32).sum(0)
-    mine = swap(part.reshape(n_far, -1, BLK), FAR).sum(0)
-    part = spread(mine, FAR, n_far).reshape(-1, BLK)
+    part = spread(part.astype(BF), "zhi", lax.axis_size("zhi")).astype(F32).sum(0)
+    part = spread(part, "yh", lax.axis_size("yh")).sum(0)
     half = spread(part, NEAR, n_near).reshape(-1, BLK)
     return spread(half, "core", 2).reshape(-1, BLK)
 
@@ -230,20 +280,43 @@
 def algebra_kernel(volume, rows_ref, p_ref, i_ref, r_ref, psi_ref, h_ref, mats):
     n = p_ref.shape[0]
     nblk = n // BLK
-    spots = pairs(nblk)
-    for g in range(NGRAM):
-        for b, (r, c) in enumerate(spots):
-            at = (g * len(spots) + b) * BLK
-            tile = rows_ref[at : at + BLK] * volume
-            mats[g, r * BLK : (r + 1) * BLK, c * BLK : (c + 1) * BLK] = tile
-            if r != c:
-                mats[g, c * BLK : (c + 1) * BLK, r * BLK : (r + 1) * BLK] = tile.T
+    row, col = tri(BLK)
+
+    def put(g, r, c, tile):
+        mats[g, r * BLK : (r + 1) * BLK, c * BLK : (c + 1) * BLK] = tile
+
+    at = 2 * nblk * n
+    lines = {}
+    for r, c in pairs(nblk):
+        tile = rows_ref[at : at + BLK] * volume
+        at += BLK
+        if r == c:
+            for g, k in ((1, BLK - 4), (3, BLK - 2)):
+                second = pltpu.roll(tile[k + 1 : k + 2], 64, 1)
+                lines[g, r] = jnp.where(col[:1] < 64, tile[k : k + 1], second)
+            put(4, r, r, jnp.where(row <= col, tile, tile.T))
+        else:
+            put(4, r, c, tile)
+            put(4, c, r, tile.T)
+    for g in (0, 2):
+        for r in range(nblk):
+            for c in range(nblk):
+                at = (g // 2 * nblk + c) * n + r * BLK
+                tile = rows_ref[at : at + BLK] * volume
+                flip = tile.T
+                if r == c:
+                    put(g, r, r, jnp.where(row <= col, tile, flip))
+                    other = jnp.where(row >= col, tile, flip)
+                    put(g + 1, r, r, jnp.where(row == col, lines[g + 1, r], other))
+                else:
+                    to = g if r < c else g + 1
+                    put(to, r, c, tile)
+                    put(to, c, r, flip)
     s, g1, hw, hw2, w4 = (mats[g] for g in range(NGRAM))
     w1 = s - TAU * g1
     w2 = w1 - TAU * hw
     w3 = w2 - TAU * hw2
-    row = lax.broadcasted_iota(jnp.int32, (n, n), 0)
-    col = lax.broadcasted_iota(jnp.int32, (n, n), 1)
+    row, col = tri(n)
     diag = jnp.where(row == col, 1.5, 0.0).astype(F32)
 
     def left(h, x):
@@ -306,20 +379,15 @@
     chunk = cells // n_band
     volume = 1.0 / (cells * lax.axis_size("dx") * lax.axis_size("dy"))
 
-    image, image_q = images(orbitals, potential)
-
-    send = jnp.stack([orbitals.reshape(image.shape), image, image_q]).reshape(3, nb, n_band, chunk // BLK, BLK)
+    psi, image, image_q = images(orbitals, potential)
+
+    send = jnp.stack([psi, image, image_q]).reshape(3, nb, n_band, chunk // BLK, BLK)
     send = send.transpose(2, 0, 1, 3, 4).reshape(n_band, -1, BLK)
     got = swap(send, BAND).reshape(n_band, 3, nb, chunk // BLK, BLK)
     p, i, r = got.transpose(1, 0, 2, 3, 4).reshape(3, bands, chunk)
 
-    qf = p.astype(F32) - TAU * i.astype(F32)
-    qb = qf.astype(BF)
-    tb = (qf - TAU * r.astype(F32)).astype(BF)
-    grams = [gram(p, p), gram(p, i), gram(qb, i), gram(qb, r), gram(tb, tb)]
-    rows = jnp.concatenate([b for g in grams for b in pack(g)], axis=0)
-    unit = 8 * n_band * lax.axis_size("dx") * lax.axis_size("dy")
-    rows = jnp.pad(rows, ((0, -rows.shape[0] % unit), (0, 0)))
+    count = bands // BLK * 2 * bands + len(pairs(bands // BLK)) * BLK
+    (rows,) = call(gram_kernel, [jax.ShapeDtypeStruct((count, BLK), BF)], (p, i, r))
     psi2, h2 = algebra(reduced(rows), p, i, r, volume)
 
     back = swap(psi2.reshape(n_band, nb, chunk), BAND)

time: 184 us -> 170 us (0.924)
  waiting for transfers between devices: 24.3 us -> 14.5 us
  starting transfers between devices: 28 us -> 23.7 us
  blocking collectives: 99.8 us -> 103 us
  Pallas kernels: 13.3 us -> 15.6 us
    all_to_all x2 -> x1, waiting for transfers between devices: 22.8 us -> 13 us  [swap(): return lax.all_to_all(x, axes, split_axis=0, concat_axis=0, tiled=True)]
    all_to_all x2 -> x1, starting transfers between devices: 9.29 us -> 5 us  [swap(): return lax.all_to_all(x, axes, split_axis=0, concat_axis=0, tiled=True)]
    all_to_all x6 -> x7, blocking collectives: 99.8 us -> 103 us  [swap(): return lax.all_to_all(x, axes, split_axis=0, concat_axis=0, tiled=True)]
    pallas_call x3 -> x4, Pallas kernels: 13.3 us -> 15.6 us  [call(): pl.pallas_call(kernel, out_shape=tuple(outs), in_specs=specs + [pl.BlockS...]
    unnamed x42 -> x18, local copies, waits for them, and re-layouts: 8.38 us -> 8.11 us
  transfers between devices with their start and end apart: 7 -> 6, of which waited for: 3 -> 2; matrix products, arithmetic and copies ran while one was open for 0% -> 1% of each run, Pallas kernels for 0% -> 0%
where the time goes in v4:
time: 170 us; the launch traced here: 169 us
  blocking collectives  103 us (61%)
  starting transfers between devices  23.7 us (14%)
  Pallas kernels  15.6 us (9%)
  waiting for transfers between devices  14.5 us (9%)
  local copies, waits for them, and re-layouts  11.3 us (7%)
    all_to_all x7, blocking collectives, swap(): return lax.all_to_all(x, axes, split_axis=0, concat_axis=0, tiled=True)  103 us
    pallas_call x4, Pallas kernels, call(): pl.pallas_call(kernel, out_shape=tuple(outs), in_specs=specs + [pl.BlockS...  15.6 us
    all_to_all x1, waiting for transfers between devices, swap(): return lax.all_to_all(x, axes, split_axis=0, concat_axis=0, tiled=True)  13 us
    unnamed x18, local copies, waits for them, and re-layouts  8.11 us
    ppermute x1, starting transfers between devices, images(): chigh = lax.ppermute(cfirst, ('dx', 'dy'), cdown)  5.47 us
    all_to_all x1, starting transfers between devices, swap(): return lax.all_to_all(x, axes, split_axis=0, concat_axis=0, tiled=True)  5 us
    ppermute x1, starting transfers between devices, images(): other = lax.ppermute(own, 'dy', [(0, 1), (1, 0)])  4.83 us
  transfers between devices with their start and end apart: 6, of which 2 were waited for; matrix products, arithmetic and copies ran while one was open for 1% of the time, Pallas kernels for 0%

profile of v4, /device:TPU:1, one launch (start us, length us, event | category | flops | bytes accessed | tf_op | source)
XLA Modules:
  0.0 169.3 jit_solution(15057162484576343559)
XLA Ops:
  0.6 0.0 copy-start.2
  0.6 0.9 copy-done.2
  1.6 0.8 copy-done.7
  2.4 0.4 shard_map.95
  2.8 4.8 %collective-permute-start = (bf16[7,128,128]{2,1,0:T(8,128)(2,1)S(1)}, bf16[7,128,128]{2,1,0:T(8,128)(2,1)S(1)}, u32[]{:S(2)}, u32[]{:S(2)}) collective-permute-start(bf16[7,128,128]{2,1,0:T(8,128)(2,1)S(1)} %get-tuple-element.12.p_ref), channel_id=1, source_target_pairs={{0,1},{1,0},{2,3},{3,2},{4,5},{5,4},{6,7},{7,6},{8,9},{9,8},{10,11... | collective-permute-start | bytes 688136 | tf_op jit(solution)/shard_map/ppermute | solution.py:170
  7.6 3.1 %collective-permute-start.1 = (bf16[7,96,128]{2,1,0:T(8,128)(2,1)S(1)}, bf16[7,96,128]{2,1,0:T(8,128)(2,1)S(1)}, u32[]{:S(2)}, u32[]{:S(2)}) collective-permute-start(bf16[7,96,128]{2,1,0:T(8,128)(2,1)S(1)} %get-tuple-element.14), channel_id=1, source_target_pairs={{0,2},{2,4},{4,6},{6,0},{1,3},{3,5},{5,7},{7,1},{8,10},{10,12},{12... | collective-permute-start | bytes 516104 | tf_op jit(solution)/shard_map/ppermute | solution.py:168
  10.8 3.4 %collective-permute-start.2 = (bf16[7,96,128]{2,1,0:T(8,128)(2,1)S(1)}, bf16[7,96,128]{2,1,0:T(8,128)(2,1)S(1)}, u32[]{:S(2)}, u32[]{:S(2)}) collective-permute-start(bf16[7,96,128]{2,1,0:T(8,128)(2,1)S(1)} %get-tuple-element.15), channel_id=1, source_target_pairs={{2,0},{4,2},{6,4},{0,6},{3,1},{5,3},{7,5},{1,7},{10,8},{12,10},{14... | collective-permute-start | bytes 516104 | tf_op jit(solution)/shard_map/ppermute | solution.py:169
  14.2 1.9 %collective-permute-start.3 = (bf16[6,48,128]{2,1,0:T(8,128)(2,1)S(1)}, bf16[6,48,128]{2,1,0:T(8,128)(2,1)S(1)}, u32[]{:S(2)}, u32[]{:S(2)}) collective-permute-start(bf16[6,48,128]{2,1,0:T(8,128)(2,1)S(1)} %get-tuple-element.16), channel_id=1, source_target_pairs={{0,3},{1,2},{2,5},{3,4},{4,7},{5,6},{6,1},{7,0},{8,11},{9,10},{10,... | collective-permute-start | bytes 221192 | tf_op jit(solution)/shard_map/ppermute | solution.py:173
  16.1 5.5 %collective-permute-start.4 = (bf16[6,48,128]{2,1,0:T(8,128)(2,1)S(1)}, bf16[6,48,128]{2,1,0:T(8,128)(2,1)S(1)}, u32[]{:S(2)}, u32[]{:S(2)}) collective-permute-start(bf16[6,48,128]{2,1,0:T(8,128)(2,1)S(1)} %get-tuple-element.17), channel_id=1, source_target_pairs={{2,1},{3,0},{4,3},{5,2},{6,5},{7,4},{0,7},{1,6},{10,9},{11,8},{12,... | collective-permute-start | bytes 221192 | tf_op jit(solution)/shard_map/ppermute | solution.py:174
  21.6 0.0 collective-permute-done.3.clo_ref
  21.6 1.5 collective-permute-done.4.chi_ref
  23.1 0.0 collective-permute-done.1.lo_ref
  23.1 0.0 collective-permute-done.2.hi_ref
  23.1 0.0 collective-permute-done.other_ref
  23.1 0.0 copy-start
  23.1 1.0 copy-done
  24.1 1.0 copy-done.1
  25.2 0.9 copy-done.3
  26.1 0.9 copy-done.4
  27.0 0.9 copy-done.5
  27.9 0.9 copy-done.6
  28.7 4.2 %shard_map.96 = (bf16[6,128,128]{2,1,0:T(8,128)(2,1)S(1)}, bf16[6,128,128]{2,1,0:T(8,128)(2,1)S(1)}) custom-call(bf16[7,128,128]{2,1,0:T(8,128)(2,1)S(1)} %get-tuple-element.12.p_ref, f32[128,128]{1,0:T(8,128)S(1)} %get-tuple-element.13.v_ref, bf16[7,128,128]{2,1,0:T(8,128)(2,1)S(1)} %collective-permute-done.other_ref, ...), custom_call_target="tpu_custom_call" | custom-call | tf_op jit(solution)/shard_map/pallas_call | solution.py:138
  33.1 0.1 pad_maximum_fusion
  33.2 0.4 copy.40
  33.6 38.9 %all_to_all.40 = bf16[64,36,128]{2,1,0:T(8,128)(2,1)S(1)} all-to-all(bf16[64,36,128]{2,1,0:T(8,128)(2,1)S(1)} %copy.40), channel_id=1, replica_groups=mesh['zhi'=4,'yh'=4,'yl'=2,'core'=2,'dx'=4,'dy'=2] {'zhi','yh','yl','core'}, dimensions={0} | all-to-all | bytes 1179648 | tf_op jit(solution)/shard_map/all_to_all | solution.py:201
  72.5 0.1 copy.41
  72.7 0.2 copy.43
  72.9 0.2 copy.44
  73.1 0.2 copy.42
  73.3 0.1 copy_bitcast_fusion
  73.4 0.7 shard_map.97
  74.1 5.1 %all_to_all.41 = bf16[2,1536,128]{2,1,0:T(8,128)(2,1)S(1)} all-to-all(bf16[2,1536,128]{2,1,0:T(8,128)(2,1)S(1)} %bitcast.30), channel_id=1, replica_groups=mesh['zhi'=4,'yh'=4,'yl'=2,'core'=2,'dx'=4,'dy'=2] {'core'}, dimensions={0} | all-to-all | bytes 1572864 | tf_op jit(solution)/shard_map/all_to_all | solution.py:201
  79.2 0.4 reduce_sum.42
  79.6 12.5 %all_to_all.42 = bf16[16,96,128]{2,1,0:T(8,128)(2,1)S(1)} all-to-all(bf16[16,96,128]{2,1,0:T(8,128)(2,1)S(1)} %bitcast.40), channel_id=1, replica_groups=mesh['zhi'=4,'yh'=4,'yl'=2,'core'=2,'dx'=4,'dy'=2] {'dx','dy','yl'}, dimensions={0} | all-to-all | bytes 786432 | tf_op jit(solution)/shard_map/all_to_all | solution.py:201
  92.1 0.1 reduce_sum.43
  92.1 11.4 %all_to_all.43 = bf16[4,96,128]{2,1,0:T(8,128)(2,1)S(1)} all-to-all(bf16[4,96,128]{2,1,0:T(8,128)(2,1)S(1)} %broadcast_in_dim.10), channel_id=1, replica_groups=mesh['zhi'=4,'yh'=4,'yl'=2,'core'=2,'dx'=4,'dy'=2] {'zhi'}, dimensions={0} | all-to-all | bytes 196608 | tf_op jit(solution)/shard_map/all_to_all | solution.py:201
  103.6 11.1 %all_to_all.44 = f32[4,96,128]{2,1,0:T(8,128)S(1)} all-to-all(f32[4,96,128]{2,1,0:T(8,128)S(1)} %broadcast_in_dim.11), channel_id=1, replica_groups=mesh['zhi'=4,'yh'=4,'yl'=2,'core'=2,'dx'=4,'dy'=2] {'yh'}, dimensions={0} | all-to-all | bytes 393216 | tf_op jit(solution)/shard_map/all_to_all | solution.py:201
  114.6 0.1 broadcast_in_dim.12
  114.7 13.1 %all_to_all.45 = f32[16,96,128]{2,1,0:T(8,128)S(1)} all-to-all(f32[16,96,128]{2,1,0:T(8,128)S(1)} %broadcast_in_dim.12), channel_id=1, replica_groups=mesh['zhi'=4,'yh'=4,'yl'=2,'core'=2,'dx'=4,'dy'=2] {'dx','dy','yl'}, dimensions={0} | all-to-all | bytes 1572864 | tf_op jit(solution)/shard_map/all_to_all | solution.py:201
  127.8 0.1 broadcast_in_dim.14
  127.9 10.7 %all_to_all.46 = f32[2,1536,128]{2,1,0:T(8,128)S(1)} all-to-all(f32[2,1536,128]{2,1,0:T(8,128)S(1)} %broadcast_in_dim.14), channel_id=1, replica_groups=mesh['zhi'=4,'yh'=4,'yl'=2,'core'=2,'dx'=4,'dy'=2] {'core'}, dimensions={0} | all-to-all | bytes 3145728 | tf_op jit(solution)/shard_map/all_to_all | solution.py:201
  138.6 10.2 %shard_map.98 = (bf16[384,256]{1,0:T(8,128)(2,1)S(1)}, f32[384,384]{1,0:T(8,128)S(1)}) custom-call(f32[3072,128]{1,0:T(8,128)S(1)} %bitcast.29, bf16[384,256]{1,0:T(8,128)(2,1)S(1)} %bitcast.32, bf16[384,256]{1,0:T(8,128)(2,1)S(1)} %get-tuple-element.36.i_ref, bf16[384,256]{1,0:T(8,128)(2,1)S(1)} %get-tuple-element.35.r_ref), custom_call_target="tpu_custom_call" | custom-call | tf_op jit(solution)/shard_map/pallas_call | solution.py:138
  148.9 0.8 reshape.56
  149.6 5.0 %all-to-all-start.7 = ((bf16[64,6,256]{2,1,0:T(8,128)(2,1)}), bf16[64,6,256]{2,1,0:T(8,128)(2,1)S(1)}, u32[]{:S(2)}, u32[]{:S(2)}) async-start(bf16[64,6,256]{2,1,0:T(8,128)(2,1)} %reshape.56), calls=%async_computation.7 | async-start | bytes 524288 | tf_op jit(solution)/shard_map/all_to_all | solution.py:201
  154.6 0.1 constant_dynamic-slice_fusion
  154.8 0.7 copy.46
  155.5 13.0 %all-to-all-done.7 = bf16[64,6,256]{2,1,0:T(8,128)(2,1)S(1)} async-done(((bf16[64,6,256]{2,1,0:T(8,128)(2,1)}), bf16[64,6,256]{2,1,0:T(8,128)(2,1)S(1)}, u32[]{:S(2)}, u32[]{:S(2)}) %all-to-all-start.7) | async-done | bytes 196640 | tf_op jit(solution)/shard_map/all_to_all | solution.py:201
  168.5 0.7 reshape.57
  (17 shorter events, 0.3 us)
Async XLA Ops:
  0.6 0.9 copy-start.2
  1.6 0.8 copy-start.7
  2.8 20.3 %collective-permute-start = (bf16[7,128,128]{2,1,0:T(8,128)(2,1)S(1)}, bf16[7,128,128]{2,1,0:T(8,128)(2,1)S(1)}, u32[]{:S(2)}, u32[]{:S(2)}) collective-permute-start(bf16[7,128,128]{2,1,0:T(8,128)(2,1)S(1)} %get-tuple-element.12.p_ref), channel_id=1, source_target_pairs={{0,1},{1,0},{2,3},{3,2},{4,5},{5,4},{6,7},{7,6},{8,9},{9,8},{10,11... | collective-permute-start | bytes 688136 | tf_op jit(solution)/shard_map/ppermute | solution.py:170
  7.6 15.5 %collective-permute-start.1 = (bf16[7,96,128]{2,1,0:T(8,128)(2,1)S(1)}, bf16[7,96,128]{2,1,0:T(8,128)(2,1)S(1)}, u32[]{:S(2)}, u32[]{:S(2)}) collective-permute-start(bf16[7,96,128]{2,1,0:T(8,128)(2,1)S(1)} %get-tuple-element.14), channel_id=1, source_target_pairs={{0,2},{2,4},{4,6},{6,0},{1,3},{3,5},{5,7},{7,1},{8,10},{10,12},{12... | collective-permute-start | bytes 516104 | tf_op jit(solution)/shard_map/ppermute | solution.py:168
  10.8 12.3 %collective-permute-start.2 = (bf16[7,96,128]{2,1,0:T(8,128)(2,1)S(1)}, bf16[7,96,128]{2,1,0:T(8,128)(2,1)S(1)}, u32[]{:S(2)}, u32[]{:S(2)}) collective-permute-start(bf16[7,96,128]{2,1,0:T(8,128)(2,1)S(1)} %get-tuple-element.15), channel_id=1, source_target_pairs={{2,0},{4,2},{6,4},{0,6},{3,1},{5,3},{7,5},{1,7},{10,8},{12,10},{14... | collective-permute-start | bytes 516104 | tf_op jit(solution)/shard_map/ppermute | solution.py:169
  14.2 7.5 %collective-permute-start.3 = (bf16[6,48,128]{2,1,0:T(8,128)(2,1)S(1)}, bf16[6,48,128]{2,1,0:T(8,128)(2,1)S(1)}, u32[]{:S(2)}, u32[]{:S(2)}) collective-permute-start(bf16[6,48,128]{2,1,0:T(8,128)(2,1)S(1)} %get-tuple-element.16), channel_id=1, source_target_pairs={{0,3},{1,2},{2,5},{3,4},{4,7},{5,6},{6,1},{7,0},{8,11},{9,10},{10,... | collective-permute-start | bytes 221192 | tf_op jit(solution)/shard_map/ppermute | solution.py:173
  16.1 7.0 %collective-permute-start.4 = (bf16[6,48,128]{2,1,0:T(8,128)(2,1)S(1)}, bf16[6,48,128]{2,1,0:T(8,128)(2,1)S(1)}, u32[]{:S(2)}, u32[]{:S(2)}) collective-permute-start(bf16[6,48,128]{2,1,0:T(8,128)(2,1)S(1)} %get-tuple-element.17), channel_id=1, source_target_pairs={{2,1},{3,0},{4,3},{5,2},{6,5},{7,4},{0,7},{1,6},{10,9},{11,8},{12,... | collective-permute-start | bytes 221192 | tf_op jit(solution)/shard_map/ppermute | solution.py:174
  23.1 1.0 copy-start
  24.1 1.0 copy-start.1
  25.1 0.9 copy-start.3
  26.1 0.9 copy-start.4
  27.0 0.9 copy-start.5
  27.9 0.9 copy-start.6
  149.6 18.9 %all-to-all-start.7 = ((bf16[64,6,256]{2,1,0:T(8,128)(2,1)}), bf16[64,6,256]{2,1,0:T(8,128)(2,1)S(1)}, u32[]{:S(2)}, u32[]{:S(2)}) async-start(bf16[64,6,256]{2,1,0:T(8,128)(2,1)} %reshape.56), calls=%async_computation.7 | async-start | bytes 524288 | tf_op jit(solution)/shard_map/all_to_all | solution.py:201

commit v5 on v4

--- a/solution.py
+++ b/solution.py
@@ -51,24 +51,14 @@
     for offset in range(1, 7):
         for shift in (offset, -offset):
             matrix[at, (at + shift) % length] += -0.5 * COEFFS[offset]
-    return np.kron(np.eye(2), matrix)
+    return matrix
 
 
 def slab(side, first, last, wy):
     return [(side, x, y) for x in range(first, last) for y in range(wy)]
 
 
-def pack_kernel(
-    p_hbm, v_hbm, own_ref, last_ref, first_ref, clast_ref, cfirst_ref, v_ref, p_ref, sems
-):
-    copies = [
-        pltpu.make_async_copy(p_hbm, p_ref, sems.at[0]),
-        pltpu.make_async_copy(v_hbm, v_ref, sems.at[1]),
-    ]
-    for copy in copies:
-        copy.start()
-    for copy in copies:
-        copy.wait()
+def pack_kernel(p_ref, v_ref, own_ref, last_ref, first_ref, clast_ref, cfirst_ref):
     nb, rows, _ = p_ref.shape
     wide, narrow = last_ref.shape[1], clast_ref.shape[1]
     v = v_ref[...].astype(BF)
@@ -84,13 +74,22 @@
 
 def stencil_kernel(
     p_ref, v_ref, other_ref, lo_ref, hi_ref, clo_ref, chi_ref,
-    a1h, a1l, a2h, a2l, zh, zl, i_ref, r_ref, field,
-    a1h_ref, a1l_ref, a2h_ref, a2l_ref, zh_ref, zl_ref, sems,
+    table_ref, i_ref, r_ref, field,
 ):
-    tables = ((a1h, a1h_ref), (a1l, a1l_ref), (zh, zh_ref), (zl, zl_ref), (a2h, a2h_ref), (a2l, a2l_ref))
-    copies = [pltpu.make_async_copy(a, b, sems.at[k]) for k, (a, b) in enumerate(tables)]
-    for copy in copies:
-        copy.start()
+    size = field.shape[0]
+    middle = p_ref.shape[1] + 2 * clo_ref.shape[1] + other_ref.shape[1]
+    last = 2 * middle + i_ref.shape[1]
+    end = last + i_ref.shape[1]
+    corner = table_ref.shape[1] - BLK
+    a1h, a1l = table_ref[:middle, :size], table_ref[middle : 2 * middle, :size]
+    a2h, a2l = table_ref[2 * middle : last, :middle], table_ref[last:end, :middle]
+    zh = table_ref[2 * middle : 2 * middle + BLK, corner:]
+    zl = table_ref[2 * middle + BLK : 2 * middle + 2 * BLK, corner:]
+
+    def along_z(x):
+        halves = (x[:, :BLK], x[:, BLK:])
+        return jnp.concatenate([dot(h, zh) + dot(h, zl) for h in halves], axis=1)
+
     nb, rows, _ = i_ref.shape
     wide, narrow = lo_ref.shape[1], clo_ref.shape[1]
 
@@ -99,8 +98,6 @@
 
     v = jnp.concatenate([v_ref[...], around(lo_ref[nb], hi_ref[nb], other_ref[nb])], axis=0)
     v = jnp.concatenate([v, v], axis=1)
-    for copy in copies:
-        copy.wait()
     for b in range(0, nb, 2):
         at = 0
         for ref in (p_ref, lo_ref, hi_ref, other_ref, clo_ref, chi_ref):
@@ -118,14 +115,12 @@
             ],
             axis=0,
         )
-        image = dot(a1h_ref[...], f) + dot(a1l_ref[...], f)
-        image = image + dot(centre, zh_ref[...]) + dot(centre, zl_ref[...])
+        image = dot(a1h, f) + dot(a1l, f) + along_z(centre)
         centre = centre.astype(F32)
         image = (image + v * centre).astype(BF)
         q = (centre - TAU * image.astype(F32)).astype(BF)
         own = q[:rows]
-        second = dot(a2h_ref[...], q) + dot(a2l_ref[...], q)
-        second = second + dot(own, zh_ref[...]) + dot(own, zl_ref[...])
+        second = dot(a2h, q) + dot(a2l, q) + along_z(own)
         second = (second + v[:rows] * own.astype(F32)).astype(BF)
         i_ref[b] = image[:rows, :BLK]
         i_ref[b + 1] = image[:rows, BLK:]
@@ -133,12 +128,11 @@
         r_ref[b + 1] = second[:, BLK:]
 
 
-def call(kernel, outs, args, scratch=(), limit=32, hbm=0):
-    specs = [pl.BlockSpec(memory_space=pltpu.VMEM)] * (len(args) - hbm)
+def call(kernel, outs, args, scratch=(), limit=32):
     return pl.pallas_call(
         kernel,
         out_shape=tuple(outs),
-        in_specs=specs + [pl.BlockSpec(memory_space=pl.ANY)] * hbm,
+        in_specs=[pl.BlockSpec(memory_space=pltpu.VMEM)] * len(args),
         out_specs=(pl.BlockSpec(memory_space=pltpu.VMEM),) * len(outs),
         scratch_shapes=list(scratch),
         compiler_params=pltpu.CompilerParams(vmem_limit_bytes=limit * 1024 * 1024),
@@ -154,13 +148,27 @@
     def shape(count, size):
         return jax.ShapeDtypeStruct((count, size, BLK), BF)
 
-    own, last, first, clast, cfirst, v = call(
+    whole = (
+        slab(0, 0, wx, wy) + slab(0, -12, 0, wy) + slab(0, wx, wx + 12, wy)
+        + slab(1, 0, wx, wy) + slab(1, -6, 0, wy) + slab(1, wx, wx + 6, wy)
+    )
+    middle = (
+        slab(0, 0, wx, wy) + slab(0, -6, 0, wy) + slab(0, wx, wx + 6, wy) + slab(1, 0, wx, wy)
+    )
+    big = parts(plane_matrix(middle, whole, wy))
+    small = parts(plane_matrix(slab(0, 0, wx, wy), middle, wy))
+    line = parts(line_matrix(BLK))
+    table = np.zeros((2 * len(middle) + 2 * max(rows, BLK), 5 * BLK), ml_dtypes.bfloat16)
+    for k in range(2):
+        table[k * len(middle) : (k + 1) * len(middle), : len(whole)] = big[k]
+        at = 2 * len(middle) + k * rows
+        table[at : at + rows, : len(middle)] = small[k]
+        at = 2 * len(middle) + k * BLK
+        table[at : at + BLK, -BLK:] = line[k]
+    own, last, first, clast, cfirst = call(
         pack_kernel,
-        [shape(nb + 1, rows)] + [shape(nb + 1, wide)] * 2 + [shape(nb, narrow)] * 2
-        + [jax.ShapeDtypeStruct((rows, BLK), F32)],
+        [shape(nb + 1, rows)] + [shape(nb + 1, wide)] * 2 + [shape(nb, narrow)] * 2,
         (p, v),
-        [pltpu.VMEM(p.shape, BF), pltpu.SemaphoreType.DMA((2,))],
-        hbm=2,
     )
     count = lax.axis_size("dx")
     up = [(k, (k + 1) % count) for k in range(count)]
@@ -173,28 +181,13 @@
     clow = lax.ppermute(clast, ("dx", "dy"), cup)
     chigh = lax.ppermute(cfirst, ("dx", "dy"), cdown)
 
-    whole = (
-        slab(0, 0, wx, wy) + slab(0, -12, 0, wy) + slab(0, wx, wx + 12, wy)
-        + slab(1, 0, wx, wy) + slab(1, -6, 0, wy) + slab(1, wx, wx + 6, wy)
-    )
-    middle = (
-        slab(0, 0, wx, wy) + slab(0, -6, 0, wy) + slab(0, wx, wx + 6, wy) + slab(1, 0, wx, wy)
-    )
-    tables = (
-        *parts(plane_matrix(middle, whole, wy)),
-        *parts(plane_matrix(slab(0, 0, wx, wy), middle, wy)),
-        *parts(line_matrix(BLK)),
-    )
     image, image_q = call(
         stencil_kernel,
         [shape(nb, rows)] * 2,
-        (own, v, other, low, high, clow, chigh) + tuple(jnp.asarray(t) for t in tables),
-        [pltpu.VMEM((len(whole), 2 * BLK), BF)]
-        + [pltpu.VMEM(t.shape, BF) for t in tables]
-        + [pltpu.SemaphoreType.DMA((len(tables),))],
-        hbm=len(tables),
-    )
-    return own[:nb], image, image_q
+        (p, v, other, low, high, clow, chigh, jnp.asarray(table)),
+        [pltpu.VMEM((len(whole), 2 * BLK), BF)],
+    )
+    return p, image, image_q
 
 
 def swap(x, axes):
@@ -319,20 +312,13 @@
     row, col = tri(n)
     diag = jnp.where(row == col, 1.5, 0.0).astype(F32)
 
-    def left(h, x):
-        high, low = split(x)
-        return dot(h, high) + dot(h, low)
-
-    def right(x, h):
-        high, low = split(x)
-        return dot(high, h) + dot(low, h)
-
     def full(a, x):
         high, low = split(x)
         return dot(a[0], high) + dot(a[0], low) + dot(a[1], high)
 
     def outer(high, middle, low, h):
-        b = TAU * right(middle + (0.5 * TAU) * left(h, low), h)
+        b = middle + (0.5 * TAU) * dot(h, low.astype(BF))
+        b = TAU * dot(b.astype(BF), h)
         return high + b + b.T
 
     h = g1.astype(BF)
@@ -342,10 +328,15 @@
     def both(x):
         return full(m1, full(m1, x).T)
 
+    def both_rounded(x):
+        x = x.astype(BF)
+        x = (dot(m1[0], x) + dot(m1[1], x)).T.astype(BF)
+        return dot(m1[0], x) + dot(m1[1], x)
+
     h2 = both(outer(hw2, hw, g1, h))
     h_ref[...] = h2
-    s1 = both(c1)
-    w2b = both(outer(w4, w3, w2, h))
+    s1 = both_rounded(c1)
+    w2b = both_rounded(outer(w4, w3, w2, h))
     hh = h2.astype(BF)
     m2 = split(diag - 0.5 * outer(w2b, s1 - TAU * h2, s1, hh))
 
@@ -356,7 +347,7 @@
     t = q - TAU * r_ref[...].astype(F32)
     psi1 = full(m1, q + hp)
     wpsi1 = full(m1, t + hq)
-    psi_ref[...] = full(m2, wpsi1 + TAU * left(hh, psi1)).astype(BF)
+    psi_ref[...] = full(m2, wpsi1 + TAU * dot(hh, psi1.astype(BF))).astype(BF)
 
 
 def algebra(rows, p, i, r, volume):

time: 170 us -> 162 us (0.953)
  Pallas kernels: 15.6 us -> 10.8 us
  local copies, waits for them, and re-layouts: 11.3 us -> 7.01 us
    pallas_call x4, Pallas kernels: 15.6 us -> 10.8 us  [call(): pl.pallas_call(kernel, out_shape=tuple(outs), in_specs=[pl.BlockSpec(memo...]
    unnamed x18 -> x8, local copies, waits for them, and re-layouts: 8.11 us -> 3.78 us
where the time goes in v5:
time: 162 us; the launch traced here: 161 us
  blocking collectives  103 us (64%)
  starting transfers between devices  23.7 us (15%)
  waiting for transfers between devices  14.5 us (9%)
  Pallas kernels  10.8 us (7%)
  local copies, waits for them, and re-layouts  7.01 us (4%)
    all_to_all x7, blocking collectives, swap(): return lax.all_to_all(x, axes, split_axis=0, concat_axis=0, tiled=True)  103 us
    all_to_all x1, waiting for transfers between devices, swap(): return lax.all_to_all(x, axes, split_axis=0, concat_axis=0, tiled=True)  13 us
    pallas_call x4, Pallas kernels, call(): pl.pallas_call(kernel, out_shape=tuple(outs), in_specs=[pl.BlockSpec(memo...  10.8 us
    ppermute x1, starting transfers between devices, images(): chigh = lax.ppermute(cfirst, ('dx', 'dy'), cdown)  5.47 us
    all_to_all x1, starting transfers between devices, swap(): return lax.all_to_all(x, axes, split_axis=0, concat_axis=0, tiled=True)  5 us
    ppermute x1, starting transfers between devices, images(): other = lax.ppermute(own, 'dy', [(0, 1), (1, 0)])  4.83 us
    unnamed x8, local copies, waits for them, and re-layouts  3.78 us
    ppermute x1, starting transfers between devices, images(): high = lax.ppermute(first, 'dx', down)  3.37 us
  transfers between devices with their start and end apart: 6, of which 2 were waited for; matrix products, arithmetic and copies ran while one was open for 1% of the time, Pallas kernels for 0%

profile of v5, /device:TPU:1, one launch (start us, length us, event | category | flops | bytes accessed | tf_op | source)
XLA Modules:
  0.0 161.1 jit_solution(14553569011668489146)
XLA Ops:
  0.6 0.0 copy-start
  0.6 0.9 copy-done
  1.6 0.0 copy-start.2
  1.6 0.8 copy-done.2
  2.4 0.1 shard_map.50
  2.5 4.8 %collective-permute-start = (bf16[7,128,128]{2,1,0:T(8,128)(2,1)S(1)}, bf16[7,128,128]{2,1,0:T(8,128)(2,1)S(1)}, u32[]{:S(2)}, u32[]{:S(2)}) collective-permute-start(bf16[7,128,128]{2,1,0:T(8,128)(2,1)S(1)} %get-tuple-element.11), channel_id=1, source_target_pairs={{0,1},{1,0},{2,3},{3,2},{4,5},{5,4},{6,7},{7,6},{8,9},{9,8},{10,11... | collective-permute-start | bytes 688136 | tf_op jit(solution)/shard_map/ppermute | solution.py:178
  7.3 3.1 %collective-permute-start.1 = (bf16[7,96,128]{2,1,0:T(8,128)(2,1)S(1)}, bf16[7,96,128]{2,1,0:T(8,128)(2,1)S(1)}, u32[]{:S(2)}, u32[]{:S(2)}) collective-permute-start(bf16[7,96,128]{2,1,0:T(8,128)(2,1)S(1)} %get-tuple-element.12), channel_id=1, source_target_pairs={{0,2},{2,4},{4,6},{6,0},{1,3},{3,5},{5,7},{7,1},{8,10},{10,12},{12... | collective-permute-start | bytes 516104 | tf_op jit(solution)/shard_map/ppermute | solution.py:176
  10.5 3.4 %collective-permute-start.2 = (bf16[7,96,128]{2,1,0:T(8,128)(2,1)S(1)}, bf16[7,96,128]{2,1,0:T(8,128)(2,1)S(1)}, u32[]{:S(2)}, u32[]{:S(2)}) collective-permute-start(bf16[7,96,128]{2,1,0:T(8,128)(2,1)S(1)} %get-tuple-element.13), channel_id=1, source_target_pairs={{2,0},{4,2},{6,4},{0,6},{3,1},{5,3},{7,5},{1,7},{10,8},{12,10},{14... | collective-permute-start | bytes 516104 | tf_op jit(solution)/shard_map/ppermute | solution.py:177
  13.8 1.9 %collective-permute-start.3 = (bf16[6,48,128]{2,1,0:T(8,128)(2,1)S(1)}, bf16[6,48,128]{2,1,0:T(8,128)(2,1)S(1)}, u32[]{:S(2)}, u32[]{:S(2)}) collective-permute-start(bf16[6,48,128]{2,1,0:T(8,128)(2,1)S(1)} %get-tuple-element.14), channel_id=1, source_target_pairs={{0,3},{1,2},{2,5},{3,4},{4,7},{5,6},{6,1},{7,0},{8,11},{9,10},{10,... | collective-permute-start | bytes 221192 | tf_op jit(solution)/shard_map/ppermute | solution.py:181
  15.8 5.5 %collective-permute-start.4 = (bf16[6,48,128]{2,1,0:T(8,128)(2,1)S(1)}, bf16[6,48,128]{2,1,0:T(8,128)(2,1)S(1)}, u32[]{:S(2)}, u32[]{:S(2)}) collective-permute-start(bf16[6,48,128]{2,1,0:T(8,128)(2,1)S(1)} %get-tuple-element.15), channel_id=1, source_target_pairs={{2,1},{3,0},{4,3},{5,2},{6,5},{7,4},{0,7},{1,6},{10,9},{11,8},{12,... | collective-permute-start | bytes 221192 | tf_op jit(solution)/shard_map/ppermute | solution.py:182
  21.2 0.0 collective-permute-done.3.clo_ref
  21.3 1.5 collective-permute-done.4.chi_ref
  22.8 0.0 collective-permute-done.1.lo_ref
  22.8 0.0 collective-permute-done.2.hi_ref
  22.8 0.0 collective-permute-done.other_ref
  22.8 0.0 copy-start.1
  22.8 1.3 copy-done.1
  24.1 2.5 %shard_map.51 = (bf16[6,128,128]{2,1,0:T(8,128)(2,1)S(1)}, bf16[6,128,128]{2,1,0:T(8,128)(2,1)S(1)}) custom-call(bf16[6,128,128]{2,1,0:T(8,128)(2,1)S(1)} %bitcast.32, f32[128,128]{1,0:T(8,128)S(1)} %bitcast.37, bf16[7,128,128]{2,1,0:T(8,128)(2,1)S(1)} %collective-permute-done.other_ref, bf16[7,96,128]{2,1,0:T(8,128)(2,1)S(1)} %collective-permute-done.1.lo_ref, ...), custom_call_target="tpu_custom_call" | custom-call | tf_op jit(solution)/shard_map/pallas_call | solution.py:132
  26.6 1.0 maximum_bitcast_fusion
  27.6 0.1 copy.27
  27.7 0.4 copy.28
  28.1 38.9 %all_to_all.40 = bf16[64,36,128]{2,1,0:T(8,128)(2,1)S(1)} all-to-all(bf16[64,36,128]{2,1,0:T(8,128)(2,1)S(1)} %copy.28), channel_id=1, replica_groups=mesh['zhi'=4,'yh'=4,'yl'=2,'core'=2,'dx'=4,'dy'=2] {'zhi','yh','yl','core'}, dimensions={0} | all-to-all | bytes 1179648 | tf_op jit(solution)/shard_map/all_to_all | solution.py:194
  67.0 0.1 copy.29
  67.2 0.2 copy.31
  67.4 0.2 copy.32
  67.6 0.2 copy.30
  67.9 0.1 copy_bitcast_fusion
  67.9 0.7 shard_map.52
  68.6 5.1 %all_to_all.41 = bf16[2,1536,128]{2,1,0:T(8,128)(2,1)S(1)} all-to-all(bf16[2,1536,128]{2,1,0:T(8,128)(2,1)S(1)} %bitcast.30), channel_id=1, replica_groups=mesh['zhi'=4,'yh'=4,'yl'=2,'core'=2,'dx'=4,'dy'=2] {'core'}, dimensions={0} | all-to-all | bytes 1572864 | tf_op jit(solution)/shard_map/all_to_all | solution.py:194
  73.7 0.4 reduce_sum.42
  74.1 12.5 %all_to_all.42 = bf16[16,96,128]{2,1,0:T(8,128)(2,1)S(1)} all-to-all(bf16[16,96,128]{2,1,0:T(8,128)(2,1)S(1)} %bitcast.43), channel_id=1, replica_groups=mesh['zhi'=4,'yh'=4,'yl'=2,'core'=2,'dx'=4,'dy'=2] {'dx','dy','yl'}, dimensions={0} | all-to-all | bytes 786432 | tf_op jit(solution)/shard_map/all_to_all | solution.py:194
  86.6 0.1 reduce_sum.43
  86.7 11.4 %all_to_all.43 = bf16[4,96,128]{2,1,0:T(8,128)(2,1)S(1)} all-to-all(bf16[4,96,128]{2,1,0:T(8,128)(2,1)S(1)} %broadcast_in_dim.10), channel_id=1, replica_groups=mesh['zhi'=4,'yh'=4,'yl'=2,'core'=2,'dx'=4,'dy'=2] {'zhi'}, dimensions={0} | all-to-all | bytes 196608 | tf_op jit(solution)/shard_map/all_to_all | solution.py:194
  98.1 11.1 %all_to_all.44 = f32[4,96,128]{2,1,0:T(8,128)S(1)} all-to-all(f32[4,96,128]{2,1,0:T(8,128)S(1)} %broadcast_in_dim.11), channel_id=1, replica_groups=mesh['zhi'=4,'yh'=4,'yl'=2,'core'=2,'dx'=4,'dy'=2] {'yh'}, dimensions={0} | all-to-all | bytes 393216 | tf_op jit(solution)/shard_map/all_to_all | solution.py:194
  109.2 0.1 broadcast_in_dim.12
  109.2 13.1 %all_to_all.45 = f32[16,96,128]{2,1,0:T(8,128)S(1)} all-to-all(f32[16,96,128]{2,1,0:T(8,128)S(1)} %broadcast_in_dim.12), channel_id=1, replica_groups=mesh['zhi'=4,'yh'=4,'yl'=2,'core'=2,'dx'=4,'dy'=2] {'dx','dy','yl'}, dimensions={0} | all-to-all | bytes 1572864 | tf_op jit(solution)/shard_map/all_to_all | solution.py:194
  122.4 0.1 broadcast_in_dim.14
  122.5 10.7 %all_to_all.46 = f32[2,1536,128]{2,1,0:T(8,128)S(1)} all-to-all(f32[2,1536,128]{2,1,0:T(8,128)S(1)} %broadcast_in_dim.14), channel_id=1, replica_groups=mesh['zhi'=4,'yh'=4,'yl'=2,'core'=2,'dx'=4,'dy'=2] {'core'}, dimensions={0} | all-to-all | bytes 3145728 | tf_op jit(solution)/shard_map/all_to_all | solution.py:194
  133.1 7.5 %shard_map.53 = (bf16[384,256]{1,0:T(8,128)(2,1)S(1)}, f32[384,384]{1,0:T(8,128)S(1)}) custom-call(f32[3072,128]{1,0:T(8,128)S(1)} %bitcast.29, bf16[384,256]{1,0:T(8,128)(2,1)S(1)} %bitcast.35, bf16[384,256]{1,0:T(8,128)(2,1)S(1)} %get-tuple-element.34.i_ref, bf16[384,256]{1,0:T(8,128)(2,1)S(1)} %get-tuple-element.33.r_ref), custom_call_target="tpu_custom_call" | custom-call | tf_op jit(solution)/shard_map/pallas_call | solution.py:132
  140.6 0.8 reshape.56
  141.4 5.0 %all-to-all-start.7 = ((bf16[64,6,256]{2,1,0:T(8,128)(2,1)}), bf16[64,6,256]{2,1,0:T(8,128)(2,1)S(1)}, u32[]{:S(2)}, u32[]{:S(2)}) async-start(bf16[64,6,256]{2,1,0:T(8,128)(2,1)} %reshape.56), calls=%async_computation.7 | async-start | bytes 524288 | tf_op jit(solution)/shard_map/all_to_all | solution.py:194
  146.4 0.1 constant_dynamic-slice_fusion
  146.6 0.7 copy.34
  147.3 13.0 %all-to-all-done.7 = bf16[64,6,256]{2,1,0:T(8,128)(2,1)S(1)} async-done(((bf16[64,6,256]{2,1,0:T(8,128)(2,1)}), bf16[64,6,256]{2,1,0:T(8,128)(2,1)S(1)}, u32[]{:S(2)}, u32[]{:S(2)}) %all-to-all-start.7) | async-done | bytes 196640 | tf_op jit(solution)/shard_map/all_to_all | solution.py:194
  160.3 0.7 reshape.57
  (7 shorter events, 0.2 us)
Async XLA Ops:
  0.6 0.9 copy-start
  1.6 0.8 copy-start.2
  2.5 20.3 %collective-permute-start = (bf16[7,128,128]{2,1,0:T(8,128)(2,1)S(1)}, bf16[7,128,128]{2,1,0:T(8,128)(2,1)S(1)}, u32[]{:S(2)}, u32[]{:S(2)}) collective-permute-start(bf16[7,128,128]{2,1,0:T(8,128)(2,1)S(1)} %get-tuple-element.11), channel_id=1, source_target_pairs={{0,1},{1,0},{2,3},{3,2},{4,5},{5,4},{6,7},{7,6},{8,9},{9,8},{10,11... | collective-permute-start | bytes 688136 | tf_op jit(solution)/shard_map/ppermute | solution.py:178
  7.3 15.5 %collective-permute-start.1 = (bf16[7,96,128]{2,1,0:T(8,128)(2,1)S(1)}, bf16[7,96,128]{2,1,0:T(8,128)(2,1)S(1)}, u32[]{:S(2)}, u32[]{:S(2)}) collective-permute-start(bf16[7,96,128]{2,1,0:T(8,128)(2,1)S(1)} %get-tuple-element.12), channel_id=1, source_target_pairs={{0,2},{2,4},{4,6},{6,0},{1,3},{3,5},{5,7},{7,1},{8,10},{10,12},{12... | collective-permute-start | bytes 516104 | tf_op jit(solution)/shard_map/ppermute | solution.py:176
  10.5 12.3 %collective-permute-start.2 = (bf16[7,96,128]{2,1,0:T(8,128)(2,1)S(1)}, bf16[7,96,128]{2,1,0:T(8,128)(2,1)S(1)}, u32[]{:S(2)}, u32[]{:S(2)}) collective-permute-start(bf16[7,96,128]{2,1,0:T(8,128)(2,1)S(1)} %get-tuple-element.13), channel_id=1, source_target_pairs={{2,0},{4,2},{6,4},{0,6},{3,1},{5,3},{7,5},{1,7},{10,8},{12,10},{14... | collective-permute-start | bytes 516104 | tf_op jit(solution)/shard_map/ppermute | solution.py:177
  13.8 7.4 %collective-permute-start.3 = (bf16[6,48,128]{2,1,0:T(8,128)(2,1)S(1)}, bf16[6,48,128]{2,1,0:T(8,128)(2,1)S(1)}, u32[]{:S(2)}, u32[]{:S(2)}) collective-permute-start(bf16[6,48,128]{2,1,0:T(8,128)(2,1)S(1)} %get-tuple-element.14), channel_id=1, source_target_pairs={{0,3},{1,2},{2,5},{3,4},{4,7},{5,6},{6,1},{7,0},{8,11},{9,10},{10,... | collective-permute-start | bytes 221192 | tf_op jit(solution)/shard_map/ppermute | solution.py:181
  15.8 7.0 %collective-permute-start.4 = (bf16[6,48,128]{2,1,0:T(8,128)(2,1)S(1)}, bf16[6,48,128]{2,1,0:T(8,128)(2,1)S(1)}, u32[]{:S(2)}, u32[]{:S(2)}) collective-permute-start(bf16[6,48,128]{2,1,0:T(8,128)(2,1)S(1)} %get-tuple-element.15), channel_id=1, source_target_pairs={{2,1},{3,0},{4,3},{5,2},{6,5},{7,4},{0,7},{1,6},{10,9},{11,8},{12,... | collective-permute-start | bytes 221192 | tf_op jit(solution)/shard_map/ppermute | solution.py:182
  22.8 1.3 copy-start.1
  141.4 18.9 %all-to-all-start.7 = ((bf16[64,6,256]{2,1,0:T(8,128)(2,1)}), bf16[64,6,256]{2,1,0:T(8,128)(2,1)S(1)}, u32[]{:S(2)}, u32[]{:S(2)}) async-start(bf16[64,6,256]{2,1,0:T(8,128)(2,1)} %reshape.56), calls=%async_computation.7 | async-start | bytes 524288 | tf_op jit(solution)/shard_map/all_to_all | solution.py:194

commit v6 on v5

--- a/solution.py
+++ b/solution.py
@@ -58,28 +58,28 @@
     return [(side, x, y) for x in range(first, last) for y in range(wy)]
 
 
-def pack_kernel(p_ref, v_ref, own_ref, last_ref, first_ref, clast_ref, cfirst_ref):
+def pack_kernel(p_ref, v_ref, own_ref):
+    nb = p_ref.shape[0]
+    own_ref[:nb] = p_ref[...]
+    own_ref[nb] = v_ref[...].astype(BF)
+
+
+def edge_kernel(wide, own_ref, other_ref, last_ref, first_ref):
+    rows = own_ref.shape[1]
+    narrow = last_ref.shape[1] - wide
+    last_ref[:, :wide] = own_ref[:, rows - wide :]
+    last_ref[:, wide:] = other_ref[:, rows - narrow :]
+    first_ref[:, :wide] = own_ref[:, :wide]
+    first_ref[:, wide:] = other_ref[:, :narrow]
+
+
+def stencil_kernel(wide, p_ref, v_ref, other_ref, lo_ref, hi_ref, table_ref, out_ref, field):
+    size = field.shape[0]
     nb, rows, _ = p_ref.shape
-    wide, narrow = last_ref.shape[1], clast_ref.shape[1]
-    v = v_ref[...].astype(BF)
-    own_ref[:nb] = p_ref[...]
-    own_ref[nb] = v
-    last_ref[:nb] = p_ref[:, rows - wide :]
-    last_ref[nb] = v[rows - wide :]
-    first_ref[:nb] = p_ref[:, :wide]
-    first_ref[nb] = v[:wide]
-    clast_ref[...] = p_ref[:, rows - narrow :]
-    cfirst_ref[...] = p_ref[:, :narrow]
-
-
-def stencil_kernel(
-    p_ref, v_ref, other_ref, lo_ref, hi_ref, clo_ref, chi_ref,
-    table_ref, i_ref, r_ref, field,
-):
-    size = field.shape[0]
-    middle = p_ref.shape[1] + 2 * clo_ref.shape[1] + other_ref.shape[1]
-    last = 2 * middle + i_ref.shape[1]
-    end = last + i_ref.shape[1]
+    narrow = lo_ref.shape[1] - wide
+    middle = 2 * rows + 2 * narrow
+    last = 2 * middle + rows
+    end = last + rows
     corner = table_ref.shape[1] - BLK
     a1h, a1l = table_ref[:middle, :size], table_ref[middle : 2 * middle, :size]
     a2h, a2l = table_ref[2 * middle : last, :middle], table_ref[last:end, :middle]
@@ -90,20 +90,21 @@
         halves = (x[:, :BLK], x[:, BLK:])
         return jnp.concatenate([dot(h, zh) + dot(h, zl) for h in halves], axis=1)
 
-    nb, rows, _ = i_ref.shape
-    wide, narrow = lo_ref.shape[1], clo_ref.shape[1]
-
     def around(low, high, other):
-        return jnp.concatenate([low[wide - narrow :], high[:narrow], other], axis=0).astype(F32)
+        return jnp.concatenate([low[wide - narrow : wide], high[:narrow], other], axis=0).astype(F32)
 
     v = jnp.concatenate([v_ref[...], around(lo_ref[nb], hi_ref[nb], other_ref[nb])], axis=0)
     v = jnp.concatenate([v, v], axis=1)
+    chunks = out_ref.shape[1]
+    parts_out = rows // chunks
     for b in range(0, nb, 2):
         at = 0
-        for ref in (p_ref, lo_ref, hi_ref, other_ref, clo_ref, chi_ref):
-            size = ref.shape[1]
-            field[at : at + size, :BLK] = ref[b]
-            field[at : at + size, BLK:] = ref[b + 1]
+        for ref, first, size in (
+            (p_ref, 0, rows), (lo_ref, 0, wide), (hi_ref, 0, wide),
+            (other_ref, 0, rows), (lo_ref, wide, narrow), (hi_ref, wide, narrow),
+        ):
+            field[at : at + size, :BLK] = ref[b, first : first + size]
+            field[at : at + size, BLK:] = ref[b + 1, first : first + size]
             at += size
         f = field[...]
         centre = jnp.concatenate(
@@ -122,10 +123,11 @@
         own = q[:rows]
         second = dot(a2h, q) + dot(a2l, q) + along_z(own)
         second = (second + v[:rows] * own.astype(F32)).astype(BF)
-        i_ref[b] = image[:rows, :BLK]
-        i_ref[b + 1] = image[:rows, BLK:]
-        r_ref[b] = second[:, :BLK]
-        r_ref[b + 1] = second[:, BLK:]
+        for k, x in enumerate((f[:rows], image[:rows], second)):
+            for h in range(parts_out):
+                for j in range(2):
+                    block = x[h * chunks : (h + 1) * chunks, j * BLK : (j + 1) * BLK]
+                    out_ref[(k * parts_out + h) * nb + b + j] = block
 
 
 def call(kernel, outs, args, scratch=(), limit=32):
@@ -139,7 +141,7 @@
     )(*args)
 
 
-def images(orbitals, potential):
+def images(orbitals, potential, chunks):
     nb, wx, wy, _ = orbitals.shape
     rows, wide, narrow = wx * wy, 12 * wy, 6 * wy
     p = orbitals.reshape(nb, rows, BLK)
@@ -165,29 +167,21 @@
         table[at : at + rows, : len(middle)] = small[k]
         at = 2 * len(middle) + k * BLK
         table[at : at + BLK, -BLK:] = line[k]
-    own, last, first, clast, cfirst = call(
-        pack_kernel,
-        [shape(nb + 1, rows)] + [shape(nb + 1, wide)] * 2 + [shape(nb, narrow)] * 2,
-        (p, v),
+    (own,) = call(pack_kernel, [shape(nb + 1, rows)], (p, v))
+    other = lax.ppermute(own, "dy", [(0, 1), (1, 0)])
+    last, first = call(
+        functools.partial(edge_kernel, wide), [shape(nb + 1, wide + narrow)] * 2, (own, other)
     )
     count = lax.axis_size("dx")
     up = [(k, (k + 1) % count) for k in range(count)]
-    down = [(b, a) for a, b in up]
     low = lax.ppermute(last, "dx", up)
-    high = lax.ppermute(first, "dx", down)
-    other = lax.ppermute(own, "dy", [(0, 1), (1, 0)])
-    cup = [(2 * a + k, 2 * b + 1 - k) for a, b in up for k in range(2)]
-    cdown = [(2 * a + k, 2 * b + 1 - k) for a, b in down for k in range(2)]
-    clow = lax.ppermute(clast, ("dx", "dy"), cup)
-    chigh = lax.ppermute(cfirst, ("dx", "dy"), cdown)
-
-    image, image_q = call(
-        stencil_kernel,
-        [shape(nb, rows)] * 2,
-        (p, v, other, low, high, clow, chigh, jnp.asarray(table)),
+    high = lax.ppermute(first, "dx", [(b, a) for a, b in up])
+    return call(
+        functools.partial(stencil_kernel, wide),
+        [shape(3 * nb * rows // chunks, chunks)],
+        (p, v, other, low, high, jnp.asarray(table)),
         [pltpu.VMEM((len(whole), 2 * BLK), BF)],
-    )
-    return p, image, image_q
+    )[0]
 
 
 def swap(x, axes):
@@ -206,8 +200,14 @@
     return lax.broadcasted_iota(jnp.int32, (n, n), 0), lax.broadcasted_iota(jnp.int32, (n, n), 1)
 
 
-def gram_kernel(p_ref, i_ref, r_ref, rows_ref):
-    p, i, r = p_ref[...], i_ref[...], r_ref[...]
+def panels(x_ref):
+    return [
+        jnp.concatenate([x_ref[k, h] for h in range(x_ref.shape[1])], axis=1) for k in range(3)
+    ]
+
+
+def gram_kernel(x_ref, rows_ref):
+    p, i, r = panels(x_ref)
     n = p.shape[0]
     nblk = n // BLK
     qf = p.astype(F32) - TAU * i.astype(F32)
@@ -270,8 +270,8 @@
     return high, (x - high.astype(F32)).astype(BF)
 
 
-def algebra_kernel(volume, rows_ref, p_ref, i_ref, r_ref, psi_ref, h_ref, mats):
-    n = p_ref.shape[0]
+def algebra_kernel(volume, rows_ref, x_ref, psi_ref, h_ref, mats):
+    n = x_ref.shape[2]
     nblk = n // BLK
     row, col = tri(BLK)
 
@@ -340,22 +340,28 @@
     hh = h2.astype(BF)
     m2 = split(diag - 0.5 * outer(w2b, s1 - TAU * h2, s1, hh))
 
-    p, i = p_ref[...], i_ref[...]
+    p, i, r = panels(x_ref)
     hp = TAU * dot(h, p)
     hq = hp - (TAU * TAU) * dot(h, i)
     q = p.astype(F32) - TAU * i.astype(F32)
-    t = q - TAU * r_ref[...].astype(F32)
+    t = q - TAU * r.astype(F32)
     psi1 = full(m1, q + hp)
     wpsi1 = full(m1, t + hq)
-    psi_ref[...] = full(m2, wpsi1 + TAU * dot(hh, psi1.astype(BF))).astype(BF)
-
-
-def algebra(rows, p, i, r, volume):
-    n, chunk = p.shape
+    psi2 = full(m2, wpsi1 + TAU * dot(hh, psi1.astype(BF))).astype(BF)
+    group = psi_ref.shape[1]
+    nh = x_ref.shape[1]
+    for b in range(n // group):
+        for h in range(nh):
+            psi_ref[b * nh + h] = psi2[b * group : (b + 1) * group, h * BLK : (h + 1) * BLK]
+
+
+def algebra(rows, x, volume, n_band):
+    n = x.shape[2]
+    count = n // n_band * x.shape[1]
     return call(
         functools.partial(algebra_kernel, volume),
-        [jax.ShapeDtypeStruct((n, chunk), BF), jax.ShapeDtypeStruct((n, n), F32)],
-        (rows, p, i, r),
+        [jax.ShapeDtypeStruct((count, n_band, BLK), BF), jax.ShapeDtypeStruct((n, n), F32)],
+        (rows, x),
         [pltpu.VMEM((NGRAM, n, n), F32)],
         48,
     )
@@ -370,21 +376,18 @@
     chunk = cells // n_band
     volume = 1.0 / (cells * lax.axis_size("dx") * lax.axis_size("dy"))
 
-    psi, image, image_q = images(orbitals, potential)
-
-    send = jnp.stack([psi, image, image_q]).reshape(3, nb, n_band, chunk // BLK, BLK)
-    send = send.transpose(2, 0, 1, 3, 4).reshape(n_band, -1, BLK)
-    got = swap(send, BAND).reshape(n_band, 3, nb, chunk // BLK, BLK)
-    p, i, r = got.transpose(1, 0, 2, 3, 4).reshape(3, bands, chunk)
+    send = images(orbitals, potential, n_band).transpose(1, 0, 2)
+    got = swap(send, BAND).transpose(1, 0, 2)
+    x = got.reshape(3, chunk // BLK, bands, BLK)
 
     count = bands // BLK * 2 * bands + len(pairs(bands // BLK)) * BLK
-    (rows,) = call(gram_kernel, [jax.ShapeDtypeStruct((count, BLK), BF)], (p, i, r))
-    psi2, h2 = algebra(reduced(rows), p, i, r, volume)
-
-    back = swap(psi2.reshape(n_band, nb, chunk), BAND)
-    new = back.transpose(1, 0, 2).reshape(shape)
-    columns = lax.dynamic_slice_in_dim(h2, lax.axis_index(BAND) * nb, nb, 1)
-    return new, columns
+    (rows,) = call(gram_kernel, [jax.ShapeDtypeStruct((count, BLK), BF)], (x,))
+    psi2, h2 = algebra(reduced(rows), x, volume, n_band)
+
+    back = swap(psi2.transpose(1, 0, 2), BAND).transpose(1, 0, 2)
+    mine = lax.dynamic_index_in_dim(h2.reshape(nb, n_band, bands), lax.axis_index(BAND), 1, False)
+    columns = mine.reshape(nb, nb, n_band).transpose(2, 1, 0).reshape(bands, nb)
+    return back.reshape(shape), columns
 
 
 def solution(mesh):

time: 162 us -> 160 us (0.988)
  waiting for transfers between devices: 14.5 us -> 20.1 us
  starting transfers between devices: 23.7 us -> 18.1 us
    ppermute x3 -> x1, starting transfers between devices: 10.8 us -> 3.19 us  [images(): high = lax.ppermute(first, 'dx', [(b, a) for a, b in up])]
    ppermute x1, waiting for transfers between devices: 0.01 us -> 3.4 us  [images(): other = lax.ppermute(own, 'dy', [(0, 1), (1, 0)])]
    ppermute x1, starting transfers between devices: 3.12 us -> 5.04 us  [images(): low = lax.ppermute(last, 'dx', up)]
    ppermute x1, waiting for transfers between devices: 0.01 us -> 1.77 us  [images(): low = lax.ppermute(last, 'dx', up)]
    unnamed x8 -> x7, local copies, waits for them, and re-layouts: 3.78 us -> 3.05 us
    pallas_call x4 -> x5, Pallas kernels: 10.8 us -> 10.8 us  [call(): pl.pallas_call(kernel, out_shape=tuple(outs), in_specs=[pl.BlockSpec(memo...]
  transfers between devices with their start and end apart: 6 -> 4, of which waited for: 2 -> 4; matrix products, arithmetic and copies ran while one was open for 1% -> 1% of each run, Pallas kernels for 0% -> 0%
where the time goes in v6:
time: 160 us
  blocking collectives  103 us (64%)
  waiting for transfers between devices  20.1 us (13%)
  starting transfers between devices  18.1 us (11%)
  Pallas kernels  10.8 us (7%)
  local copies, waits for them, and re-layouts  6.31 us (4%)
    all_to_all x7, blocking collectives, swap(): return lax.all_to_all(x, axes, split_axis=0, concat_axis=0, tiled=True)  103 us
    all_to_all x1, waiting for transfers between devices, swap(): return lax.all_to_all(x, axes, split_axis=0, concat_axis=0, tiled=True)  12.8 us
    pallas_call x5, Pallas kernels, call(): pl.pallas_call(kernel, out_shape=tuple(outs), in_specs=[pl.BlockSpec(memo...  10.8 us
    ppermute x1, starting transfers between devices, images(): low = lax.ppermute(last, 'dx', up)  5.04 us
    all_to_all x1, starting transfers between devices, swap(): return lax.all_to_all(x, axes, split_axis=0, concat_axis=0, tiled=True)  5 us
    ppermute x1, starting transfers between devices, images(): other = lax.ppermute(own, 'dy', [(0, 1), (1, 0)])  4.83 us
    ppermute x1, waiting for transfers between devices, images(): other = lax.ppermute(own, 'dy', [(0, 1), (1, 0)])  3.4 us
  transfers between devices with their start and end apart: 4, of which 4 were waited for; matrix products, arithmetic and copies ran while one was open for 1% of the time, Pallas kernels for 0%

profile of v6, /device:TPU:1, one launch (start us, length us, event | category | flops | bytes accessed | tf_op | source)
XLA Modules:
  0.0 159.5 jit_solution(4649287819872802257)
XLA Ops:
  0.6 0.0 copy-start.1
  0.6 0.9 copy-done.1
  1.6 0.0 copy-start.2
  1.6 0.8 copy-done.2
  2.4 4.8 %collective-permute-start = (bf16[7,128,128]{2,1,0:T(8,128)(2,1)S(1)}, bf16[7,128,128]{2,1,0:T(8,128)(2,1)S(1)}, u32[]{:S(2)}, u32[]{:S(2)}) collective-permute-start(bf16[7,128,128]{2,1,0:T(8,128)(2,1)S(1)} %shard_map.50.own_ref), channel_id=1, source_target_pairs={{0,1},{1,0},{2,3},{3,2},{4,5},{5,4},{6,7},{7,6},{8,9},{9,8},{10,11... | collective-permute-start | bytes 688136 | tf_op jit(solution)/shard_map/ppermute | solution.py:171
  7.3 3.4 %collective-permute-done.other_ref = bf16[7,128,128]{2,1,0:T(8,128)(2,1)S(1)} collective-permute-done((bf16[7,128,128]{2,1,0:T(8,128)(2,1)S(1)}, bf16[7,128,128]{2,1,0:T(8,128)(2,1)S(1)}, u32[]{:S(2)}, u32[]{:S(2)}) %collective-permute-start) | collective-permute-done | bytes 229408 | tf_op jit(solution)/shard_map/ppermute | solution.py:171
  10.7 5.0 %collective-permute-start.1 = (bf16[7,144,128]{2,1,0:T(8,128)(2,1)S(1)}, bf16[7,144,128]{2,1,0:T(8,128)(2,1)S(1)}, u32[]{:S(2)}, u32[]{:S(2)}) collective-permute-start(bf16[7,144,128]{2,1,0:T(8,128)(2,1)S(1)} %get-tuple-element.6), channel_id=1, source_target_pairs={{0,2},{2,4},{4,6},{6,0},{1,3},{3,5},{5,7},{7,1},{8,10},{10,12},{12... | collective-permute-start | bytes 774152 | tf_op jit(solution)/shard_map/ppermute | solution.py:177
  15.8 3.2 %collective-permute-start.2 = (bf16[7,144,128]{2,1,0:T(8,128)(2,1)S(1)}, bf16[7,144,128]{2,1,0:T(8,128)(2,1)S(1)}, u32[]{:S(2)}, u32[]{:S(2)}) collective-permute-start(bf16[7,144,128]{2,1,0:T(8,128)(2,1)S(1)} %get-tuple-element.7), channel_id=1, source_target_pairs={{2,0},{4,2},{6,4},{0,6},{3,1},{5,3},{7,5},{1,7},{10,8},{12,10},{14... | collective-permute-start | bytes 774152 | tf_op jit(solution)/shard_map/ppermute | solution.py:178
  18.9 1.8 %collective-permute-done.1.lo_ref = bf16[7,144,128]{2,1,0:T(8,128)(2,1)S(1)} collective-permute-done((bf16[7,144,128]{2,1,0:T(8,128)(2,1)S(1)}, bf16[7,144,128]{2,1,0:T(8,128)(2,1)S(1)}, u32[]{:S(2)}, u32[]{:S(2)}) %collective-permute-start.1) | collective-permute-done | bytes 258080 | tf_op jit(solution)/shard_map/ppermute | solution.py:177
  20.7 2.1 %collective-permute-done.2.hi_ref = bf16[7,144,128]{2,1,0:T(8,128)(2,1)S(1)} collective-permute-done((bf16[7,144,128]{2,1,0:T(8,128)(2,1)S(1)}, bf16[7,144,128]{2,1,0:T(8,128)(2,1)S(1)}, u32[]{:S(2)}, u32[]{:S(2)}) %collective-permute-start.2) | collective-permute-done | bytes 258080 | tf_op jit(solution)/shard_map/ppermute | solution.py:178
  22.8 0.0 copy-start
  22.8 1.3 copy-done
  24.1 2.5 %shard_map.52 = bf16[36,64,128]{2,1,0:T(8,128)(2,1)S(1)} custom-call(bf16[6,128,128]{2,1,0:T(8,128)(2,1)S(1)} %bitcast.25, f32[128,128]{1,0:T(8,128)S(1)} %bitcast.27, bf16[7,128,128]{2,1,0:T(8,128)(2,1)S(1)} %collective-permute-done.other_ref, bf16[7,144,128]{2,1,0:T(8,128)(2,1)S(1)} %collective-permute-done.1.lo_ref, ...), custom_call_target="tpu_custom_call" | custom-call | tf_op jit(solution)/shard_map/pallas_call | solution.py:134
  26.6 0.4 copy.18
  27.0 39.9 %all_to_all.40 = bf16[64,36,128]{2,1,0:T(8,128)(2,1)S(1)} all-to-all(bf16[64,36,128]{2,1,0:T(8,128)(2,1)S(1)} %copy.18), channel_id=1, replica_groups=mesh['zhi'=4,'yh'=4,'yl'=2,'core'=2,'dx'=4,'dy'=2] {'zhi','yh','yl','core'}, dimensions={0} | all-to-all | bytes 1179648 | tf_op jit(solution)/shard_map/all_to_all | solution.py:188
  66.9 0.1 copy.19
  67.1 0.7 shard_map.53
  67.8 5.1 %all_to_all.41 = bf16[2,1536,128]{2,1,0:T(8,128)(2,1)S(1)} all-to-all(bf16[2,1536,128]{2,1,0:T(8,128)(2,1)S(1)} %bitcast.22), channel_id=1, replica_groups=mesh['zhi'=4,'yh'=4,'yl'=2,'core'=2,'dx'=4,'dy'=2] {'core'}, dimensions={0} | all-to-all | bytes 1572864 | tf_op jit(solution)/shard_map/all_to_all | solution.py:188
  72.8 0.4 reduce_sum.42
  73.2 11.9 %all_to_all.42 = bf16[16,96,128]{2,1,0:T(8,128)(2,1)S(1)} all-to-all(bf16[16,96,128]{2,1,0:T(8,128)(2,1)S(1)} %bitcast.32), channel_id=1, replica_groups=mesh['zhi'=4,'yh'=4,'yl'=2,'core'=2,'dx'=4,'dy'=2] {'dx','dy','yl'}, dimensions={0} | all-to-all | bytes 786432 | tf_op jit(solution)/shard_map/all_to_all | solution.py:188
  85.0 0.1 reduce_sum.43
  85.1 11.4 %all_to_all.43 = bf16[4,96,128]{2,1,0:T(8,128)(2,1)S(1)} all-to-all(bf16[4,96,128]{2,1,0:T(8,128)(2,1)S(1)} %broadcast_in_dim.10), channel_id=1, replica_groups=mesh['zhi'=4,'yh'=4,'yl'=2,'core'=2,'dx'=4,'dy'=2] {'zhi'}, dimensions={0} | all-to-all | bytes 196608 | tf_op jit(solution)/shard_map/all_to_all | solution.py:188
  96.5 11.1 %all_to_all.44 = f32[4,96,128]{2,1,0:T(8,128)S(1)} all-to-all(f32[4,96,128]{2,1,0:T(8,128)S(1)} %broadcast_in_dim.11), channel_id=1, replica_groups=mesh['zhi'=4,'yh'=4,'yl'=2,'core'=2,'dx'=4,'dy'=2] {'yh'}, dimensions={0} | all-to-all | bytes 393216 | tf_op jit(solution)/shard_map/all_to_all | solution.py:188
  107.6 0.1 broadcast_in_dim.12
  107.7 13.1 %all_to_all.45 = f32[16,96,128]{2,1,0:T(8,128)S(1)} all-to-all(f32[16,96,128]{2,1,0:T(8,128)S(1)} %broadcast_in_dim.12), channel_id=1, replica_groups=mesh['zhi'=4,'yh'=4,'yl'=2,'core'=2,'dx'=4,'dy'=2] {'dx','dy','yl'}, dimensions={0} | all-to-all | bytes 1572864 | tf_op jit(solution)/shard_map/all_to_all | solution.py:188
  120.8 0.1 broadcast_in_dim.14
  120.9 10.7 %all_to_all.46 = f32[2,1536,128]{2,1,0:T(8,128)S(1)} all-to-all(f32[2,1536,128]{2,1,0:T(8,128)S(1)} %broadcast_in_dim.14), channel_id=1, replica_groups=mesh['zhi'=4,'yh'=4,'yl'=2,'core'=2,'dx'=4,'dy'=2] {'core'}, dimensions={0} | all-to-all | bytes 3145728 | tf_op jit(solution)/shard_map/all_to_all | solution.py:188
  131.6 7.5 %shard_map.54 = (bf16[12,64,128]{2,1,0:T(8,128)(2,1)S(1)}, f32[384,384]{1,0:T(8,128)S(1)}) custom-call(f32[3072,128]{1,0:T(8,128)S(1)} %bitcast.19, bf16[3,2,384,128]{3,2,1,0:T(8,128)(2,1)S(1)} %bitcast.21), custom_call_target="tpu_custom_call" | custom-call | tf_op jit(solution)/shard_map/pallas_call | solution.py:134
  139.1 0.8 copy.20
  139.9 5.0 %all-to-all-start.7 = ((bf16[64,12,128]{2,1,0:T(8,128)(2,1)}), bf16[64,12,128]{2,1,0:T(8,128)(2,1)S(1)}, u32[]{:S(2)}, u32[]{:S(2)}) async-start(bf16[64,12,128]{2,1,0:T(8,128)(2,1)} %copy.20), calls=%async_computation.7 | async-start | bytes 524288 | tf_op jit(solution)/shard_map/all_to_all | solution.py:188
  145.0 0.1 reshape.47
  145.1 0.1 copy.23
  145.2 0.8 reshape.48
  146.0 12.8 %all-to-all-done.7 = bf16[64,12,128]{2,1,0:T(8,128)(2,1)S(1)} async-done(((bf16[64,12,128]{2,1,0:T(8,128)(2,1)}), bf16[64,12,128]{2,1,0:T(8,128)(2,1)S(1)}, u32[]{:S(2)}, u32[]{:S(2)}) %all-to-all-start.7) | async-done | bytes 196640 | tf_op jit(solution)/shard_map/all_to_all | solution.py:188
  158.8 0.7 copy.21
  (8 shorter events, 0.1 us)
Async XLA Ops:
  0.6 0.9 copy-start.1
  1.6 0.8 copy-start.2
  2.4 8.2 %collective-permute-start = (bf16[7,128,128]{2,1,0:T(8,128)(2,1)S(1)}, bf16[7,128,128]{2,1,0:T(8,128)(2,1)S(1)}, u32[]{:S(2)}, u32[]{:S(2)}) collective-permute-start(bf16[7,128,128]{2,1,0:T(8,128)(2,1)S(1)} %shard_map.50.own_ref), channel_id=1, source_target_pairs={{0,1},{1,0},{2,3},{3,2},{4,5},{5,4},{6,7},{7,6},{8,9},{9,8},{10,11... | collective-permute-start | bytes 688136 | tf_op jit(solution)/shard_map/ppermute | solution.py:171
  10.7 10.0 %collective-permute-start.1 = (bf16[7,144,128]{2,1,0:T(8,128)(2,1)S(1)}, bf16[7,144,128]{2,1,0:T(8,128)(2,1)S(1)}, u32[]{:S(2)}, u32[]{:S(2)}) collective-permute-start(bf16[7,144,128]{2,1,0:T(8,128)(2,1)S(1)} %get-tuple-element.6), channel_id=1, source_target_pairs={{0,2},{2,4},{4,6},{6,0},{1,3},{3,5},{5,7},{7,1},{8,10},{10,12},{12... | collective-permute-start | bytes 774152 | tf_op jit(solution)/shard_map/ppermute | solution.py:177
  15.8 7.1 %collective-permute-start.2 = (bf16[7,144,128]{2,1,0:T(8,128)(2,1)S(1)}, bf16[7,144,128]{2,1,0:T(8,128)(2,1)S(1)}, u32[]{:S(2)}, u32[]{:S(2)}) collective-permute-start(bf16[7,144,128]{2,1,0:T(8,128)(2,1)S(1)} %get-tuple-element.7), channel_id=1, source_target_pairs={{2,0},{4,2},{6,4},{0,6},{3,1},{5,3},{7,5},{1,7},{10,8},{12,10},{14... | collective-permute-start | bytes 774152 | tf_op jit(solution)/shard_map/ppermute | solution.py:178
  22.8 1.3 copy-start
  139.9 18.9 %all-to-all-start.7 = ((bf16[64,12,128]{2,1,0:T(8,128)(2,1)}), bf16[64,12,128]{2,1,0:T(8,128)(2,1)S(1)}, u32[]{:S(2)}, u32[]{:S(2)}) async-start(bf16[64,12,128]{2,1,0:T(8,128)(2,1)} %copy.20), calls=%async_computation.7 | async-start | bytes 524288 | tf_op jit(solution)/shard_map/all_to_all | solution.py:188

commit v7 on v6

--- a/solution.py
+++ b/solution.py
@@ -58,22 +58,26 @@
     return [(side, x, y) for x in range(first, last) for y in range(wy)]
 
 
-def pack_kernel(p_ref, v_ref, own_ref):
-    nb = p_ref.shape[0]
-    own_ref[:nb] = p_ref[...]
-    own_ref[nb] = v_ref[...].astype(BF)
-
-
-def edge_kernel(wide, own_ref, other_ref, last_ref, first_ref):
-    rows = own_ref.shape[1]
+def hold_kernel(table_ref, held_ref):
+    held_ref[...] = table_ref[...]
+
+
+def edge_kernel(wide, p_ref, v_ref, other_ref, other_v_ref, last_ref, first_ref):
+    nb, rows, _ = p_ref.shape
     narrow = last_ref.shape[1] - wide
-    last_ref[:, :wide] = own_ref[:, rows - wide :]
-    last_ref[:, wide:] = other_ref[:, rows - narrow :]
-    first_ref[:, :wide] = own_ref[:, :wide]
-    first_ref[:, wide:] = other_ref[:, :narrow]
-
-
-def stencil_kernel(wide, p_ref, v_ref, other_ref, lo_ref, hi_ref, table_ref, out_ref, field):
+    last_ref[:nb, :wide] = p_ref[:, rows - wide :]
+    first_ref[:nb, :wide] = p_ref[:, :wide]
+    last_ref[:nb, wide:] = other_ref[:, rows - narrow :]
+    first_ref[:nb, wide:] = other_ref[:, :narrow]
+    last_ref[nb, :wide] = v_ref[rows - wide :]
+    first_ref[nb, :wide] = v_ref[:wide]
+    last_ref[nb, wide:] = other_v_ref[rows - narrow :]
+    first_ref[nb, wide:] = other_v_ref[:narrow]
+
+
+def stencil_kernel(
+    wide, p_ref, v_ref, other_ref, other_v_ref, lo_ref, hi_ref, table_ref, out_ref, field
+):
     size = field.shape[0]
     nb, rows, _ = p_ref.shape
     narrow = lo_ref.shape[1] - wide
@@ -93,7 +97,7 @@
     def around(low, high, other):
         return jnp.concatenate([low[wide - narrow : wide], high[:narrow], other], axis=0).astype(F32)
 
-    v = jnp.concatenate([v_ref[...], around(lo_ref[nb], hi_ref[nb], other_ref[nb])], axis=0)
+    v = jnp.concatenate([v_ref[...], around(lo_ref[nb], hi_ref[nb], other_v_ref[...])], axis=0)
     v = jnp.concatenate([v, v], axis=1)
     chunks = out_ref.shape[1]
     parts_out = rows // chunks
@@ -130,13 +134,14 @@
                     out_ref[(k * parts_out + h) * nb + b + j] = block
 
 
-def call(kernel, outs, args, scratch=(), limit=32):
+def call(kernel, outs, args, scratch=(), limit=32, cost=None):
     return pl.pallas_call(
         kernel,
         out_shape=tuple(outs),
         in_specs=[pl.BlockSpec(memory_space=pltpu.VMEM)] * len(args),
         out_specs=(pl.BlockSpec(memory_space=pltpu.VMEM),) * len(outs),
         scratch_shapes=list(scratch),
+        cost_estimate=cost and pl.CostEstimate(flops=0, transcendentals=0, bytes_accessed=cost),
         compiler_params=pltpu.CompilerParams(vmem_limit_bytes=limit * 1024 * 1024),
     )(*args)
 
@@ -167,10 +172,19 @@
         table[at : at + rows, : len(middle)] = small[k]
         at = 2 * len(middle) + k * BLK
         table[at : at + BLK, -BLK:] = line[k]
-    (own,) = call(pack_kernel, [shape(nb + 1, rows)], (p, v))
-    other = lax.ppermute(own, "dy", [(0, 1), (1, 0)])
+    rounded = v.astype(BF)
+    pair = [(0, 1), (1, 0)]
+    other, other_v = lax.ppermute(p, "dy", pair), lax.ppermute(rounded, "dy", pair)
+    (held,) = call(
+        hold_kernel,
+        [jax.ShapeDtypeStruct(table.shape, BF)],
+        (jnp.asarray(table),),
+        cost=4 * table.size,
+    )
     last, first = call(
-        functools.partial(edge_kernel, wide), [shape(nb + 1, wide + narrow)] * 2, (own, other)
+        functools.partial(edge_kernel, wide),
+        [shape(nb + 1, wide + narrow)] * 2,
+        (p, rounded, other, other_v),
     )
     count = lax.axis_size("dx")
     up = [(k, (k + 1) % count) for k in range(count)]
@@ -179,7 +193,7 @@
     return call(
         functools.partial(stencil_kernel, wide),
         [shape(3 * nb * rows // chunks, chunks)],
-        (p, v, other, low, high, jnp.asarray(table)),
+        (p, v, other, other_v, low, high, held),
         [pltpu.VMEM((len(whole), 2 * BLK), BF)],
     )[0]
 
@@ -248,7 +262,7 @@
     n_near = axes_size(NEAR)
     half = swap(rows.reshape(2, -1, BLK), "core").astype(F32).sum(0)
     part = swap(half.astype(BF).reshape(n_near, -1, BLK), NEAR).astype(F32).sum(0)
-    part = spread(part.astype(BF), "zhi", lax.axis_size("zhi")).astype(F32).sum(0)
+    part = spread(part, "zhi", lax.axis_size("zhi")).sum(0)
     part = spread(part, "yh", lax.axis_size("yh")).sum(0)
     half = spread(part, NEAR, n_near).reshape(-1, BLK)
     return spread(half, "core", 2).reshape(-1, BLK)

time: 160 us -> 160 us (level)
  waiting for transfers between devices: 20.1 us -> 18.1 us
    ppermute x1 -> x2, starting transfers between devices: 4.83 us -> 6.87 us  [the longest x1 4.96 us: images(): lax.ppermute(p, 'dy', pair)]
    ppermute x1 -> x2, waiting for transfers between devices: 3.4 us -> 2.73 us  [the longest x1 2.73 us: images(): lax.ppermute(rounded, 'dy', pair)]
  transfers between devices with their start and end apart: 4 -> 5, of which waited for: 4 -> 4; matrix products, arithmetic and copies ran while one was open for 1% -> 1% of each run, Pallas kernels for 0% -> 0%
where the time goes in v7:
time: 160 us; the launch traced here: 159 us
  blocking collectives  104 us (65%)
  starting transfers between devices  18.2 us (11%)
  waiting for transfers between devices  18.1 us (11%)
  Pallas kernels  10.9 us (7%)
  local copies, waits for them, and re-layouts  5.48 us (3%)
    all_to_all x7, blocking collectives, swap(): return lax.all_to_all(x, axes, split_axis=0, concat_axis=0, tiled=True)  104 us
    all_to_all x1, waiting for transfers between devices, swap(): return lax.all_to_all(x, axes, split_axis=0, concat_axis=0, tiled=True)  12.8 us
    pallas_call x5, Pallas kernels, call(): pl.pallas_call(kernel, out_shape=tuple(outs), in_specs=[pl.BlockSpec(memo...  10.9 us
    ppermute x1, starting transfers between devices, images(): lax.ppermute(p, 'dy', pair)  4.96 us
    all_to_all x1, starting transfers between devices, swap(): return lax.all_to_all(x, axes, split_axis=0, concat_axis=0, tiled=True)  4.61 us
    ppermute x1, starting transfers between devices, images(): low = lax.ppermute(last, 'dx', up)  3.57 us
  transfers between devices with their start and end apart: 5, of which 4 were waited for; matrix products, arithmetic and copies ran while one was open for 1% of the time, Pallas kernels for 0%

profile of v7, /device:TPU:1, one launch (start us, length us, event | category | flops | bytes accessed | tf_op | source)
XLA Modules:
  0.0 158.9 jit_solution(7873676228665377271)
XLA Ops:
  0.6 0.0 copy-start.3
  0.6 5.0 %collective-permute-start = (bf16[6,128,128]{2,1,0:T(8,128)(2,1)}, bf16[6,128,128]{2,1,0:T(8,128)(2,1)S(1)}, u32[]{:S(2)}, u32[]{:S(2)}) collective-permute-start(bf16[6,128,128]{2,1,0:T(8,128)(2,1)} %bitcast.25), channel_id=1, source_target_pairs={{0,1},{1,0},{2,3},{3,2},{4,5},{5,4},{6,7},{7,6},{8,9},{9,8},{10,11... | collective-permute-start | bytes 589832 | tf_op jit(solution)/shard_map/ppermute | solution.py:177
  5.6 0.8 bitcast_convert_fusion.v_ref
  6.5 1.9 %collective-permute-start.1 = (bf16[128,128]{1,0:T(8,128)(2,1)S(1)}, bf16[128,128]{1,0:T(8,128)(2,1)S(1)}, u32[]{:S(2)}, u32[]{:S(2)}) collective-permute-start(bf16[128,128]{1,0:T(8,128)(2,1)S(1)} %bitcast_convert_fusion.v_ref), channel_id=1, source_target_pairs={{0,1},{1,0},{2,3},{3,2},{4,5},{5,4},{6,7},{7,6},{8,9},{9,8},{10,11... | collective-permute-start | bytes 98312 | tf_op jit(solution)/shard_map/ppermute | solution.py:177
  8.4 2.7 %collective-permute-done.1.other_v_ref = bf16[128,128]{1,0:T(8,128)(2,1)S(1)} collective-permute-done((bf16[128,128]{1,0:T(8,128)(2,1)S(1)}, bf16[128,128]{1,0:T(8,128)(2,1)S(1)}, u32[]{:S(2)}, u32[]{:S(2)}) %collective-permute-start.1) | collective-permute-done | bytes 32800 | tf_op jit(solution)/shard_map/ppermute | solution.py:177
  11.1 0.0 collective-permute-done.other_ref
  11.1 0.0 copy-start.1
  11.1 0.9 copy-done.1
  12.0 0.0 copy-start.2
  12.1 3.6 %collective-permute-start.2 = (bf16[7,144,128]{2,1,0:T(8,128)(2,1)S(1)}, bf16[7,144,128]{2,1,0:T(8,128)(2,1)S(1)}, u32[]{:S(2)}, u32[]{:S(2)}) collective-permute-start(bf16[7,144,128]{2,1,0:T(8,128)(2,1)S(1)} %get-tuple-element.6), channel_id=1, source_target_pairs={{0,2},{2,4},{4,6},{6,0},{1,3},{3,5},{5,7},{7,1},{8,10},{10,12},{12... | collective-permute-start | bytes 774152 | tf_op jit(solution)/shard_map/ppermute | solution.py:191
  15.7 3.2 %collective-permute-start.3 = (bf16[7,144,128]{2,1,0:T(8,128)(2,1)S(1)}, bf16[7,144,128]{2,1,0:T(8,128)(2,1)S(1)}, u32[]{:S(2)}, u32[]{:S(2)}) collective-permute-start(bf16[7,144,128]{2,1,0:T(8,128)(2,1)S(1)} %get-tuple-element.7), channel_id=1, source_target_pairs={{2,0},{4,2},{6,4},{0,6},{3,1},{5,3},{7,5},{1,7},{10,8},{12,10},{14... | collective-permute-start | bytes 774152 | tf_op jit(solution)/shard_map/ppermute | solution.py:192
  18.9 0.0 copy-start
  18.9 1.3 copy-done
  20.2 0.1 shard_map.51.table_ref
  20.3 0.4 collective-permute-done.2.lo_ref
  20.6 2.1 %collective-permute-done.3.hi_ref = bf16[7,144,128]{2,1,0:T(8,128)(2,1)S(1)} collective-permute-done((bf16[7,144,128]{2,1,0:T(8,128)(2,1)S(1)}, bf16[7,144,128]{2,1,0:T(8,128)(2,1)S(1)}, u32[]{:S(2)}, u32[]{:S(2)}) %collective-permute-start.3) | collective-permute-done | bytes 258080 | tf_op jit(solution)/shard_map/ppermute | solution.py:192
  22.7 0.0 copy-done.3
  22.7 0.0 copy-done.2
  22.7 2.5 %shard_map.52 = bf16[36,64,128]{2,1,0:T(8,128)(2,1)S(1)} custom-call(bf16[6,128,128]{2,1,0:T(8,128)(2,1)S(1)} %bitcast.27, f32[128,128]{1,0:T(8,128)S(1)} %bitcast.28, bf16[6,128,128]{2,1,0:T(8,128)(2,1)S(1)} %collective-permute-done.other_ref, bf16[128,128]{1,0:T(8,128)(2,1)S(1)} %collective-permute-done.1.other_v_ref, ...), custom_call_target="tpu_custom_call" | custom-call | tf_op jit(solution)/shard_map/pallas_call | solution.py:138
  25.3 0.4 copy.18
  25.7 40.2 %all_to_all.40 = bf16[64,36,128]{2,1,0:T(8,128)(2,1)S(1)} all-to-all(bf16[64,36,128]{2,1,0:T(8,128)(2,1)S(1)} %copy.18), channel_id=1, replica_groups=mesh['zhi'=4,'yh'=4,'yl'=2,'core'=2,'dx'=4,'dy'=2] {'zhi','yh','yl','core'}, dimensions={0} | all-to-all | bytes 1179648 | tf_op jit(solution)/shard_map/all_to_all | solution.py:202
  65.9 0.1 copy.19
  66.0 0.7 shard_map.53
  66.8 5.2 %all_to_all.41 = bf16[2,1536,128]{2,1,0:T(8,128)(2,1)S(1)} all-to-all(bf16[2,1536,128]{2,1,0:T(8,128)(2,1)S(1)} %bitcast.23), channel_id=1, replica_groups=mesh['zhi'=4,'yh'=4,'yl'=2,'core'=2,'dx'=4,'dy'=2] {'core'}, dimensions={0} | all-to-all | bytes 1572864 | tf_op jit(solution)/shard_map/all_to_all | solution.py:202
  71.9 0.4 reduce_sum.39
  72.3 11.1 %all_to_all.42 = bf16[16,96,128]{2,1,0:T(8,128)(2,1)S(1)} all-to-all(bf16[16,96,128]{2,1,0:T(8,128)(2,1)S(1)} %bitcast.33), channel_id=1, replica_groups=mesh['zhi'=4,'yh'=4,'yl'=2,'core'=2,'dx'=4,'dy'=2] {'dx','dy','yl'}, dimensions={0} | all-to-all | bytes 786432 | tf_op jit(solution)/shard_map/all_to_all | solution.py:202
  83.4 0.1 convert_reduce_fusion
  83.5 12.4 %all_to_all.43 = f32[4,96,128]{2,1,0:T(8,128)S(1)} all-to-all(f32[4,96,128]{2,1,0:T(8,128)S(1)} %broadcast_in_dim.10), channel_id=1, replica_groups=mesh['zhi'=4,'yh'=4,'yl'=2,'core'=2,'dx'=4,'dy'=2] {'zhi'}, dimensions={0} | all-to-all | bytes 393216 | tf_op jit(solution)/shard_map/all_to_all | solution.py:202
  95.9 11.2 %all_to_all.44 = f32[4,96,128]{2,1,0:T(8,128)S(1)} all-to-all(f32[4,96,128]{2,1,0:T(8,128)S(1)} %broadcast_in_dim.11), channel_id=1, replica_groups=mesh['zhi'=4,'yh'=4,'yl'=2,'core'=2,'dx'=4,'dy'=2] {'yh'}, dimensions={0} | all-to-all | bytes 393216 | tf_op jit(solution)/shard_map/all_to_all | solution.py:202
  107.2 0.1 broadcast_in_dim.12
  107.2 12.8 %all_to_all.45 = f32[16,96,128]{2,1,0:T(8,128)S(1)} all-to-all(f32[16,96,128]{2,1,0:T(8,128)S(1)} %broadcast_in_dim.12), channel_id=1, replica_groups=mesh['zhi'=4,'yh'=4,'yl'=2,'core'=2,'dx'=4,'dy'=2] {'dx','dy','yl'}, dimensions={0} | all-to-all | bytes 1572864 | tf_op jit(solution)/shard_map/all_to_all | solution.py:202
  120.1 0.1 broadcast_in_dim.14
  120.2 11.2 %all_to_all.46 = f32[2,1536,128]{2,1,0:T(8,128)S(1)} all-to-all(f32[2,1536,128]{2,1,0:T(8,128)S(1)} %broadcast_in_dim.14), channel_id=1, replica_groups=mesh['zhi'=4,'yh'=4,'yl'=2,'core'=2,'dx'=4,'dy'=2] {'core'}, dimensions={0} | all-to-all | bytes 3145728 | tf_op jit(solution)/shard_map/all_to_all | solution.py:202
  131.4 7.5 %shard_map.54 = (bf16[12,64,128]{2,1,0:T(8,128)(2,1)S(1)}, f32[384,384]{1,0:T(8,128)S(1)}) custom-call(f32[3072,128]{1,0:T(8,128)S(1)} %bitcast.20, bf16[3,2,384,128]{3,2,1,0:T(8,128)(2,1)S(1)} %bitcast.22), custom_call_target="tpu_custom_call" | custom-call | tf_op jit(solution)/shard_map/pallas_call | solution.py:138
  138.8 0.8 copy.20
  139.7 4.6 %all-to-all-start.7 = ((bf16[64,12,128]{2,1,0:T(8,128)(2,1)}), bf16[64,12,128]{2,1,0:T(8,128)(2,1)S(1)}, u32[]{:S(2)}, u32[]{:S(2)}) async-start(bf16[64,12,128]{2,1,0:T(8,128)(2,1)} %copy.20), calls=%async_computation.7 | async-start | bytes 524288 | tf_op jit(solution)/shard_map/all_to_all | solution.py:202
  144.3 0.1 reshape.47
  144.4 0.1 copy.23
  144.6 0.8 reshape.48
  145.3 12.8 %all-to-all-done.7 = bf16[64,12,128]{2,1,0:T(8,128)(2,1)S(1)} async-done(((bf16[64,12,128]{2,1,0:T(8,128)(2,1)}), bf16[64,12,128]{2,1,0:T(8,128)(2,1)S(1)}, u32[]{:S(2)}, u32[]{:S(2)}) %all-to-all-start.7) | async-done | bytes 196640 | tf_op jit(solution)/shard_map/all_to_all | solution.py:202
  158.2 0.7 copy.21
  (7 shorter events, 0.1 us)
Async XLA Ops:
  0.6 22.1 %copy-start.3 = (f32[16,8,128]{2,1,0:T(8,128)S(1)}, f32[16,8,128]{2,1,0:T(8,128)}, u32[]{:S(2)}) copy-start(f32[16,8,128]{2,1,0:T(8,128)} %param.4) | copy-start | bytes 196612
  0.6 10.5 %collective-permute-start = (bf16[6,128,128]{2,1,0:T(8,128)(2,1)}, bf16[6,128,128]{2,1,0:T(8,128)(2,1)S(1)}, u32[]{:S(2)}, u32[]{:S(2)}) collective-permute-start(bf16[6,128,128]{2,1,0:T(8,128)(2,1)} %bitcast.25), channel_id=1, source_target_pairs={{0,1},{1,0},{2,3},{3,2},{4,5},{5,4},{6,7},{7,6},{8,9},{9,8},{10,11... | collective-permute-start | bytes 589832 | tf_op jit(solution)/shard_map/ppermute | solution.py:177
  6.5 4.6 %collective-permute-start.1 = (bf16[128,128]{1,0:T(8,128)(2,1)S(1)}, bf16[128,128]{1,0:T(8,128)(2,1)S(1)}, u32[]{:S(2)}, u32[]{:S(2)}) collective-permute-start(bf16[128,128]{1,0:T(8,128)(2,1)S(1)} %bitcast_convert_fusion.v_ref), channel_id=1, source_target_pairs={{0,1},{1,0},{2,3},{3,2},{4,5},{5,4},{6,7},{7,6},{8,9},{9,8},{10,11... | collective-permute-start | bytes 98312 | tf_op jit(solution)/shard_map/ppermute | solution.py:177
  11.1 0.9 copy-start.1
  12.0 10.7 %copy-start.2 = (bf16[6,16,8,128]{3,2,1,0:T(8,128)(2,1)S(1)}, bf16[6,16,8,128]{3,2,1,0:T(8,128)(2,1)}, u32[]{:S(2)}) copy-start(bf16[6,16,8,128]{3,2,1,0:T(8,128)(2,1)} %param.3) | copy-start | bytes 589828
  12.1 8.5 %collective-permute-start.2 = (bf16[7,144,128]{2,1,0:T(8,128)(2,1)S(1)}, bf16[7,144,128]{2,1,0:T(8,128)(2,1)S(1)}, u32[]{:S(2)}, u32[]{:S(2)}) collective-permute-start(bf16[7,144,128]{2,1,0:T(8,128)(2,1)S(1)} %get-tuple-element.6), channel_id=1, source_target_pairs={{0,2},{2,4},{4,6},{6,0},{1,3},{3,5},{5,7},{7,1},{8,10},{10,12},{12... | collective-permute-start | bytes 774152 | tf_op jit(solution)/shard_map/ppermute | solution.py:191
  15.7 7.1 %collective-permute-start.3 = (bf16[7,144,128]{2,1,0:T(8,128)(2,1)S(1)}, bf16[7,144,128]{2,1,0:T(8,128)(2,1)S(1)}, u32[]{:S(2)}, u32[]{:S(2)}) collective-permute-start(bf16[7,144,128]{2,1,0:T(8,128)(2,1)S(1)} %get-tuple-element.7), channel_id=1, source_target_pairs={{2,0},{4,2},{6,4},{0,6},{3,1},{5,3},{7,5},{1,7},{10,8},{12,10},{14... | collective-permute-start | bytes 774152 | tf_op jit(solution)/shard_map/ppermute | solution.py:192
  18.9 1.3 copy-start
  139.7 18.5 %all-to-all-start.7 = ((bf16[64,12,128]{2,1,0:T(8,128)(2,1)}), bf16[64,12,128]{2,1,0:T(8,128)(2,1)S(1)}, u32[]{:S(2)}, u32[]{:S(2)}) async-start(bf16[64,12,128]{2,1,0:T(8,128)(2,1)} %copy.20), calls=%async_computation.7 | async-start | bytes 524288 | tf_op jit(solution)/shard_map/all_to_all | solution.py:202

commit v8 on v7

--- a/solution.py
+++ b/solution.py
@@ -220,7 +220,13 @@
     ]
 
 
-def gram_kernel(x_ref, rows_ref):
+def core_halves(count):
+    half = count // 2
+    core = lax.axis_index("core")
+    return [pl.ds(pl.multiple_of(c * half, BLK), half) for c in (core, 1 - core)]
+
+
+def gram_kernel(x_ref, mine_ref, theirs_ref, rows_ref):
     p, i, r = panels(x_ref)
     n = p.shape[0]
     nblk = n // BLK
@@ -256,16 +262,20 @@
                 block = jnp.where((row == at_row) & (col < 64), line, block)
         rows_ref[at : at + BLK] = block.astype(BF)
         at += BLK
-
-
-def reduced(rows):
+    mine, theirs = core_halves(rows_ref.shape[0])
+    mine_ref[...] = rows_ref[mine]
+    theirs_ref[...] = rows_ref[theirs]
+
+
+def reduced(mine, theirs):
     n_near = axes_size(NEAR)
-    half = swap(rows.reshape(2, -1, BLK), "core").astype(F32).sum(0)
+    pair = [(0, 1), (1, 0)]
+    half = mine.astype(F32) + lax.ppermute(theirs, "core", pair).astype(F32)
     part = swap(half.astype(BF).reshape(n_near, -1, BLK), NEAR).astype(F32).sum(0)
     part = spread(part, "zhi", lax.axis_size("zhi")).sum(0)
     part = spread(part, "yh", lax.axis_size("yh")).sum(0)
     half = spread(part, NEAR, n_near).reshape(-1, BLK)
-    return spread(half, "core", 2).reshape(-1, BLK)
+    return half, lax.ppermute(half, "core", pair)
 
 
 def axes_size(axes):
@@ -284,9 +294,12 @@
     return high, (x - high.astype(F32)).astype(BF)
 
 
-def algebra_kernel(volume, rows_ref, x_ref, psi_ref, h_ref, mats):
+def algebra_kernel(volume, mine_ref, theirs_ref, x_ref, psi_ref, h_ref, mats, rows_ref):
     n = x_ref.shape[2]
     nblk = n // BLK
+    mine, theirs = core_halves(rows_ref.shape[0])
+    rows_ref[mine] = mine_ref[...]
+    rows_ref[theirs] = theirs_ref[...]
     row, col = tri(BLK)
 
     def put(g, r, c, tile):
@@ -369,14 +382,14 @@
             psi_ref[b * nh + h] = psi2[b * group : (b + 1) * group, h * BLK : (h + 1) * BLK]
 
 
-def algebra(rows, x, volume, n_band):
+def algebra(mine, theirs, x, volume, n_band):
     n = x.shape[2]
     count = n // n_band * x.shape[1]
     return call(
         functools.partial(algebra_kernel, volume),
         [jax.ShapeDtypeStruct((count, n_band, BLK), BF), jax.ShapeDtypeStruct((n, n), F32)],
-        (rows, x),
-        [pltpu.VMEM((NGRAM, n, n), F32)],
+        (mine, theirs, x),
+        [pltpu.VMEM((NGRAM, n, n), F32), pltpu.VMEM((2 * mine.shape[0], BLK), F32)],
         48,
     )
 
@@ -395,8 +408,13 @@
     x = got.reshape(3, chunk // BLK, bands, BLK)
 
     count = bands // BLK * 2 * bands + len(pairs(bands // BLK)) * BLK
-    (rows,) = call(gram_kernel, [jax.ShapeDtypeStruct((count, BLK), BF)], (x,))
-    psi2, h2 = algebra(reduced(rows), x, volume, n_band)
+    halves = call(
+        gram_kernel,
+        [jax.ShapeDtypeStruct((count // 2, BLK), BF)] * 2,
+        (x,),
+        [pltpu.VMEM((count, BLK), BF)],
+    )
+    psi2, h2 = algebra(*reduced(*halves), x, volume, n_band)
 
     back = swap(psi2.transpose(1, 0, 2), BAND).transpose(1, 0, 2)
     mine = lax.dynamic_index_in_dim(h2.reshape(nb, n_band, bands), lax.axis_index(BAND), 1, False)

time: 160 us -> 159 us (level)
  blocking collectives: 104 us -> 88.8 us
  starting transfers between devices: 18.2 us -> 29.8 us
  waiting for transfers between devices: 18.1 us -> 21.1 us
    all_to_all x7 -> x5, blocking collectives: 104 us -> 88.8 us  [swap(): return lax.all_to_all(x, axes, split_axis=0, concat_axis=0, tiled=True)]
    ppermute x0 -> x2, starting transfers between devices: none -> 10.6 us  [the longest x1 7.49 us: reduced(): return (half, lax.ppermute(half, 'core', pair))]
    ppermute x0 -> x2, waiting for transfers between devices: none -> 3.04 us  [the longest x1 1.71 us: reduced(): return (half, lax.ppermute(half, 'core', pair))]
  transfers between devices with their start and end apart: 5 -> 7, of which waited for: 4 -> 6; matrix products, arithmetic and copies ran while one was open for 1% -> 1% of each run, Pallas kernels for 0% -> 0%
where the time goes in v8:
time: 159 us; the launch traced here: 158 us
  blocking collectives  88.8 us (56%)
  starting transfers between devices  29.8 us (19%)
  waiting for transfers between devices  21.1 us (13%)
  Pallas kernels  11.3 us (7%)
  local copies, waits for them, and re-layouts  5.39 us (3%)
    all_to_all x5, blocking collectives, swap(): return lax.all_to_all(x, axes, split_axis=0, concat_axis=0, tiled=True)  88.8 us
    all_to_all x1, waiting for transfers between devices, swap(): return lax.all_to_all(x, axes, split_axis=0, concat_axis=0, tiled=True)  12.8 us
    pallas_call x5, Pallas kernels, call(): pl.pallas_call(kernel, out_shape=tuple(outs), in_specs=[pl.BlockSpec(memo...  11.3 us
    ppermute x1, starting transfers between devices, reduced(): return (half, lax.ppermute(half, 'core', pair))  7.49 us
    all_to_all x1, starting transfers between devices, swap(): return lax.all_to_all(x, axes, split_axis=0, concat_axis=0, tiled=True)  5.85 us
    ppermute x1, starting transfers between devices, images(): lax.ppermute(p, 'dy', pair)  4.83 us
    ppermute x1, starting transfers between devices, images(): low = lax.ppermute(last, 'dx', up)  3.43 us
    ppermute x1, starting transfers between devices, images(): high = lax.ppermute(first, 'dx', [(b, a) for a, b in up])  3.19 us
  transfers between devices with their start and end apart: 7, of which 6 were waited for; matrix products, arithmetic and copies ran while one was open for 1% of the time, Pallas kernels for 0%

profile of v8, /device:TPU:1, one launch (start us, length us, event | category | flops | bytes accessed | tf_op | source)
XLA Modules:
  0.0 158.2 jit_solution(14573884425900486355)
XLA Ops:
  0.6 4.8 %collective-permute-start = (bf16[6,128,128]{2,1,0:T(8,128)(2,1)}, bf16[6,128,128]{2,1,0:T(8,128)(2,1)S(1)}, u32[]{:S(2)}, u32[]{:S(2)}) collective-permute-start(bf16[6,128,128]{2,1,0:T(8,128)(2,1)} %bitcast.23), channel_id=1, source_target_pairs={{0,1},{1,0},{2,3},{3,2},{4,5},{5,4},{6,7},{7,6},{8,9},{9,8},{10,11... | collective-permute-start | bytes 589832 | tf_op jit(solution)/shard_map/ppermute | solution.py:177
  5.5 0.8 bitcast_convert_fusion.v_ref
  6.3 1.9 %collective-permute-start.1 = (bf16[128,128]{1,0:T(8,128)(2,1)S(1)}, bf16[128,128]{1,0:T(8,128)(2,1)S(1)}, u32[]{:S(2)}, u32[]{:S(2)}) collective-permute-start(bf16[128,128]{1,0:T(8,128)(2,1)S(1)} %bitcast_convert_fusion.v_ref), channel_id=1, source_target_pairs={{0,1},{1,0},{2,3},{3,2},{4,5},{5,4},{6,7},{7,6},{8,9},{9,8},{10,11... | collective-permute-start | bytes 98312 | tf_op jit(solution)/shard_map/ppermute | solution.py:177
  8.2 2.7 %collective-permute-done.1.other_v_ref = bf16[128,128]{1,0:T(8,128)(2,1)S(1)} collective-permute-done((bf16[128,128]{1,0:T(8,128)(2,1)S(1)}, bf16[128,128]{1,0:T(8,128)(2,1)S(1)}, u32[]{:S(2)}, u32[]{:S(2)}) %collective-permute-start.1) | collective-permute-done | bytes 32800 | tf_op jit(solution)/shard_map/ppermute | solution.py:177
  11.0 0.0 collective-permute-done.other_ref
  11.0 0.0 copy-start.1
  11.0 0.9 copy-done.1
  11.9 3.4 %collective-permute-start.2 = (bf16[7,144,128]{2,1,0:T(8,128)(2,1)S(1)}, bf16[7,144,128]{2,1,0:T(8,128)(2,1)S(1)}, u32[]{:S(2)}, u32[]{:S(2)}) collective-permute-start(bf16[7,144,128]{2,1,0:T(8,128)(2,1)S(1)} %get-tuple-element.8), channel_id=1, source_target_pairs={{0,2},{2,4},{4,6},{6,0},{1,3},{3,5},{5,7},{7,1},{8,10},{10,12},{12... | collective-permute-start | bytes 774152 | tf_op jit(solution)/shard_map/ppermute | solution.py:191
  15.4 3.2 %collective-permute-start.3 = (bf16[7,144,128]{2,1,0:T(8,128)(2,1)S(1)}, bf16[7,144,128]{2,1,0:T(8,128)(2,1)S(1)}, u32[]{:S(2)}, u32[]{:S(2)}) collective-permute-start(bf16[7,144,128]{2,1,0:T(8,128)(2,1)S(1)} %get-tuple-element.9), channel_id=1, source_target_pairs={{2,0},{4,2},{6,4},{0,6},{3,1},{5,3},{7,5},{1,7},{10,8},{12,10},{14... | collective-permute-start | bytes 774152 | tf_op jit(solution)/shard_map/ppermute | solution.py:192
  18.6 0.0 copy-start
  18.6 1.3 copy-done
  19.9 0.0 copy-start.2
  19.9 0.0 copy-start.3
  19.9 0.1 shard_map.51.table_ref
  20.0 0.4 collective-permute-done.2.lo_ref
  20.4 2.1 %collective-permute-done.3.hi_ref = bf16[7,144,128]{2,1,0:T(8,128)(2,1)S(1)} collective-permute-done((bf16[7,144,128]{2,1,0:T(8,128)(2,1)S(1)}, bf16[7,144,128]{2,1,0:T(8,128)(2,1)S(1)}, u32[]{:S(2)}, u32[]{:S(2)}) %collective-permute-start.3) | collective-permute-done | bytes 258080 | tf_op jit(solution)/shard_map/ppermute | solution.py:192
  22.5 0.0 copy-done.2
  22.5 0.0 copy-done.3
  22.5 2.5 %shard_map.52 = bf16[36,64,128]{2,1,0:T(8,128)(2,1)S(1)} custom-call(bf16[6,128,128]{2,1,0:T(8,128)(2,1)S(1)} %bitcast.25, f32[128,128]{1,0:T(8,128)S(1)} %bitcast.26, bf16[6,128,128]{2,1,0:T(8,128)(2,1)S(1)} %collective-permute-done.other_ref, bf16[128,128]{1,0:T(8,128)(2,1)S(1)} %collective-permute-done.1.other_v_ref, ...), custom_call_target="tpu_custom_call" | custom-call | tf_op jit(solution)/shard_map/pallas_call | solution.py:138
  25.0 0.4 copy.18
  25.4 40.2 %all_to_all.30 = bf16[64,36,128]{2,1,0:T(8,128)(2,1)S(1)} all-to-all(bf16[64,36,128]{2,1,0:T(8,128)(2,1)S(1)} %copy.18), channel_id=1, replica_groups=mesh['zhi'=4,'yh'=4,'yl'=2,'core'=2,'dx'=4,'dy'=2] {'zhi','yh','yl','core'}, dimensions={0} | all-to-all | bytes 1179648 | tf_op jit(solution)/shard_map/all_to_all | solution.py:202
  65.6 0.1 copy.19
  65.7 0.9 shard_map.53
  66.6 3.1 %collective-permute-start.4 = (bf16[1536,128]{1,0:T(8,128)(2,1)S(1)}, bf16[1536,128]{1,0:T(8,128)(2,1)S(1)}, u32[]{:S(2)}, u32[]{:S(2)}) collective-permute-start(bf16[1536,128]{1,0:T(8,128)(2,1)S(1)} %get-tuple-element.11), channel_id=1, source_target_pairs={{0,8},{8,0},{1,9},{9,1},{2,10},{10,2},{3,11},{11,3},{4,12},{12,4},... | collective-permute-start | bytes 1179656 | tf_op jit(solution)/shard_map/ppermute | solution.py:273
  69.7 1.3 collective-permute-done.4
  71.0 0.1 add_convert_fusion
  71.1 11.2 %all_to_all.31 = bf16[16,96,128]{2,1,0:T(8,128)(2,1)S(1)} all-to-all(bf16[16,96,128]{2,1,0:T(8,128)(2,1)S(1)} %bitcast.30), channel_id=1, replica_groups=mesh['zhi'=4,'yh'=4,'yl'=2,'core'=2,'dx'=4,'dy'=2] {'dx','dy','yl'}, dimensions={0} | all-to-all | bytes 786432 | tf_op jit(solution)/shard_map/all_to_all | solution.py:202
  82.3 0.1 convert_reduce_fusion
  82.4 12.5 %all_to_all.32 = f32[4,96,128]{2,1,0:T(8,128)S(1)} all-to-all(f32[4,96,128]{2,1,0:T(8,128)S(1)} %broadcast_in_dim.6), channel_id=1, replica_groups=mesh['zhi'=4,'yh'=4,'yl'=2,'core'=2,'dx'=4,'dy'=2] {'zhi'}, dimensions={0} | all-to-all | bytes 393216 | tf_op jit(solution)/shard_map/all_to_all | solution.py:202
  94.9 11.7 %all_to_all.33 = f32[4,96,128]{2,1,0:T(8,128)S(1)} all-to-all(f32[4,96,128]{2,1,0:T(8,128)S(1)} %broadcast_in_dim.7), channel_id=1, replica_groups=mesh['zhi'=4,'yh'=4,'yl'=2,'core'=2,'dx'=4,'dy'=2] {'yh'}, dimensions={0} | all-to-all | bytes 393216 | tf_op jit(solution)/shard_map/all_to_all | solution.py:202
  106.6 0.1 broadcast_in_dim.8
  106.7 13.3 %all_to_all.34 = f32[16,96,128]{2,1,0:T(8,128)S(1)} all-to-all(f32[16,96,128]{2,1,0:T(8,128)S(1)} %broadcast_in_dim.8), channel_id=1, replica_groups=mesh['zhi'=4,'yh'=4,'yl'=2,'core'=2,'dx'=4,'dy'=2] {'dx','dy','yl'}, dimensions={0} | all-to-all | bytes 1572864 | tf_op jit(solution)/shard_map/all_to_all | solution.py:202
  120.0 7.5 %collective-permute-start.5 = (f32[1536,128]{1,0:T(8,128)S(1)}, f32[1536,128]{1,0:T(8,128)S(1)}, u32[]{:S(2)}, u32[]{:S(2)}) collective-permute-start(f32[1536,128]{1,0:T(8,128)S(1)} %bitcast.20), channel_id=1, source_target_pairs={{0,8},{8,0},{1,9},{9,1},{2,10},{10,2},{3,11},{11,3},{4,12},{12,4},... | collective-permute-start | bytes 2359304 | tf_op jit(solution)/shard_map/ppermute | solution.py:278
  127.5 1.7 %collective-permute-done.5.theirs_ref = f32[1536,128]{1,0:T(8,128)S(1)} collective-permute-done((f32[1536,128]{1,0:T(8,128)S(1)}, f32[1536,128]{1,0:T(8,128)S(1)}, u32[]{:S(2)}, u32[]{:S(2)}) %collective-permute-start.5) | collective-permute-done | bytes 786464 | tf_op jit(solution)/shard_map/ppermute | solution.py:278
  129.2 7.7 %shard_map.54 = (bf16[12,64,128]{2,1,0:T(8,128)(2,1)S(1)}, f32[384,384]{1,0:T(8,128)S(1)}) custom-call(f32[1536,128]{1,0:T(8,128)S(1)} %bitcast.21, f32[1536,128]{1,0:T(8,128)S(1)} %collective-permute-done.5.theirs_ref, bf16[3,2,384,128]{3,2,1,0:T(8,128)(2,1)S(1)} %bitcast.19), custom_call_target="tpu_custom_call" | custom-call | tf_op jit(solution)/shard_map/pallas_call | solution.py:138
  136.9 0.8 copy.20
  137.7 5.9 %all-to-all-start.5 = ((bf16[64,12,128]{2,1,0:T(8,128)(2,1)}), bf16[64,12,128]{2,1,0:T(8,128)(2,1)S(1)}, u32[]{:S(2)}, u32[]{:S(2)}) async-start(bf16[64,12,128]{2,1,0:T(8,128)(2,1)} %copy.20), calls=%async_computation.5 | async-start | bytes 524288 | tf_op jit(solution)/shard_map/all_to_all | solution.py:202
  143.6 0.1 reshape.42
  143.7 0.1 copy.23
  143.9 0.8 reshape.43
  144.6 12.8 %all-to-all-done.5 = bf16[64,12,128]{2,1,0:T(8,128)(2,1)S(1)} async-done(((bf16[64,12,128]{2,1,0:T(8,128)(2,1)}), bf16[64,12,128]{2,1,0:T(8,128)(2,1)S(1)}, u32[]{:S(2)}, u32[]{:S(2)}) %all-to-all-start.5) | async-done | bytes 196640 | tf_op jit(solution)/shard_map/all_to_all | solution.py:202
  157.5 0.7 copy.21
  (7 shorter events, 0.1 us)
Async XLA Ops:
  0.6 10.3 %collective-permute-start = (bf16[6,128,128]{2,1,0:T(8,128)(2,1)}, bf16[6,128,128]{2,1,0:T(8,128)(2,1)S(1)}, u32[]{:S(2)}, u32[]{:S(2)}) collective-permute-start(bf16[6,128,128]{2,1,0:T(8,128)(2,1)} %bitcast.23), channel_id=1, source_target_pairs={{0,1},{1,0},{2,3},{3,2},{4,5},{5,4},{6,7},{7,6},{8,9},{9,8},{10,11... | collective-permute-start | bytes 589832 | tf_op jit(solution)/shard_map/ppermute | solution.py:177
  6.3 4.6 %collective-permute-start.1 = (bf16[128,128]{1,0:T(8,128)(2,1)S(1)}, bf16[128,128]{1,0:T(8,128)(2,1)S(1)}, u32[]{:S(2)}, u32[]{:S(2)}) collective-permute-start(bf16[128,128]{1,0:T(8,128)(2,1)S(1)} %bitcast_convert_fusion.v_ref), channel_id=1, source_target_pairs={{0,1},{1,0},{2,3},{3,2},{4,5},{5,4},{6,7},{7,6},{8,9},{9,8},{10,11... | collective-permute-start | bytes 98312 | tf_op jit(solution)/shard_map/ppermute | solution.py:177
  11.0 0.9 copy-start.1
  11.9 8.4 %collective-permute-start.2 = (bf16[7,144,128]{2,1,0:T(8,128)(2,1)S(1)}, bf16[7,144,128]{2,1,0:T(8,128)(2,1)S(1)}, u32[]{:S(2)}, u32[]{:S(2)}) collective-permute-start(bf16[7,144,128]{2,1,0:T(8,128)(2,1)S(1)} %get-tuple-element.8), channel_id=1, source_target_pairs={{0,2},{2,4},{4,6},{6,0},{1,3},{3,5},{5,7},{7,1},{8,10},{10,12},{12... | collective-permute-start | bytes 774152 | tf_op jit(solution)/shard_map/ppermute | solution.py:191
  15.4 7.1 %collective-permute-start.3 = (bf16[7,144,128]{2,1,0:T(8,128)(2,1)S(1)}, bf16[7,144,128]{2,1,0:T(8,128)(2,1)S(1)}, u32[]{:S(2)}, u32[]{:S(2)}) collective-permute-start(bf16[7,144,128]{2,1,0:T(8,128)(2,1)S(1)} %get-tuple-element.9), channel_id=1, source_target_pairs={{2,0},{4,2},{6,4},{0,6},{3,1},{5,3},{7,5},{1,7},{10,8},{12,10},{14... | collective-permute-start | bytes 774152 | tf_op jit(solution)/shard_map/ppermute | solution.py:192
  18.6 1.3 copy-start
  19.9 2.6 %copy-start.2 = (bf16[6,16,8,128]{3,2,1,0:T(8,128)(2,1)S(1)}, bf16[6,16,8,128]{3,2,1,0:T(8,128)(2,1)}, u32[]{:S(2)}) copy-start(bf16[6,16,8,128]{3,2,1,0:T(8,128)(2,1)} %param.3) | copy-start | bytes 589828
  19.9 2.6 %copy-start.3 = (f32[16,8,128]{2,1,0:T(8,128)S(1)}, f32[16,8,128]{2,1,0:T(8,128)}, u32[]{:S(2)}) copy-start(f32[16,8,128]{2,1,0:T(8,128)} %param.4) | copy-start | bytes 196612
  66.6 4.4 %collective-permute-start.4 = (bf16[1536,128]{1,0:T(8,128)(2,1)S(1)}, bf16[1536,128]{1,0:T(8,128)(2,1)S(1)}, u32[]{:S(2)}, u32[]{:S(2)}) collective-permute-start(bf16[1536,128]{1,0:T(8,128)(2,1)S(1)} %get-tuple-element.11), channel_id=1, source_target_pairs={{0,8},{8,0},{1,9},{9,1},{2,10},{10,2},{3,11},{11,3},{4,12},{12,4},... | collective-permute-start | bytes 1179656 | tf_op jit(solution)/shard_map/ppermute | solution.py:273
  120.0 9.2 %collective-permute-start.5 = (f32[1536,128]{1,0:T(8,128)S(1)}, f32[1536,128]{1,0:T(8,128)S(1)}, u32[]{:S(2)}, u32[]{:S(2)}) collective-permute-start(f32[1536,128]{1,0:T(8,128)S(1)} %bitcast.20), channel_id=1, source_target_pairs={{0,8},{8,0},{1,9},{9,1},{2,10},{10,2},{3,11},{11,3},{4,12},{12,4},... | collective-permute-start | bytes 2359304 | tf_op jit(solution)/shard_map/ppermute | solution.py:278
  137.7 19.7 %all-to-all-start.5 = ((bf16[64,12,128]{2,1,0:T(8,128)(2,1)}), bf16[64,12,128]{2,1,0:T(8,128)(2,1)S(1)}, u32[]{:S(2)}, u32[]{:S(2)}) async-start(bf16[64,12,128]{2,1,0:T(8,128)(2,1)} %copy.20), calls=%async_computation.5 | async-start | bytes 524288 | tf_op jit(solution)/shard_map/all_to_all | solution.py:202

commit v9 on v8

--- a/solution.py
+++ b/solution.py
@@ -175,6 +175,7 @@
     rounded = v.astype(BF)
     pair = [(0, 1), (1, 0)]
     other, other_v = lax.ppermute(p, "dy", pair), lax.ppermute(rounded, "dy", pair)
+    (psi,) = call(hold_kernel, [shape(nb, rows)], (p,), cost=4 * p.size)
     (held,) = call(
         hold_kernel,
         [jax.ShapeDtypeStruct(table.shape, BF)],
@@ -184,7 +185,7 @@
     last, first = call(
         functools.partial(edge_kernel, wide),
         [shape(nb + 1, wide + narrow)] * 2,
-        (p, rounded, other, other_v),
+        (psi, rounded, other, other_v),
     )
     count = lax.axis_size("dx")
     up = [(k, (k + 1) % count) for k in range(count)]
@@ -193,7 +194,7 @@
     return call(
         functools.partial(stencil_kernel, wide),
         [shape(3 * nb * rows // chunks, chunks)],
-        (p, v, other, other_v, low, high, held),
+        (psi, v, other, other_v, low, high, held),
         [pltpu.VMEM((len(whole), 2 * BLK), BF)],
     )[0]
 

time: 159 us -> 158 us (level)
    pallas_call x5 -> x6, Pallas kernels: 11.3 us -> 11.3 us  [call(): pl.pallas_call(kernel, out_shape=tuple(outs), in_specs=[pl.BlockSpec(memo...]
where the time goes in v9:
time: 158 us; the launch traced here: 157 us
  blocking collectives  88.8 us (56%)
  starting transfers between devices  29.8 us (19%)
  waiting for transfers between devices  20.2 us (13%)
  Pallas kernels  11.3 us (7%)
  local copies, waits for them, and re-layouts  5.38 us (3%)
    all_to_all x5, blocking collectives, swap(): return lax.all_to_all(x, axes, split_axis=0, concat_axis=0, tiled=True)  88.8 us
    all_to_all x1, waiting for transfers between devices, swap(): return lax.all_to_all(x, axes, split_axis=0, concat_axis=0, tiled=True)  12.8 us
    pallas_call x6, Pallas kernels, call(): pl.pallas_call(kernel, out_shape=tuple(outs), in_specs=[pl.BlockSpec(memo...  11.3 us
    ppermute x1, starting transfers between devices, reduced(): return (half, lax.ppermute(half, 'core', pair))  7.49 us
    all_to_all x1, starting transfers between devices, swap(): return lax.all_to_all(x, axes, split_axis=0, concat_axis=0, tiled=True)  5.85 us
    ppermute x1, starting transfers between devices, images(): lax.ppermute(p, 'dy', pair)  4.83 us
    ppermute x1, starting transfers between devices, images(): low = lax.ppermute(last, 'dx', up)  3.43 us
    ppermute x1, starting transfers between devices, images(): high = lax.ppermute(first, 'dx', [(b, a) for a, b in up])  3.19 us
  transfers between devices with their start and end apart: 7, of which 6 were waited for; matrix products, arithmetic and copies ran while one was open for 1% of the time, Pallas kernels for 0%

profile of v9, /device:TPU:1, one launch (start us, length us, event | category | flops | bytes accessed | tf_op | source)
XLA Modules:
  0.0 157.3 jit_solution(1415345405895528630)
XLA Ops:
  0.6 4.8 %collective-permute-start = (bf16[6,128,128]{2,1,0:T(8,128)(2,1)}, bf16[6,128,128]{2,1,0:T(8,128)(2,1)S(1)}, u32[]{:S(2)}, u32[]{:S(2)}) collective-permute-start(bf16[6,128,128]{2,1,0:T(8,128)(2,1)} %bitcast.25), channel_id=1, source_target_pairs={{0,1},{1,0},{2,3},{3,2},{4,5},{5,4},{6,7},{7,6},{8,9},{9,8},{10,11... | collective-permute-start | bytes 589832 | tf_op jit(solution)/shard_map/ppermute | solution.py:177
  5.5 0.8 bitcast_convert_fusion.v_ref
  6.3 1.9 %collective-permute-start.1 = (bf16[128,128]{1,0:T(8,128)(2,1)S(1)}, bf16[128,128]{1,0:T(8,128)(2,1)S(1)}, u32[]{:S(2)}, u32[]{:S(2)}) collective-permute-start(bf16[128,128]{1,0:T(8,128)(2,1)S(1)} %bitcast_convert_fusion.v_ref), channel_id=1, source_target_pairs={{0,1},{1,0},{2,3},{3,2},{4,5},{5,4},{6,7},{7,6},{8,9},{9,8},{10,11... | collective-permute-start | bytes 98312 | tf_op jit(solution)/shard_map/ppermute | solution.py:177
  8.2 0.0 copy-start.2
  8.2 0.9 copy-done.2
  9.2 1.8 %collective-permute-done.1.other_v_ref = bf16[128,128]{1,0:T(8,128)(2,1)S(1)} collective-permute-done((bf16[128,128]{1,0:T(8,128)(2,1)S(1)}, bf16[128,128]{1,0:T(8,128)(2,1)S(1)}, u32[]{:S(2)}, u32[]{:S(2)}) %collective-permute-start.1) | collective-permute-done | bytes 32800 | tf_op jit(solution)/shard_map/ppermute | solution.py:177
  11.0 0.0 collective-permute-done.other_ref
  11.0 3.4 %collective-permute-start.2 = (bf16[7,144,128]{2,1,0:T(8,128)(2,1)S(1)}, bf16[7,144,128]{2,1,0:T(8,128)(2,1)S(1)}, u32[]{:S(2)}, u32[]{:S(2)}) collective-permute-start(bf16[7,144,128]{2,1,0:T(8,128)(2,1)S(1)} %get-tuple-element.8), channel_id=1, source_target_pairs={{0,2},{2,4},{4,6},{6,0},{1,3},{3,5},{5,7},{7,1},{8,10},{10,12},{12... | collective-permute-start | bytes 774152 | tf_op jit(solution)/shard_map/ppermute | solution.py:192
  14.5 3.2 %collective-permute-start.3 = (bf16[7,144,128]{2,1,0:T(8,128)(2,1)S(1)}, bf16[7,144,128]{2,1,0:T(8,128)(2,1)S(1)}, u32[]{:S(2)}, u32[]{:S(2)}) collective-permute-start(bf16[7,144,128]{2,1,0:T(8,128)(2,1)S(1)} %get-tuple-element.9), channel_id=1, source_target_pairs={{2,0},{4,2},{6,4},{0,6},{3,1},{5,3},{7,5},{1,7},{10,8},{12,10},{14... | collective-permute-start | bytes 774152 | tf_op jit(solution)/shard_map/ppermute | solution.py:193
  17.7 0.0 copy-start
  17.7 1.3 copy-done
  18.9 0.0 copy-start.1
  18.9 0.1 shard_map.52.table_ref
  19.0 0.4 collective-permute-done.2.lo_ref
  19.4 2.1 %collective-permute-done.3.hi_ref = bf16[7,144,128]{2,1,0:T(8,128)(2,1)S(1)} collective-permute-done((bf16[7,144,128]{2,1,0:T(8,128)(2,1)S(1)}, bf16[7,144,128]{2,1,0:T(8,128)(2,1)S(1)}, u32[]{:S(2)}, u32[]{:S(2)}) %collective-permute-start.3) | collective-permute-done | bytes 258080 | tf_op jit(solution)/shard_map/ppermute | solution.py:193
  21.5 0.0 copy-done.1
  21.5 2.5 %shard_map.53 = bf16[36,64,128]{2,1,0:T(8,128)(2,1)S(1)} custom-call(bf16[6,128,128]{2,1,0:T(8,128)(2,1)S(1)} %shard_map.50.p_ref, f32[128,128]{1,0:T(8,128)S(1)} %bitcast.23, bf16[6,128,128]{2,1,0:T(8,128)(2,1)S(1)} %collective-permute-done.other_ref, bf16[128,128]{1,0:T(8,128)(2,1)S(1)} %collective-permute-done.1.other_v_ref, ...), custom_call_target="tpu_custom_call" | custom-call | tf_op jit(solution)/shard_map/pallas_call | solution.py:138
  24.1 0.4 copy.18
  24.5 40.2 %all_to_all.30 = bf16[64,36,128]{2,1,0:T(8,128)(2,1)S(1)} all-to-all(bf16[64,36,128]{2,1,0:T(8,128)(2,1)S(1)} %copy.18), channel_id=1, replica_groups=mesh['zhi'=4,'yh'=4,'yl'=2,'core'=2,'dx'=4,'dy'=2] {'zhi','yh','yl','core'}, dimensions={0} | all-to-all | bytes 1179648 | tf_op jit(solution)/shard_map/all_to_all | solution.py:203
  64.7 0.1 copy.19
  64.8 0.9 shard_map.54
  65.7 3.1 %collective-permute-start.4 = (bf16[1536,128]{1,0:T(8,128)(2,1)S(1)}, bf16[1536,128]{1,0:T(8,128)(2,1)S(1)}, u32[]{:S(2)}, u32[]{:S(2)}) collective-permute-start(bf16[1536,128]{1,0:T(8,128)(2,1)S(1)} %get-tuple-element.11), channel_id=1, source_target_pairs={{0,8},{8,0},{1,9},{9,1},{2,10},{10,2},{3,11},{11,3},{4,12},{12,4},... | collective-permute-start | bytes 1179656 | tf_op jit(solution)/shard_map/ppermute | solution.py:274
  68.8 1.3 collective-permute-done.4
  70.1 0.1 add_convert_fusion
  70.2 11.1 %all_to_all.31 = bf16[16,96,128]{2,1,0:T(8,128)(2,1)S(1)} all-to-all(bf16[16,96,128]{2,1,0:T(8,128)(2,1)S(1)} %bitcast.29), channel_id=1, replica_groups=mesh['zhi'=4,'yh'=4,'yl'=2,'core'=2,'dx'=4,'dy'=2] {'dx','dy','yl'}, dimensions={0} | all-to-all | bytes 786432 | tf_op jit(solution)/shard_map/all_to_all | solution.py:203
  81.3 0.1 convert_reduce_fusion
  81.4 12.5 %all_to_all.32 = f32[4,96,128]{2,1,0:T(8,128)S(1)} all-to-all(f32[4,96,128]{2,1,0:T(8,128)S(1)} %broadcast_in_dim.6), channel_id=1, replica_groups=mesh['zhi'=4,'yh'=4,'yl'=2,'core'=2,'dx'=4,'dy'=2] {'zhi'}, dimensions={0} | all-to-all | bytes 393216 | tf_op jit(solution)/shard_map/all_to_all | solution.py:203
  94.0 11.7 %all_to_all.33 = f32[4,96,128]{2,1,0:T(8,128)S(1)} all-to-all(f32[4,96,128]{2,1,0:T(8,128)S(1)} %broadcast_in_dim.7), channel_id=1, replica_groups=mesh['zhi'=4,'yh'=4,'yl'=2,'core'=2,'dx'=4,'dy'=2] {'yh'}, dimensions={0} | all-to-all | bytes 393216 | tf_op jit(solution)/shard_map/all_to_all | solution.py:203
  105.7 0.1 broadcast_in_dim.8
  105.8 13.3 %all_to_all.34 = f32[16,96,128]{2,1,0:T(8,128)S(1)} all-to-all(f32[16,96,128]{2,1,0:T(8,128)S(1)} %broadcast_in_dim.8), channel_id=1, replica_groups=mesh['zhi'=4,'yh'=4,'yl'=2,'core'=2,'dx'=4,'dy'=2] {'dx','dy','yl'}, dimensions={0} | all-to-all | bytes 1572864 | tf_op jit(solution)/shard_map/all_to_all | solution.py:203
  119.0 7.5 %collective-permute-start.5 = (f32[1536,128]{1,0:T(8,128)S(1)}, f32[1536,128]{1,0:T(8,128)S(1)}, u32[]{:S(2)}, u32[]{:S(2)}) collective-permute-start(f32[1536,128]{1,0:T(8,128)S(1)} %bitcast.20), channel_id=1, source_target_pairs={{0,8},{8,0},{1,9},{9,1},{2,10},{10,2},{3,11},{11,3},{4,12},{12,4},... | collective-permute-start | bytes 2359304 | tf_op jit(solution)/shard_map/ppermute | solution.py:279
  126.5 1.7 %collective-permute-done.5.theirs_ref = f32[1536,128]{1,0:T(8,128)S(1)} collective-permute-done((f32[1536,128]{1,0:T(8,128)S(1)}, f32[1536,128]{1,0:T(8,128)S(1)}, u32[]{:S(2)}, u32[]{:S(2)}) %collective-permute-start.5) | collective-permute-done | bytes 786464 | tf_op jit(solution)/shard_map/ppermute | solution.py:279
  128.2 7.7 %shard_map.55 = (bf16[12,64,128]{2,1,0:T(8,128)(2,1)S(1)}, f32[384,384]{1,0:T(8,128)S(1)}) custom-call(f32[1536,128]{1,0:T(8,128)S(1)} %bitcast.21, f32[1536,128]{1,0:T(8,128)S(1)} %collective-permute-done.5.theirs_ref, bf16[3,2,384,128]{3,2,1,0:T(8,128)(2,1)S(1)} %bitcast.19), custom_call_target="tpu_custom_call" | custom-call | tf_op jit(solution)/shard_map/pallas_call | solution.py:138
  136.0 0.8 copy.20
  136.8 5.9 %all-to-all-start.5 = ((bf16[64,12,128]{2,1,0:T(8,128)(2,1)}), bf16[64,12,128]{2,1,0:T(8,128)(2,1)S(1)}, u32[]{:S(2)}, u32[]{:S(2)}) async-start(bf16[64,12,128]{2,1,0:T(8,128)(2,1)} %copy.20), calls=%async_computation.5 | async-start | bytes 524288 | tf_op jit(solution)/shard_map/all_to_all | solution.py:203
  142.7 0.1 reshape.42
  142.8 0.1 copy.23
  142.9 0.8 reshape.43
  143.7 12.8 %all-to-all-done.5 = bf16[64,12,128]{2,1,0:T(8,128)(2,1)S(1)} async-done(((bf16[64,12,128]{2,1,0:T(8,128)(2,1)}), bf16[64,12,128]{2,1,0:T(8,128)(2,1)S(1)}, u32[]{:S(2)}, u32[]{:S(2)}) %all-to-all-start.5) | async-done | bytes 196640 | tf_op jit(solution)/shard_map/all_to_all | solution.py:203
  156.5 0.7 copy.21
  (8 shorter events, 0.1 us)
Async XLA Ops:
  0.6 10.3 %collective-permute-start = (bf16[6,128,128]{2,1,0:T(8,128)(2,1)}, bf16[6,128,128]{2,1,0:T(8,128)(2,1)S(1)}, u32[]{:S(2)}, u32[]{:S(2)}) collective-permute-start(bf16[6,128,128]{2,1,0:T(8,128)(2,1)} %bitcast.25), channel_id=1, source_target_pairs={{0,1},{1,0},{2,3},{3,2},{4,5},{5,4},{6,7},{7,6},{8,9},{9,8},{10,11... | collective-permute-start | bytes 589832 | tf_op jit(solution)/shard_map/ppermute | solution.py:177
  6.3 4.6 %collective-permute-start.1 = (bf16[128,128]{1,0:T(8,128)(2,1)S(1)}, bf16[128,128]{1,0:T(8,128)(2,1)S(1)}, u32[]{:S(2)}, u32[]{:S(2)}) collective-permute-start(bf16[128,128]{1,0:T(8,128)(2,1)S(1)} %bitcast_convert_fusion.v_ref), channel_id=1, source_target_pairs={{0,1},{1,0},{2,3},{3,2},{4,5},{5,4},{6,7},{7,6},{8,9},{9,8},{10,11... | collective-permute-start | bytes 98312 | tf_op jit(solution)/shard_map/ppermute | solution.py:177
  8.2 0.9 copy-start.2
  11.0 8.4 %collective-permute-start.2 = (bf16[7,144,128]{2,1,0:T(8,128)(2,1)S(1)}, bf16[7,144,128]{2,1,0:T(8,128)(2,1)S(1)}, u32[]{:S(2)}, u32[]{:S(2)}) collective-permute-start(bf16[7,144,128]{2,1,0:T(8,128)(2,1)S(1)} %get-tuple-element.8), channel_id=1, source_target_pairs={{0,2},{2,4},{4,6},{6,0},{1,3},{3,5},{5,7},{7,1},{8,10},{10,12},{12... | collective-permute-start | bytes 774152 | tf_op jit(solution)/shard_map/ppermute | solution.py:192
  14.5 7.1 %collective-permute-start.3 = (bf16[7,144,128]{2,1,0:T(8,128)(2,1)S(1)}, bf16[7,144,128]{2,1,0:T(8,128)(2,1)S(1)}, u32[]{:S(2)}, u32[]{:S(2)}) collective-permute-start(bf16[7,144,128]{2,1,0:T(8,128)(2,1)S(1)} %get-tuple-element.9), channel_id=1, source_target_pairs={{2,0},{4,2},{6,4},{0,6},{3,1},{5,3},{7,5},{1,7},{10,8},{12,10},{14... | collective-permute-start | bytes 774152 | tf_op jit(solution)/shard_map/ppermute | solution.py:193
  17.7 1.3 copy-start
  18.9 2.6 %copy-start.1 = (f32[16,8,128]{2,1,0:T(8,128)S(1)}, f32[16,8,128]{2,1,0:T(8,128)}, u32[]{:S(2)}) copy-start(f32[16,8,128]{2,1,0:T(8,128)} %param.4) | copy-start | bytes 196612
  65.7 4.4 %collective-permute-start.4 = (bf16[1536,128]{1,0:T(8,128)(2,1)S(1)}, bf16[1536,128]{1,0:T(8,128)(2,1)S(1)}, u32[]{:S(2)}, u32[]{:S(2)}) collective-permute-start(bf16[1536,128]{1,0:T(8,128)(2,1)S(1)} %get-tuple-element.11), channel_id=1, source_target_pairs={{0,8},{8,0},{1,9},{9,1},{2,10},{10,2},{3,11},{11,3},{4,12},{12,4},... | collective-permute-start | bytes 1179656 | tf_op jit(solution)/shard_map/ppermute | solution.py:274
  119.0 9.2 %collective-permute-start.5 = (f32[1536,128]{1,0:T(8,128)S(1)}, f32[1536,128]{1,0:T(8,128)S(1)}, u32[]{:S(2)}, u32[]{:S(2)}) collective-permute-start(f32[1536,128]{1,0:T(8,128)S(1)} %bitcast.20), channel_id=1, source_target_pairs={{0,8},{8,0},{1,9},{9,1},{2,10},{10,2},{3,11},{11,3},{4,12},{12,4},... | collective-permute-start | bytes 2359304 | tf_op jit(solution)/shard_map/ppermute | solution.py:279
  136.8 19.7 %all-to-all-start.5 = ((bf16[64,12,128]{2,1,0:T(8,128)(2,1)}), bf16[64,12,128]{2,1,0:T(8,128)(2,1)S(1)}, u32[]{:S(2)}, u32[]{:S(2)}) async-start(bf16[64,12,128]{2,1,0:T(8,128)(2,1)} %copy.20), calls=%async_computation.5 | async-start | bytes 524288 | tf_op jit(solution)/shard_map/all_to_all | solution.py:203

commit v10 on v9

--- a/solution.py
+++ b/solution.py
@@ -373,8 +373,8 @@
     hq = hp - (TAU * TAU) * dot(h, i)
     q = p.astype(F32) - TAU * i.astype(F32)
     t = q - TAU * r.astype(F32)
-    psi1 = full(m1, q + hp)
-    wpsi1 = full(m1, t + hq)
+    both_panels = full(m1, jnp.concatenate([q + hp, t + hq], axis=1))
+    psi1, wpsi1 = both_panels[:, : q.shape[1]], both_panels[:, q.shape[1] :]
     psi2 = full(m2, wpsi1 + TAU * dot(hh, psi1.astype(BF))).astype(BF)
     group = psi_ref.shape[1]
     nh = x_ref.shape[1]

time: 158 us -> 158 us (level)
  no operation moved by 1% of the time
where the time goes in v10:
time: 158 us; the launch traced here: 157 us
  blocking collectives  88.8 us (56%)
  starting transfers between devices  29.8 us (19%)
  waiting for transfers between devices  20.2 us (13%)
  Pallas kernels  11.3 us (7%)
  local copies, waits for them, and re-layouts  5.38 us (3%)
    all_to_all x5, blocking collectives, swap(): return lax.all_to_all(x, axes, split_axis=0, concat_axis=0, tiled=True)  88.8 us
    all_to_all x1, waiting for transfers between devices, swap(): return lax.all_to_all(x, axes, split_axis=0, concat_axis=0, tiled=True)  12.8 us
    pallas_call x6, Pallas kernels, call(): pl.pallas_call(kernel, out_shape=tuple(outs), in_specs=[pl.BlockSpec(memo...  11.3 us
    ppermute x1, starting transfers between devices, reduced(): return (half, lax.ppermute(half, 'core', pair))  7.49 us
    all_to_all x1, starting transfers between devices, swap(): return lax.all_to_all(x, axes, split_axis=0, concat_axis=0, tiled=True)  5.85 us
    ppermute x1, starting transfers between devices, images(): lax.ppermute(p, 'dy', pair)  4.83 us
    ppermute x1, starting transfers between devices, images(): low = lax.ppermute(last, 'dx', up)  3.43 us
    ppermute x1, starting transfers between devices, images(): high = lax.ppermute(first, 'dx', [(b, a) for a, b in up])  3.19 us
  transfers between devices with their start and end apart: 7, of which 6 were waited for; matrix products, arithmetic and copies ran while one was open for 1% of the time, Pallas kernels for 0%

profile of v10, /device:TPU:1, one launch (start us, length us, event | category | flops | bytes accessed | tf_op | source)
XLA Modules:
  0.0 157.3 jit_solution(1415345405895528630)
XLA Ops:
  0.6 4.8 %collective-permute-start = (bf16[6,128,128]{2,1,0:T(8,128)(2,1)}, bf16[6,128,128]{2,1,0:T(8,128)(2,1)S(1)}, u32[]{:S(2)}, u32[]{:S(2)}) collective-permute-start(bf16[6,128,128]{2,1,0:T(8,128)(2,1)} %bitcast.25), channel_id=1, source_target_pairs={{0,1},{1,0},{2,3},{3,2},{4,5},{5,4},{6,7},{7,6},{8,9},{9,8},{10,11... | collective-permute-start | bytes 589832 | tf_op jit(solution)/shard_map/ppermute | solution.py:177
  5.5 0.8 bitcast_convert_fusion.v_ref
  6.3 1.9 %collective-permute-start.1 = (bf16[128,128]{1,0:T(8,128)(2,1)S(1)}, bf16[128,128]{1,0:T(8,128)(2,1)S(1)}, u32[]{:S(2)}, u32[]{:S(2)}) collective-permute-start(bf16[128,128]{1,0:T(8,128)(2,1)S(1)} %bitcast_convert_fusion.v_ref), channel_id=1, source_target_pairs={{0,1},{1,0},{2,3},{3,2},{4,5},{5,4},{6,7},{7,6},{8,9},{9,8},{10,11... | collective-permute-start | bytes 98312 | tf_op jit(solution)/shard_map/ppermute | solution.py:177
  8.2 0.0 copy-start.2
  8.2 0.9 copy-done.2
  9.2 1.8 %collective-permute-done.1.other_v_ref = bf16[128,128]{1,0:T(8,128)(2,1)S(1)} collective-permute-done((bf16[128,128]{1,0:T(8,128)(2,1)S(1)}, bf16[128,128]{1,0:T(8,128)(2,1)S(1)}, u32[]{:S(2)}, u32[]{:S(2)}) %collective-permute-start.1) | collective-permute-done | bytes 32800 | tf_op jit(solution)/shard_map/ppermute | solution.py:177
  11.0 0.0 collective-permute-done.other_ref
  11.0 3.4 %collective-permute-start.2 = (bf16[7,144,128]{2,1,0:T(8,128)(2,1)S(1)}, bf16[7,144,128]{2,1,0:T(8,128)(2,1)S(1)}, u32[]{:S(2)}, u32[]{:S(2)}) collective-permute-start(bf16[7,144,128]{2,1,0:T(8,128)(2,1)S(1)} %get-tuple-element.8), channel_id=1, source_target_pairs={{0,2},{2,4},{4,6},{6,0},{1,3},{3,5},{5,7},{7,1},{8,10},{10,12},{12... | collective-permute-start | bytes 774152 | tf_op jit(solution)/shard_map/ppermute | solution.py:192
  14.5 3.2 %collective-permute-start.3 = (bf16[7,144,128]{2,1,0:T(8,128)(2,1)S(1)}, bf16[7,144,128]{2,1,0:T(8,128)(2,1)S(1)}, u32[]{:S(2)}, u32[]{:S(2)}) collective-permute-start(bf16[7,144,128]{2,1,0:T(8,128)(2,1)S(1)} %get-tuple-element.9), channel_id=1, source_target_pairs={{2,0},{4,2},{6,4},{0,6},{3,1},{5,3},{7,5},{1,7},{10,8},{12,10},{14... | collective-permute-start | bytes 774152 | tf_op jit(solution)/shard_map/ppermute | solution.py:193
  17.7 0.0 copy-start
  17.7 1.3 copy-done
  18.9 0.0 copy-start.1
  18.9 0.1 shard_map.52.table_ref
  19.0 0.4 collective-permute-done.2.lo_ref
  19.4 2.1 %collective-permute-done.3.hi_ref = bf16[7,144,128]{2,1,0:T(8,128)(2,1)S(1)} collective-permute-done((bf16[7,144,128]{2,1,0:T(8,128)(2,1)S(1)}, bf16[7,144,128]{2,1,0:T(8,128)(2,1)S(1)}, u32[]{:S(2)}, u32[]{:S(2)}) %collective-permute-start.3) | collective-permute-done | bytes 258080 | tf_op jit(solution)/shard_map/ppermute | solution.py:193
  21.5 0.0 copy-done.1
  21.5 2.5 %shard_map.53 = bf16[36,64,128]{2,1,0:T(8,128)(2,1)S(1)} custom-call(bf16[6,128,128]{2,1,0:T(8,128)(2,1)S(1)} %shard_map.50.p_ref, f32[128,128]{1,0:T(8,128)S(1)} %bitcast.23, bf16[6,128,128]{2,1,0:T(8,128)(2,1)S(1)} %collective-permute-done.other_ref, bf16[128,128]{1,0:T(8,128)(2,1)S(1)} %collective-permute-done.1.other_v_ref, ...), custom_call_target="tpu_custom_call" | custom-call | tf_op jit(solution)/shard_map/pallas_call | solution.py:138
  24.1 0.4 copy.18
  24.5 40.2 %all_to_all.30 = bf16[64,36,128]{2,1,0:T(8,128)(2,1)S(1)} all-to-all(bf16[64,36,128]{2,1,0:T(8,128)(2,1)S(1)} %copy.18), channel_id=1, replica_groups=mesh['zhi'=4,'yh'=4,'yl'=2,'core'=2,'dx'=4,'dy'=2] {'zhi','yh','yl','core'}, dimensions={0} | all-to-all | bytes 1179648 | tf_op jit(solution)/shard_map/all_to_all | solution.py:203
  64.7 0.1 copy.19
  64.8 0.9 shard_map.54
  65.7 3.1 %collective-permute-start.4 = (bf16[1536,128]{1,0:T(8,128)(2,1)S(1)}, bf16[1536,128]{1,0:T(8,128)(2,1)S(1)}, u32[]{:S(2)}, u32[]{:S(2)}) collective-permute-start(bf16[1536,128]{1,0:T(8,128)(2,1)S(1)} %get-tuple-element.11), channel_id=1, source_target_pairs={{0,8},{8,0},{1,9},{9,1},{2,10},{10,2},{3,11},{11,3},{4,12},{12,4},... | collective-permute-start | bytes 1179656 | tf_op jit(solution)/shard_map/ppermute | solution.py:274
  68.8 1.3 collective-permute-done.4
  70.1 0.1 add_convert_fusion
  70.2 11.1 %all_to_all.31 = bf16[16,96,128]{2,1,0:T(8,128)(2,1)S(1)} all-to-all(bf16[16,96,128]{2,1,0:T(8,128)(2,1)S(1)} %bitcast.29), channel_id=1, replica_groups=mesh['zhi'=4,'yh'=4,'yl'=2,'core'=2,'dx'=4,'dy'=2] {'dx','dy','yl'}, dimensions={0} | all-to-all | bytes 786432 | tf_op jit(solution)/shard_map/all_to_all | solution.py:203
  81.3 0.1 convert_reduce_fusion
  81.4 12.5 %all_to_all.32 = f32[4,96,128]{2,1,0:T(8,128)S(1)} all-to-all(f32[4,96,128]{2,1,0:T(8,128)S(1)} %broadcast_in_dim.6), channel_id=1, replica_groups=mesh['zhi'=4,'yh'=4,'yl'=2,'core'=2,'dx'=4,'dy'=2] {'zhi'}, dimensions={0} | all-to-all | bytes 393216 | tf_op jit(solution)/shard_map/all_to_all | solution.py:203
  94.0 11.7 %all_to_all.33 = f32[4,96,128]{2,1,0:T(8,128)S(1)} all-to-all(f32[4,96,128]{2,1,0:T(8,128)S(1)} %broadcast_in_dim.7), channel_id=1, replica_groups=mesh['zhi'=4,'yh'=4,'yl'=2,'core'=2,'dx'=4,'dy'=2] {'yh'}, dimensions={0} | all-to-all | bytes 393216 | tf_op jit(solution)/shard_map/all_to_all | solution.py:203
  105.7 0.1 broadcast_in_dim.8
  105.8 13.3 %all_to_all.34 = f32[16,96,128]{2,1,0:T(8,128)S(1)} all-to-all(f32[16,96,128]{2,1,0:T(8,128)S(1)} %broadcast_in_dim.8), channel_id=1, replica_groups=mesh['zhi'=4,'yh'=4,'yl'=2,'core'=2,'dx'=4,'dy'=2] {'dx','dy','yl'}, dimensions={0} | all-to-all | bytes 1572864 | tf_op jit(solution)/shard_map/all_to_all | solution.py:203
  119.0 7.5 %collective-permute-start.5 = (f32[1536,128]{1,0:T(8,128)S(1)}, f32[1536,128]{1,0:T(8,128)S(1)}, u32[]{:S(2)}, u32[]{:S(2)}) collective-permute-start(f32[1536,128]{1,0:T(8,128)S(1)} %bitcast.20), channel_id=1, source_target_pairs={{0,8},{8,0},{1,9},{9,1},{2,10},{10,2},{3,11},{11,3},{4,12},{12,4},... | collective-permute-start | bytes 2359304 | tf_op jit(solution)/shard_map/ppermute | solution.py:279
  126.5 1.7 %collective-permute-done.5.theirs_ref = f32[1536,128]{1,0:T(8,128)S(1)} collective-permute-done((f32[1536,128]{1,0:T(8,128)S(1)}, f32[1536,128]{1,0:T(8,128)S(1)}, u32[]{:S(2)}, u32[]{:S(2)}) %collective-permute-start.5) | collective-permute-done | bytes 786464 | tf_op jit(solution)/shard_map/ppermute | solution.py:279
  128.2 7.7 %shard_map.55 = (bf16[12,64,128]{2,1,0:T(8,128)(2,1)S(1)}, f32[384,384]{1,0:T(8,128)S(1)}) custom-call(f32[1536,128]{1,0:T(8,128)S(1)} %bitcast.21, f32[1536,128]{1,0:T(8,128)S(1)} %collective-permute-done.5.theirs_ref, bf16[3,2,384,128]{3,2,1,0:T(8,128)(2,1)S(1)} %bitcast.19), custom_call_target="tpu_custom_call" | custom-call | tf_op jit(solution)/shard_map/pallas_call | solution.py:138
  136.0 0.8 copy.20
  136.8 5.9 %all-to-all-start.5 = ((bf16[64,12,128]{2,1,0:T(8,128)(2,1)}), bf16[64,12,128]{2,1,0:T(8,128)(2,1)S(1)}, u32[]{:S(2)}, u32[]{:S(2)}) async-start(bf16[64,12,128]{2,1,0:T(8,128)(2,1)} %copy.20), calls=%async_computation.5 | async-start | bytes 524288 | tf_op jit(solution)/shard_map/all_to_all | solution.py:203
  142.7 0.1 reshape.42
  142.8 0.1 copy.23
  142.9 0.8 reshape.43
  143.7 12.8 %all-to-all-done.5 = bf16[64,12,128]{2,1,0:T(8,128)(2,1)S(1)} async-done(((bf16[64,12,128]{2,1,0:T(8,128)(2,1)}), bf16[64,12,128]{2,1,0:T(8,128)(2,1)S(1)}, u32[]{:S(2)}, u32[]{:S(2)}) %all-to-all-start.5) | async-done | bytes 196640 | tf_op jit(solution)/shard_map/all_to_all | solution.py:203
  156.5 0.7 copy.21
  (8 shorter events, 0.1 us)
Async XLA Ops:
  0.6 10.3 %collective-permute-start = (bf16[6,128,128]{2,1,0:T(8,128)(2,1)}, bf16[6,128,128]{2,1,0:T(8,128)(2,1)S(1)}, u32[]{:S(2)}, u32[]{:S(2)}) collective-permute-start(bf16[6,128,128]{2,1,0:T(8,128)(2,1)} %bitcast.25), channel_id=1, source_target_pairs={{0,1},{1,0},{2,3},{3,2},{4,5},{5,4},{6,7},{7,6},{8,9},{9,8},{10,11... | collective-permute-start | bytes 589832 | tf_op jit(solution)/shard_map/ppermute | solution.py:177
  6.3 4.6 %collective-permute-start.1 = (bf16[128,128]{1,0:T(8,128)(2,1)S(1)}, bf16[128,128]{1,0:T(8,128)(2,1)S(1)}, u32[]{:S(2)}, u32[]{:S(2)}) collective-permute-start(bf16[128,128]{1,0:T(8,128)(2,1)S(1)} %bitcast_convert_fusion.v_ref), channel_id=1, source_target_pairs={{0,1},{1,0},{2,3},{3,2},{4,5},{5,4},{6,7},{7,6},{8,9},{9,8},{10,11... | collective-permute-start | bytes 98312 | tf_op jit(solution)/shard_map/ppermute | solution.py:177
  8.2 0.9 copy-start.2
  11.0 8.4 %collective-permute-start.2 = (bf16[7,144,128]{2,1,0:T(8,128)(2,1)S(1)}, bf16[7,144,128]{2,1,0:T(8,128)(2,1)S(1)}, u32[]{:S(2)}, u32[]{:S(2)}) collective-permute-start(bf16[7,144,128]{2,1,0:T(8,128)(2,1)S(1)} %get-tuple-element.8), channel_id=1, source_target_pairs={{0,2},{2,4},{4,6},{6,0},{1,3},{3,5},{5,7},{7,1},{8,10},{10,12},{12... | collective-permute-start | bytes 774152 | tf_op jit(solution)/shard_map/ppermute | solution.py:192
  14.5 7.1 %collective-permute-start.3 = (bf16[7,144,128]{2,1,0:T(8,128)(2,1)S(1)}, bf16[7,144,128]{2,1,0:T(8,128)(2,1)S(1)}, u32[]{:S(2)}, u32[]{:S(2)}) collective-permute-start(bf16[7,144,128]{2,1,0:T(8,128)(2,1)S(1)} %get-tuple-element.9), channel_id=1, source_target_pairs={{2,0},{4,2},{6,4},{0,6},{3,1},{5,3},{7,5},{1,7},{10,8},{12,10},{14... | collective-permute-start | bytes 774152 | tf_op jit(solution)/shard_map/ppermute | solution.py:193
  17.7 1.3 copy-start
  18.9 2.6 %copy-start.1 = (f32[16,8,128]{2,1,0:T(8,128)S(1)}, f32[16,8,128]{2,1,0:T(8,128)}, u32[]{:S(2)}) copy-start(f32[16,8,128]{2,1,0:T(8,128)} %param.4) | copy-start | bytes 196612
  65.7 4.4 %collective-permute-start.4 = (bf16[1536,128]{1,0:T(8,128)(2,1)S(1)}, bf16[1536,128]{1,0:T(8,128)(2,1)S(1)}, u32[]{:S(2)}, u32[]{:S(2)}) collective-permute-start(bf16[1536,128]{1,0:T(8,128)(2,1)S(1)} %get-tuple-element.11), channel_id=1, source_target_pairs={{0,8},{8,0},{1,9},{9,1},{2,10},{10,2},{3,11},{11,3},{4,12},{12,4},... | collective-permute-start | bytes 1179656 | tf_op jit(solution)/shard_map/ppermute | solution.py:274
  119.0 9.2 %collective-permute-start.5 = (f32[1536,128]{1,0:T(8,128)S(1)}, f32[1536,128]{1,0:T(8,128)S(1)}, u32[]{:S(2)}, u32[]{:S(2)}) collective-permute-start(f32[1536,128]{1,0:T(8,128)S(1)} %bitcast.20), channel_id=1, source_target_pairs={{0,8},{8,0},{1,9},{9,1},{2,10},{10,2},{3,11},{11,3},{4,12},{12,4},... | collective-permute-start | bytes 2359304 | tf_op jit(solution)/shard_map/ppermute | solution.py:279
  136.8 19.7 %all-to-all-start.5 = ((bf16[64,12,128]{2,1,0:T(8,128)(2,1)}), bf16[64,12,128]{2,1,0:T(8,128)(2,1)S(1)}, u32[]{:S(2)}, u32[]{:S(2)}) async-start(bf16[64,12,128]{2,1,0:T(8,128)(2,1)} %copy.20), calls=%async_computation.5 | async-start | bytes 524288 | tf_op jit(solution)/shard_map/all_to_all | solution.py:203
